TPU v7x, 32 devices: a whole 2x2x4 slice. The times are simulated.
32 devices in a mesh: dp: 2 (over x), row: 4 (over y, core), col: 4 (over z).
Axes of the slice: x: 2, y: 2, z: 4, core: 2. Of those that a mesh axis runs over, the one named last changes fastest.
Arguments:
- block_input: bfloat16 [2048, 768], P(('dp', 'row'), 'col'), may hold values from -6 to 6
- ln1_gain: float32 [768], P('col'), may hold values from 0.1 to 1.9
- ln1_bias: float32 [768], P('col'), may hold values from -1.75 to 1.75
- qkv_weight: bfloat16 [4, 4, 110592], P('col', 'row'), may hold values from -0.21875 to 0.21875
- qv_bias: float32 [2, 768], P(None, 'row'), may hold values from -1.75 to 1.75
- out_weight: bfloat16 [4, 4, 36864], P('row', 'col'), may hold values from -1.25 to 1.25
- out_bias: float32 [768], P('col'), may hold values from -1.75 to 1.75
- ln2_gain: float32 [768], P('col'), may hold values from 0.1 to 1.9
- ln2_bias: float32 [768], P('col'), may hold values from -1.75 to 1.75
- up_weight: bfloat16 [768, 3072], P('col', 'row'), may hold values from -0.21875 to 0.21875
- up_bias: float32 [3072], P('row'), may hold values from -3 to 3
- down_weight: bfloat16 [768, 3072], P('col', 'row'), may hold values from -0.109375 to 0.109375
- down_bias: float32 [768], P('col'), may hold values from -1.75 to 1.75
- out_grad: bfloat16 [2048, 768], P(('dp', 'row'), 'col'), may hold values from -6 to 6
Outputs:
- block_output: bfloat16 [2048, 768], P(('dp', 'row'), 'col')
- input_grad: bfloat16 [2048, 768], P(('dp', 'row'), 'col')
- ln1_gain_grad: float32 [768], P('col')
- ln1_bias_grad: float32 [768], P('col')
- qkv_weight_grad: float32 [4, 4, 110592], P('col', 'row')
- qv_bias_grad: float32 [2, 768], P(None, 'row')
- out_weight_grad: float32 [4, 4, 36864], P('row', 'col')
- out_bias_grad: float32 [768], P('col')
- ln2_gain_grad: float32 [768], P('col')
- ln2_bias_grad: float32 [768], P('col')
- up_weight_grad: float32 [768, 3072], P('col', 'row')
- up_bias_grad: float32 [3072], P('row')
- down_weight_grad: float32 [768, 3072], P('col', 'row')
- down_bias_grad: float32 [768], P('col')
All inputs are finite; a program needn't handle non-finite values.
Results may differ from a plain program's by a relative error of at most 0.015.
Values may be sent and summed in bfloat16 or wider, within the bound.
No kernel may reach another device: no remote copies, remote signals or barrier semaphores. Data moves between devices by JAX's collectives and lax.ppermute only.
A program may use at most 64 MiB of HBM per device.

v0:
```python
import math

import jax
import jax.numpy as jnp
from jax import lax
from jax.sharding import PartitionSpec as P

D = 768
HEAD = 64


def feature_sums(first, second):
    return lax.psum((first, second), "col")


def normalize(resid, gain, shift):
    total, squares = feature_sums(
        jnp.sum(resid, axis=-1, keepdims=True), jnp.sum(resid * resid, axis=-1, keepdims=True)
    )
    mean_value = total / D
    variance = squares / D - mean_value * mean_value
    inverse = lax.rsqrt(variance + 1e-05)
    centred = (resid - mean_value) * inverse
    return ((centred * gain + shift).astype(jnp.bfloat16), centred, inverse)


def norm_back(grad_norm, centred, inverse, gain):
    scaled = grad_norm * gain
    first, second = feature_sums(
        jnp.sum(scaled, axis=-1, keepdims=True), jnp.sum(scaled * centred, axis=-1, keepdims=True)
    )
    return inverse * (scaled - first / D - centred * second / D)


def gather_rows(local):
    return lax.all_gather(local, "row", axis=0, tiled=True)


def gather_cols(local):
    return lax.all_gather(local, "col", axis=0, tiled=True)


def multiply(left, matrix, flipped):
    if flipped:
        return lax.dot_general(
            left, matrix, (((1,), (1,)), ((), ())), preferred_element_type=jnp.float32
        )
    return jnp.dot(left, matrix, preferred_element_type=jnp.float32)


def sum_over_cols(whole, matrix, flipped):
    share = whole.shape[0] // lax.axis_size("col")

    def term(start, count):
        return multiply(whole, matrix, flipped)

    return lax.psum_scatter(
        term(jnp.int32(0), share * lax.axis_size("col")), "col", scatter_dimension=0, tiled=True
    )


def sum_over_rows(whole, matrix, flipped):
    share = whole.shape[0] // lax.axis_size("row")

    def term(start, count):
        return multiply(whole, matrix, flipped)

    return lax.psum_scatter(
        term(jnp.int32(0), share * lax.axis_size("row")), "row", scatter_dimension=0, tiled=True
    )


def outer_sum(left, right):
    return lax.dot_general(
        left, right, (((0,), (0,)), ((), ())), preferred_element_type=jnp.float32
    )


def column_sums(whole):
    return jnp.sum(whole, axis=0, dtype=jnp.float32)


def gelu_tanh(values):
    return jax.nn.gelu(values, approximate=True)


def head_scores(queries, keys_head, causal):
    raw = lax.dot_general(
        queries, keys_head, (((1,), (1,)), ((), ())), preferred_element_type=jnp.float32
    )
    return jnp.where(causal, raw * (1.0 / math.sqrt(HEAD)), -1e30)


def body(
    block_input,
    ln1_gain,
    ln1_bias,
    qkv_weight,
    qv_bias,
    out_weight,
    out_bias,
    ln2_gain,
    ln2_bias,
    up_weight,
    up_bias,
    down_weight,
    down_bias,
    out_grad,
):
    scale = 1.0 / math.sqrt(HEAD)
    width_in = D // lax.axis_size("col")
    width_out = D // lax.axis_size("row")
    qkv_flat = qkv_weight.reshape(width_in, 3 * width_out)
    out_mat = out_weight.reshape(width_out, width_in)
    resid_in = block_input.astype(jnp.float32)
    normed_one, centred_one, inverse_one = normalize(resid_in, ln1_gain, ln1_bias)
    normed_one_all = gather_rows(normed_one)
    projected = sum_over_cols(normed_one_all, qkv_flat, False)
    local_rows = projected.shape[0]
    shifts = jnp.stack([qv_bias[0], jnp.zeros_like(qv_bias[0]), qv_bias[1]])
    projected = (projected.reshape(local_rows, 3, width_out) + shifts).astype(jnp.bfloat16)
    queries = projected[:, 0]
    keys_all, values_all = (
        lax.all_gather(projected[:, 1], "col", axis=0, tiled=True),
        lax.all_gather(projected[:, 2], "col", axis=0, tiled=True),
    )
    seq_len = keys_all.shape[0]
    query_places = lax.axis_index("col") * local_rows + lax.iota(jnp.int32, local_rows)
    key_places = lax.iota(jnp.int32, seq_len)
    causal = key_places[None, :] <= query_places[:, None]
    heads_here = width_out // HEAD
    head_outputs = []
    log_totals = []
    for head_index in range(heads_here):
        lower = head_index * HEAD
        scores = head_scores(
            queries[:, lower : lower + HEAD], keys_all[:, lower : lower + HEAD], causal
        )
        top_score = jnp.max(scores, axis=-1, keepdims=True)
        expd = jnp.exp(scores - top_score)
        row_total = jnp.sum(expd, axis=-1, keepdims=True)
        probs = expd / row_total
        log_totals.append(top_score + jnp.log(row_total))
        head_outputs.append(
            jnp.dot(
                probs.astype(jnp.bfloat16),
                values_all[:, lower : lower + HEAD],
                preferred_element_type=jnp.float32,
            )
        )
    attended = jnp.concatenate(head_outputs, axis=1).astype(jnp.bfloat16)
    attended_all = gather_cols(attended)
    resid_one = resid_in + sum_over_rows(attended_all, out_mat, False) + out_bias
    normed_two, centred_two, inverse_two = normalize(resid_one, ln2_gain, ln2_bias)
    normed_two_all = gather_rows(normed_two)
    hidden_pre = sum_over_cols(normed_two_all, up_weight, False) + up_bias
    hidden_act = gelu_tanh(hidden_pre).astype(jnp.bfloat16)
    hidden_all = gather_cols(hidden_act)
    block_output = (resid_one + sum_over_rows(hidden_all, down_weight, True) + down_bias).astype(
        jnp.bfloat16
    )
    grad_all = gather_rows(out_grad)
    d_down_bias = column_sums(grad_all)
    d_down_weight = outer_sum(grad_all, hidden_all)
    d_act = sum_over_cols(grad_all, down_weight, False)
    gelu_pull = jax.vjp(gelu_tanh, hidden_pre)[1]
    d_pre = gelu_pull(d_act)[0].astype(jnp.bfloat16)
    d_pre_all = gather_cols(d_pre)
    d_up_bias = column_sums(d_pre_all)
    d_up_weight = outer_sum(normed_two_all, d_pre_all)
    d_normed_two = sum_over_rows(d_pre_all, up_weight, True)
    d_ln2_bias = jnp.sum(d_normed_two, axis=0)
    d_ln2_gain = jnp.sum(d_normed_two * centred_two, axis=0)
    d_resid_one = out_grad.astype(jnp.float32) + norm_back(
        d_normed_two, centred_two, inverse_two, ln2_gain
    )
    grad_proj = d_resid_one.astype(jnp.bfloat16)
    grad_proj_all = gather_rows(grad_proj)
    d_out_bias = column_sums(grad_proj_all)
    d_out_weight = outer_sum(attended_all, grad_proj_all).reshape(1, 1, width_out * width_in)
    d_attended = sum_over_cols(grad_proj_all, out_mat, True).astype(jnp.bfloat16)
    query_grads = []
    key_grads = []
    value_grads = []
    for head_index in range(heads_here):
        lower = head_index * HEAD
        query_head = queries[:, lower : lower + HEAD]
        keys_head = keys_all[:, lower : lower + HEAD]
        values_head = values_all[:, lower : lower + HEAD]
        grad_head = d_attended[:, lower : lower + HEAD]
        scores = head_scores(query_head, keys_head, causal)
        probs = jnp.exp(scores - log_totals[head_index])
        value_grads.append(outer_sum(probs.astype(jnp.bfloat16), grad_head))
        grad_probs = lax.dot_general(
            grad_head, values_head, (((1,), (1,)), ((), ())), preferred_element_type=jnp.float32
        )
        grad_scores = probs * (grad_probs - jnp.sum(grad_probs * probs, axis=-1, keepdims=True))
        grad_scores = grad_scores.astype(jnp.bfloat16)
        query_grads.append(
            jnp.dot(grad_scores, keys_head, preferred_element_type=jnp.float32) * scale
        )
        key_grads.append(outer_sum(grad_scores, query_head) * scale)
    d_queries = jnp.concatenate(query_grads, axis=1)
    d_keys, d_values = (
        lax.psum_scatter(
            jnp.concatenate(key_grads, axis=1).astype(jnp.bfloat16),
            "col",
            scatter_dimension=0,
            tiled=True,
        ).astype(jnp.float32),
        lax.psum_scatter(
            jnp.concatenate(value_grads, axis=1).astype(jnp.bfloat16),
            "col",
            scatter_dimension=0,
            tiled=True,
        ).astype(jnp.float32),
    )
    d_projected = (
        jnp.stack([d_queries, d_keys, d_values], axis=1)
        .astype(jnp.bfloat16)
        .reshape(local_rows, 3 * width_out)
    )
    d_projected_all = gather_cols(d_projected)
    bias_sums = column_sums(d_projected_all).reshape(3, width_out)
    d_qv_bias = jnp.stack([bias_sums[0], bias_sums[2]])
    d_qkv_weight = outer_sum(normed_one_all, d_projected_all).reshape(
        1, 1, width_in * 3 * width_out
    )
    d_normed_one = sum_over_rows(d_projected_all, qkv_flat, True)
    d_ln1_bias = jnp.sum(d_normed_one, axis=0)
    d_ln1_gain = jnp.sum(d_normed_one * centred_one, axis=0)
    input_grad = (d_resid_one + norm_back(d_normed_one, centred_one, inverse_one, ln1_gain)).astype(
        jnp.bfloat16
    )
    d_ln1_gain, d_ln1_bias, d_ln2_gain, d_ln2_bias = lax.psum(
        (d_ln1_gain, d_ln1_bias, d_ln2_gain, d_ln2_bias), ("dp", "row")
    )
    (
        d_qkv_weight,
        d_qv_bias,
        d_out_weight,
        d_out_bias,
        d_up_weight,
        d_up_bias,
        d_down_weight,
        d_down_bias,
    ) = (
        lax.psum(d_qkv_weight.astype(jnp.bfloat16), "dp").astype(jnp.float32),
        lax.psum(d_qv_bias.astype(jnp.bfloat16), "dp").astype(jnp.float32),
        lax.psum(d_out_weight.astype(jnp.bfloat16), "dp").astype(jnp.float32),
        lax.psum(d_out_bias.astype(jnp.bfloat16), "dp").astype(jnp.float32),
        lax.psum(d_up_weight.astype(jnp.bfloat16), "dp").astype(jnp.float32),
        lax.psum(d_up_bias.astype(jnp.bfloat16), "dp").astype(jnp.float32),
        lax.psum(d_down_weight.astype(jnp.bfloat16), "dp").astype(jnp.float32),
        lax.psum(d_down_bias.astype(jnp.bfloat16), "dp").astype(jnp.float32),
    )
    return (
        block_output,
        input_grad,
        d_ln1_gain,
        d_ln1_bias,
        d_qkv_weight,
        d_qv_bias,
        d_out_weight,
        d_out_bias,
        d_ln2_gain,
        d_ln2_bias,
        d_up_weight,
        d_up_bias,
        d_down_weight,
        d_down_bias,
    )


def solution(mesh):
    in_specs = (
        P(("dp", "row"), "col"),
        P("col"),
        P("col"),
        P("col", "row", None),
        P(None, "row"),
        P("row", "col", None),
        P("col"),
        P("col"),
        P("col"),
        P("col", "row"),
        P("row"),
        P("col", "row"),
        P("col"),
        P(("dp", "row"), "col"),
    )
    out_specs = (
        P(("dp", "row"), "col"),
        P(("dp", "row"), "col"),
        P("col"),
        P("col"),
        P("col", "row", None),
        P(None, "row"),
        P("row", "col", None),
        P("col"),
        P("col"),
        P("col"),
        P("col", "row"),
        P("row"),
        P("col", "row"),
        P("col"),
    )
    return jax.shard_map(body, mesh=mesh, in_specs=in_specs, out_specs=out_specs, check_vma=False)
```

profile of v0, /device:TPU:0, one launch (start us, length us, event | category | flops | bytes accessed | tf_op | source)
XLA Modules:
  0.0 620.6 jit_solution(9238203206953459952)
XLA Ops:
  10.7 13.5 %all-reduce.4 = (f32[256,1]{0,1:T(1,128)S(1)}, f32[256,1]{0,1:T(1,128)S(1)}) all-reduce(f32[256,1]{0,1:T(1,128)S(1)} %bitcast.89, f32[256,1]{0,1:T(1,128)S(1)} %bitcast.88), channel_id=1, replica_groups=mesh['dp'=2,'row'=4,'col'=4] {'col'}, use_global_device_ids=true, to_apply=%region_3.0 | all-reduce | flops 512 | bytes 4096 | tf_op jit(solution)/shard_map/psum | solution.py:13
  25.7 6.5 %all_gather.30 = bf16[1024,192]{0,1:T(8,128)(2,1)S(1)} all-gather(bf16[256,192]{0,1:T(8,128)(2,1)S(1)} %fusion.35), channel_id=1, replica_groups=mesh['dp'=2,'row'=4,'col'=4] {'row'}, dimensions={0}, use_global_device_ids=true | all-gather | bytes 491520 | tf_op jit(solution)/shard_map/all_gather | solution.py:36
  36.6 44.5 %reduce-scatter.11.cloned.1.call-done = f32[256,576]{0,1:T(8,128)} async-done(((f32[1024,576]{0,1:T(8,128)}), f32[256,576]{0,1:T(8,128)}) %reduce-scatter.11.cloned.1.call-update) | async-done | bytes 589840 | tf_op jit(solution)/shard_map/reduce_scatter | solution.py:57
  82.3 14.6 %all-gather = bf16[1024,1,192]{0,2,1:T(8,128)(2,1)S(1)} all-gather(bf16[256,1,192]{0,2,1:T(8,128)(2,1)S(1)} %get-tuple-element.50), channel_id=2, replica_groups=mesh['dp'=2,'row'=4,'col'=4] {'col'}, dimensions={0}, use_global_device_ids=true | all-gather | bytes 491520 | tf_op jit(solution)/shard_map/all_gather | solution.py:124
  98.2 14.2 %all-gather.1 = bf16[1024,1,192]{0,2,1:T(8,128)(2,1)S(1)} all-gather(bf16[256,1,192]{0,2,1:T(8,128)(2,1)S(1)} %get-tuple-element.49), channel_id=3, replica_groups=mesh['dp'=2,'row'=4,'col'=4] {'col'}, dimensions={0}, use_global_device_ids=true | all-gather | bytes 491520 | tf_op jit(solution)/shard_map/all_gather | solution.py:125
  115.1 14.2 %all_gather.33 = bf16[1024,192]{0,1:T(8,128)(2,1)S(1)} all-gather(bf16[256,192]{0,1:T(8,128)(2,1)S(1)} %pad_maximum_fusion.3), channel_id=1, replica_groups=mesh['dp'=2,'row'=4,'col'=4] {'col'}, dimensions={0}, use_global_device_ids=true | all-gather | bytes 491520 | tf_op jit(solution)/shard_map/all_gather | solution.py:40
  131.4 6.7 %all_gather.36 = bf16[1024,192]{0,1:T(8,128)(2,1)S(1)} all-gather(bf16[256,192]{0,1:T(8,128)(2,1)} %param.27), channel_id=1, replica_groups=mesh['dp'=2,'row'=4,'col'=4] {'row'}, dimensions={0}, use_global_device_ids=true | all-gather | bytes 491520 | tf_op jit(solution)/shard_map/all_gather | solution.py:36
  142.1 12.3 %reduce-scatter.13.cloned.1.call-done = f32[256,192]{0,1:T(8,128)} async-done(((f32[1024,192]{0,1:T(8,128)}), f32[256,192]{0,1:T(8,128)}) %reduce-scatter.13.cloned.1.call-update) | async-done | bytes 196624 | tf_op jit(solution)/shard_map/reduce_scatter | solution.py:68
  156.1 12.3 %all-reduce.3 = (f32[256,1]{0,1:T(1,128)S(1)}, f32[256,1]{0,1:T(1,128)}) all-reduce(f32[256,1]{0,1:T(1,128)S(1)} %bitcast.91, f32[256,1]{0,1:T(1,128)S(1)} %bitcast.90), channel_id=1, replica_groups=mesh['dp'=2,'row'=4,'col'=4] {'col'}, use_global_device_ids=true, to_apply=%region_15.16 | all-reduce | flops 512 | bytes 4096 | tf_op jit(solution)/shard_map/psum | solution.py:13
  179.5 37.7 %reduce-scatter.19.cloned.1.call-done = f32[256,768]{1,0:T(8,128)} async-done(((f32[1024,768]{1,0:T(8,128)}), f32[256,768]{1,0:T(8,128)}) %reduce-scatter.19.cloned.1.call-update) | async-done | bytes 786448 | tf_op jit(solution)/shard_map/reduce_scatter | solution.py:57
  217.2 62.6 %reduce-scatter.15.cloned.1.call-done = f32[256,768]{1,0:T(8,128)} async-done(((f32[1024,768]{1,0:T(8,128)}), f32[256,768]{1,0:T(8,128)}) %reduce-scatter.15.cloned.1.call-update) | async-done | bytes 786448 | tf_op jit(solution)/shard_map/reduce_scatter | solution.py:57
  282.6 37.2 %all-gather.8.cloned.1.call-done = bf16[1024,768]{1,0:T(8,128)(2,1)} async-done(((bf16[256,768]{1,0:T(8,128)(2,1)}), bf16[1024,768]{1,0:T(8,128)(2,1)}) %all-gather.8.cloned.1.call-update) | async-done | bytes 1572880 | tf_op jit(solution)/shard_map/all_gather | solution.py:40
  322.9 22.2 %reduce-scatter.21.cloned.1.call-done = f32[256,192]{0,1:T(8,128)} async-done(((f32[1024,192]{0,1:T(8,128)}), f32[256,192]{0,1:T(8,128)}) %reduce-scatter.21.cloned.1.call-update) | async-done | bytes 196624 | tf_op jit(solution)/shard_map/reduce_scatter | solution.py:68
  346.9 12.3 %all-reduce.2 = (f32[256]{0:T(256)}, f32[256,1]{0,1:T(1,128)}) all-reduce(f32[256]{0:T(256)S(1)} %get-tuple-element.15, f32[256,1]{0,1:T(1,128)} %bitcast.92), channel_id=1, replica_groups=mesh['dp'=2,'row'=4,'col'=4] {'col'}, use_global_device_ids=true, to_apply=%region_23.24 | all-reduce | flops 512 | bytes 4096 | tf_op jit(solution)/shard_map/psum | solution.py:13
  361.7 6.1 all_gather.38
  373.6 18.1 %reduce-scatter.23.cloned.1.call-done = f32[256,192]{0,1:T(8,128)} async-done(((f32[1024,192]{0,1:T(8,128)}), f32[256,192]{0,1:T(8,128)}) %reduce-scatter.23.cloned.1.call-update) | async-done | bytes 196624 | tf_op jit(solution)/shard_map/reduce_scatter | solution.py:57
  410.5 11.1 %reduce-scatter.27.cloned.1.call-done = bf16[256,192]{0,1:T(8,128)(2,1)} async-done(((bf16[1024,192]{0,1:T(8,128)(2,1)}), bf16[256,192]{0,1:T(8,128)(2,1)}) %reduce-scatter.27.cloned.1.call-update) | async-done | bytes 98320 | tf_op jit(solution)/shard_map/reduce_scatter | solution.py:211
  421.6 21.4 %reduce-scatter.25.cloned.1.call-done = bf16[256,192]{0,1:T(8,128)(2,1)} async-done(((bf16[1024,192]{0,1:T(8,128)(2,1)}), bf16[256,192]{0,1:T(8,128)(2,1)}) %reduce-scatter.25.cloned.1.call-update) | async-done | bytes 98320 | tf_op jit(solution)/shard_map/reduce_scatter | solution.py:205
  446.0 34.4 %all-gather.6.cloned.1.call-done = bf16[1024,768]{1,0:T(8,128)(2,1)} async-done(((bf16[256,768]{1,0:T(8,128)(2,1)}), bf16[1024,768]{1,0:T(8,128)(2,1)}) %all-gather.6.cloned.1.call-update) | async-done | bytes 1572880 | tf_op jit(solution)/shard_map/all_gather | solution.py:40
  484.1 29.1 %all-gather.10.cloned.1.call-done = bf16[1024,576]{0,1:T(8,128)(2,1)} async-done(((bf16[256,576]{0,1:T(8,128)(2,1)}), bf16[1024,576]{0,1:T(8,128)(2,1)}) %all-gather.10.cloned.1.call-update) | async-done | bytes 1179664 | tf_op jit(solution)/shard_map/all_gather | solution.py:40
  532.7 27.3 %all-reduce.9.cloned.1.call-done = (bf16[1,1,110592]{2,1,0:T(2,128)(2,1)}, bf16[1,1,36864]{2,1,0:T(2,128)(2,1)}, bf16[192,768]{1,0:T(8,128)(2,1)}, bf16[192,768]{1,0:T(8,128)(2,1)}) async-done(((bf16[1,1,110592]{2,1,0:T(2,128)(2,1)}, bf16[1,1,36864]{2,1,0:T(2,128)(2,1)}, bf16[192,768]{1,0:T(8,128)(2,1)}, bf16[192,768]{1,0:T(8,128)(2,1)}), (bf16[1,1,110592]{2,1,0:T(2,128)(2,1)}, ...) | async-done | bytes 884752 | tf_op jit(solution)/shard_map/psum | solution.py:248
  566.8 19.2 %reduce-scatter.29.cloned.1.call-done = f32[256,192]{0,1:T(8,128)} async-done(((f32[1024,192]{0,1:T(8,128)}), f32[256,192]{0,1:T(8,128)}) %reduce-scatter.29.cloned.1.call-update) | async-done | bytes 196624 | tf_op jit(solution)/shard_map/reduce_scatter | solution.py:68
  587.2 13.3 %all-reduce = (f32[192]{0:T(256)}, f32[192]{0:T(256)}, f32[192]{0:T(256)}, f32[192]{0:T(256)}) all-reduce(f32[192]{0:T(256)S(1)} %get-tuple-element.16, f32[192]{0:T(256)S(1)} %get-tuple-element.21, f32[192]{0:T(256)S(1)} %copy-done.41, f32[192]{0:T(256)S(1)} %copy-done.42), channel_id=1, replica_groups=mesh['dp'=2,'row'=4,'col'=4] {'dp','row'}, use_global_device_ids=true, to_apply=%region_36.37 | all-reduce | flops 768 | bytes 6144 | tf_op jit(solution)/shard_map/psum | solution.py:235
  600.5 11.6 %all-reduce.1 = (f32[256]{0:T(256)S(1)}, f32[256,1]{0,1:T(1,128)S(1)}) all-reduce(f32[256]{0:T(256)S(1)} %get-tuple-element.17, f32[256,1]{0,1:T(1,128)S(1)} %bitcast.87), channel_id=1, replica_groups=mesh['dp'=2,'row'=4,'col'=4] {'col'}, use_global_device_ids=true, to_apply=%region_34.35 | all-reduce | flops 512 | bytes 4096 | tf_op jit(solution)/shard_map/psum | solution.py:13
  (227 shorter events, 103.5 us)
Async XLA Ops:
  7.2 169.9 %copy-start = (bf16[192,768]{1,0:T(8,128)(2,1)S(1)}, bf16[192,768]{1,0:T(8,128)(2,1)}, u32[]{:S(2)}) copy-start(bf16[192,768]{1,0:T(8,128)(2,1)} %param.23) | copy-start | bytes 884740
  7.2 73.9 %reduce-scatter.11.cloned.1.call-start = ((), (), s32[]{:S(2)}) async-start(), calls=%async_computation.10 | async-start | bytes 2949120 | tf_op jit(solution)/shard_map/reduce_scatter | solution.py:57
  35.0 119.4 %reduce-scatter.13.cloned.1.call-start = ((), (), s32[]{:S(2)}) async-start(), calls=%async_computation.11 | async-start | bytes 983040 | tf_op jit(solution)/shard_map/reduce_scatter | solution.py:68
  36.4 92.9 %copy-start.23 = (bf16[192,192]{1,0:T(8,128)(2,1)}, bf16[192,192]{1,0:T(8,128)(2,1)S(1)}, u32[]{:S(2)}) copy-start(bf16[192,192]{1,0:T(8,128)(2,1)S(1)} %reshape.120) | copy-start | bytes 221188
  131.3 85.8 %reduce-scatter.19.cloned.1.call-start = ((), (), s32[]{:S(2)}) async-start(), calls=%async_computation.15 | async-start | bytes 3932160 | tf_op jit(solution)/shard_map/reduce_scatter | solution.py:57
  142.1 137.7 %reduce-scatter.15.cloned.1.call-start = ((), (), s32[]{:S(2)}) async-start(), calls=%async_computation.12 | async-start | bytes 3932160 | tf_op jit(solution)/shard_map/reduce_scatter | solution.py:57
  179.4 100.3 %copy-start.40 = (f32[768]{0:T(1024)S(1)}, f32[768]{0:T(1024)}, u32[]{:S(2)}) copy-start(f32[768]{0:T(1024)} %param.24) | copy-start | bytes 9220
  179.4 140.4 %all-gather.8.cloned.1.call-start = ((), (), s32[]{:S(2)}) async-start(), calls=%async_computation.16 | async-start | bytes 1966080 | tf_op jit(solution)/shard_map/all_gather | solution.py:40
  282.6 62.5 %reduce-scatter.21.cloned.1.call-start = ((), (), s32[]{:S(2)}) async-start(), calls=%async_computation.17 | async-start | bytes 983040 | tf_op jit(solution)/shard_map/reduce_scatter | solution.py:68
  322.9 68.9 %reduce-scatter.23.cloned.1.call-start = ((), (), s32[]{:S(2)}) async-start(), calls=%async_computation.18 | async-start | bytes 983040 | tf_op jit(solution)/shard_map/reduce_scatter | solution.py:57
  370.7 50.8 %reduce-scatter.27.cloned.1.call-start = ((), (), s32[]{:S(2)}) async-start(), calls=%async_computation.20 | async-start | bytes 491520 | tf_op jit(solution)/shard_map/reduce_scatter | solution.py:211
  401.6 41.4 %reduce-scatter.25.cloned.1.call-start = ((), (), s32[]{:S(2)}) async-start(), calls=%async_computation.19 | async-start | bytes 491520 | tf_op jit(solution)/shard_map/reduce_scatter | solution.py:205
  406.1 74.3 %all-gather.6.cloned.1.call-start = ((), (), s32[]{:S(2)}) async-start(), calls=%async_computation.13 | async-start | bytes 1966080 | tf_op jit(solution)/shard_map/all_gather | solution.py:40
  406.7 106.5 %all-gather.10.cloned.1.call-start = ((), (), s32[]{:S(2)}) async-start(), calls=%async_computation.21 | async-start | bytes 1474560 | tf_op jit(solution)/shard_map/all_gather | solution.py:40
  444.7 115.4 %all-reduce.9.cloned.1.call-start = ((), (), s32[]{:S(2)}) async-start(), calls=%async_computation.23 | async-start | bytes 2359296 | tf_op jit(solution)/shard_map/psum | solution.py:248
  518.0 68.1 %reduce-scatter.29.cloned.1.call-start = ((), (), s32[]{:S(2)}) async-start(), calls=%async_computation.22 | async-start | bytes 983040 | tf_op jit(solution)/shard_map/reduce_scatter | solution.py:68
  520.4 91.7 %reduce-scatter.17.cloned.1.call-start = ((), (), s32[]{:S(2)}) async-start(), calls=%async_computation.14 | async-start | bytes 983040 | tf_op jit(solution)/shard_map/reduce_scatter | solution.py:68
  525.3 60.7 %copy-start.32 = (f32[256,1]{0,1:T(1,128)S(1)}, f32[256,1]{0,1:T(1,128)}, u32[]{:S(2)}) copy-start(f32[256,1]{0,1:T(1,128)} %copy-done.31) | copy-start | bytes 3076
  525.3 60.7 %copy-start.34 = (f32[256,1]{0,1:T(1,128)S(1)}, f32[256,1]{0,1:T(1,128)}, u32[]{:S(2)}) copy-start(f32[256,1]{0,1:T(1,128)} %copy-done.33) | copy-start | bytes 3076
  525.3 60.7 %copy-start.35 = (f32[192]{0:T(256)S(1)}, f32[192]{0:T(256)}, u32[]{:S(2)}) copy-start(f32[192]{0:T(256)} %param.15) | copy-start | bytes 2308
  560.1 52.1 %copy-start.24 = (bf16[256,192]{0,1:T(8,128)(2,1)S(1)}, bf16[256,192]{0,1:T(8,128)(2,1)}, u32[]{:S(2)}) copy-start(bf16[256,192]{0,1:T(8,128)(2,1)} %param.27) | copy-start | bytes 294916
  560.1 52.1 %copy-start.30 = (f32[192]{0:T(256)S(1)}, f32[192]{0:T(256)}, u32[]{:S(2)}) copy-start(f32[192]{0:T(256)} %param.21) | copy-start | bytes 2308
  560.1 52.1 %copy-start.37 = (f32[256,1]{0,1:T(1,128)S(1)}, f32[256,1]{0,1:T(1,128)}, u32[]{:S(2)}) copy-start(f32[256,1]{0,1:T(1,128)} %copy-done.36) | copy-start | bytes 3076
  560.1 52.1 %copy-start.43 = (f32[256]{0:T(256)S(1)}, f32[256]{0:T(256)}, u32[]{:S(2)}) copy-start(f32[256]{0:T(256)} %get-tuple-element.32) | copy-start | bytes 3076
  (45 other events, 594.0 us)
Sparse Core Ops, SparseCore 0:
  35.1 45.9 reduce-scatter.10
  131.4 22.9 reduce-scatter.12
  156.8 60.2 reduce-scatter.18
  219.4 60.2 reduce-scatter.14
  282.7 37.1 all-gather.7
  323.0 22.1 reduce-scatter.20
  370.8 20.8 reduce-scatter.22
  401.7 19.8 reduce-scatter.26
  424.0 18.9 reduce-scatter.24
  444.9 35.3 all-gather.5
  482.5 30.6 all-gather.9
  518.1 41.8 all-reduce.8
  562.8 23.2 reduce-scatter.28
  588.4 23.2 reduce-scatter.16
where the time goes:
time: 622 us; the launch traced here: 621 us
  waiting for transfers between devices  378 us (61%)
  blocking collectives  137 us (22%)
  matrix products  40.7 us (7%)
  other arithmetic  39.7 us (6%)
  between operations  14.6 us (2%)
  local copies, waits for them, and re-layouts  10.4 us (2%)
    reduce_scatter x4, waiting for transfers between devices, sum_over_cols(): lax.psum_scatter(term(jnp.int32(0), share * lax.axis_size('col')), 'col',...  163 us
    all_gather x3, waiting for transfers between devices, gather_cols(): return lax.all_gather(local, 'col', axis=0, tiled=True)  101 us
    reduce_scatter x4, waiting for transfers between devices, sum_over_rows(): lax.psum_scatter(term(jnp.int32(0), share * lax.axis_size('row')), 'row',...  53.8 us
    psum x4, blocking collectives, feature_sums(): return lax.psum((first, second), 'col')  49.7 us
    psum x1, waiting for transfers between devices, body(): lax.psum(d_qkv_weight.astype(jnp.bfloat16), 'dp').astype(jnp.float32)  27.3 us
    all_gather x4, blocking collectives, gather_rows(): return lax.all_gather(local, 'row', axis=0, tiled=True)  25.5 us
    reduce_scatter x1, waiting for transfers between devices, body(): lax.psum_scatter(jnp.concatenate(key_grads, axis=1).astype(jnp.bfloat16),...  21.4 us
    all_gather x1, blocking collectives, body(): lax.all_gather(projected[:, 1], 'col', axis=0, tiled=True)  14.6 us
  transfers between devices with their start and end apart: 14, of which 13 were waited for; matrix products, arithmetic and copies ran while one was open for 7% of the time, Pallas kernels for 0%

commit v1 on v0

v1 whole, which is shorter than its diff:
```python
import math

import jax
import jax.numpy as jnp
from jax import lax
from jax.experimental import pallas as pl
from jax.experimental.pallas import tpu as pltpu
from jax.sharding import PartitionSpec as P

D = 768
HEAD = 64
SCALE = 1.0 / math.sqrt(HEAD)
bf16 = jnp.bfloat16
f32 = jnp.float32


def dot_nn(a, b):
    return lax.dot_general(a, b, (((1,), (0,)), ((), ())), preferred_element_type=f32)


def dot_nt(a, b):
    return lax.dot_general(a, b, (((1,), (1,)), ((), ())), preferred_element_type=f32)


def dot_tn(a, b):
    return lax.dot_general(a, b, (((0,), (0,)), ((), ())), preferred_element_type=f32)


def swap(value, axis, bit):
    n = lax.axis_size(axis)
    return lax.ppermute(value, axis, [(i, i ^ bit) for i in range(n)])


def row_bits():
    n = lax.axis_size("row")
    bits = []
    b = n // 2
    while b:
        bits.append(b)
        b //= 2
    return bits


def row_order():
    order = [0]
    for b in row_bits():
        order = order + [o ^ b for o in order]
    return order


def gather_row(value):
    for b in row_bits():
        value = jnp.concatenate([value, swap(value, "row", b)], axis=0)
    return value


def scatter_row(partial):
    for b in reversed(row_bits()):
        half = partial.shape[0] // 2
        partial = partial[:half] + swap(partial[half:].astype(bf16), "row", b).astype(f32)
    return partial


def turn_cols(value, split, concat):
    return lax.all_to_all(value, "col", split, concat, tiled=True)


def sum_cols(parts):
    n = lax.axis_size("col")
    c = lax.axis_index("col")
    total = lax.dynamic_index_in_dim(parts, c, 0, keepdims=False).astype(f32)
    for k in range(1, n):
        piece = lax.dynamic_index_in_dim(parts, (c + k) % n, 0, keepdims=False)
        total = total + lax.ppermute(piece, "col", [(i, (i + k) % n) for i in range(n)]).astype(f32)
    return total


def sum_grad(grad):
    n_dp = lax.axis_size("dp")
    n_col, rows, width = grad.shape
    if n_dp == 2:
        d = lax.axis_index("dp")
        halves = grad.astype(bf16).reshape(n_col, 2, rows // 2, width)
        mine = lax.dynamic_index_in_dim(halves, d, 1, keepdims=False)
        other = lax.dynamic_index_in_dim(halves, 1 - d, 1, keepdims=False)
        both = (mine.astype(f32) + swap(other, "dp", 1).astype(f32)).astype(bf16)
        part = sum_cols(both).astype(bf16)
        away = swap(part, "dp", 1)
        low = jnp.where(d == 0, part, away)
        high = jnp.where(d == 0, away, part)
        return jnp.concatenate([low, high], axis=0).astype(f32)
    total = sum_cols(grad.astype(bf16)).astype(bf16)
    return lax.psum(total, "dp").astype(f32)


def natural(order, row_ref, n_col, body):
    n_row = len(order)
    r = row_ref[0]
    for place in range(n_row):
        want = place ^ r
        k = jnp.int32(0)
        for idx, o in enumerate(order):
            k = jnp.where(want == o, idx, k)
        for c in range(n_col):
            body(place, c, k)


def load_natural(order, row_ref, src, dst, chunk):
    n_col = src.shape[0]
    block = n_col * chunk

    def one(place, c, k):
        rows = pl.ds(pl.multiple_of(k * chunk, chunk), chunk)
        dst[place * block + c * chunk : place * block + (c + 1) * chunk, :] = src[c, rows, :]

    natural(order, row_ref, n_col, one)


def store_natural(order, row_ref, src, dst, chunk):
    n_col = dst.shape[0]
    block = n_col * chunk

    def one(place, c, k):
        rows = pl.ds(pl.multiple_of(k * chunk, chunk), chunk)
        dst[c, rows, :] = src[place * block + c * chunk : place * block + (c + 1) * chunk, :]

    natural(order, row_ref, n_col, one)


def block_probs(q, k, block, i):
    scores = dot_nt(q, k) * SCALE
    rows = lax.broadcasted_iota(jnp.int32, scores.shape, 0) + i * block
    cols = lax.broadcasted_iota(jnp.int32, scores.shape, 1)
    scores = jnp.where(cols <= rows, scores, -1e30)
    top = jnp.max(scores, axis=-1, keepdims=True)
    e = jnp.exp(scores - top)
    return e / jnp.sum(e, axis=-1, keepdims=True)


def forward_kernel(order, chunk, row_ref, qkv_ref, out_ref, nat, res):
    load_natural(order, row_ref, qkv_ref, nat, chunk)
    seq = nat.shape[0]
    block = seq // len(order)
    k = nat[:, HEAD : 2 * HEAD]
    v = nat[:, 2 * HEAD :]
    for i in range(len(order)):
        upto = (i + 1) * block
        p = block_probs(nat[i * block : upto, :HEAD], k[:upto], block, i)
        res[i * block : upto, :] = dot_nn(p.astype(bf16), v[:upto]).astype(bf16)
    store_natural(order, row_ref, res, out_ref, chunk)


def backward_kernel(order, chunk, row_ref, qkv_ref, do_ref, out_ref, nat, dnat, res, dkt, dvt):
    load_natural(order, row_ref, qkv_ref, nat, chunk)
    load_natural(order, row_ref, do_ref, dnat, chunk)
    seq = nat.shape[0]
    block = seq // len(order)
    k = nat[:, HEAD : 2 * HEAD]
    v = nat[:, 2 * HEAD :]
    dkt[...] = jnp.zeros_like(dkt)
    dvt[...] = jnp.zeros_like(dvt)
    for i in range(len(order)):
        upto = (i + 1) * block
        q = nat[i * block : upto, :HEAD]
        do = dnat[i * block : upto, :]
        p = block_probs(q, k[:upto], block, i)
        dvt[:, :upto] += dot_tn(do, p.astype(bf16))
        dp = dot_nt(do, v[:upto])
        ds = (p * (dp - jnp.sum(dp * p, axis=-1, keepdims=True))).astype(bf16)
        res[i * block : upto, :HEAD] = (dot_nn(ds, k[:upto]) * SCALE).astype(bf16)
        dkt[:, :upto] += dot_tn(q, ds)
    res[:, HEAD : 2 * HEAD] = (dkt[...].T * SCALE).astype(bf16)
    res[:, 2 * HEAD :] = dvt[...].T.astype(bf16)
    store_natural(order, row_ref, res, out_ref, chunk)


def attention_forward(row, qkv, order, chunk):
    n_col, tokens, width = qkv.shape
    seq = n_col * tokens
    return pl.pallas_call(
        lambda *refs: forward_kernel(order, chunk, *refs),
        out_shape=jax.ShapeDtypeStruct((n_col, tokens, HEAD), bf16),
        in_specs=[pl.BlockSpec(memory_space=pltpu.SMEM), pl.BlockSpec(memory_space=pltpu.VMEM)],
        out_specs=pl.BlockSpec(memory_space=pltpu.VMEM),
        scratch_shapes=[pltpu.VMEM((seq, width), bf16), pltpu.VMEM((seq, HEAD), bf16)],
        compiler_params=pltpu.CompilerParams(vmem_limit_bytes=32 * 1024 * 1024),
    )(row, qkv)


def attention_backward(row, qkv, d_out, order, chunk):
    n_col, tokens, width = qkv.shape
    seq = n_col * tokens
    return pl.pallas_call(
        lambda *refs: backward_kernel(order, chunk, *refs),
        out_shape=jax.ShapeDtypeStruct((n_col, tokens, width), bf16),
        in_specs=[
            pl.BlockSpec(memory_space=pltpu.SMEM),
            pl.BlockSpec(memory_space=pltpu.VMEM),
            pl.BlockSpec(memory_space=pltpu.VMEM),
        ],
        out_specs=pl.BlockSpec(memory_space=pltpu.VMEM),
        scratch_shapes=[
            pltpu.VMEM((seq, width), bf16),
            pltpu.VMEM((seq, HEAD), bf16),
            pltpu.VMEM((seq, width), bf16),
            pltpu.VMEM((HEAD, seq), f32),
            pltpu.VMEM((HEAD, seq), f32),
        ],
        compiler_params=pltpu.CompilerParams(vmem_limit_bytes=32 * 1024 * 1024),
    )(row, qkv, d_out)


def norm_stats(v):
    mean = jnp.sum(v, axis=-1, keepdims=True) / D
    var = jnp.sum(v * v, axis=-1, keepdims=True) / D - mean * mean
    inverse = lax.rsqrt(var + 1e-05)
    return (v - mean) * inverse, inverse


def norm_back(grad, centred, inverse, gain):
    scaled = grad * gain
    first = jnp.sum(scaled, axis=-1, keepdims=True) / D
    second = jnp.sum(scaled * centred, axis=-1, keepdims=True) / D
    return inverse * (scaled - first - centred * second)


def gelu_tanh(values):
    return jax.nn.gelu(values, approximate=True)


def column_sums(whole):
    return jnp.sum(whole, axis=0, dtype=f32)


def to_heads(value, parts):
    n_col = lax.axis_size("col")
    t = value.shape[0]
    heads = value.shape[1] // (parts * HEAD)
    cut = value.reshape(t, parts, heads, HEAD).transpose(2, 0, 1, 3).reshape(heads, t, parts * HEAD)
    cut = jnp.concatenate([cut, jnp.zeros((n_col - heads, t, parts * HEAD), value.dtype)], axis=0)
    return turn_cols(cut, 0, 0)


def from_heads(value, parts, heads):
    back = turn_cols(value, 0, 0)[:heads]
    t = back.shape[1]
    return back.reshape(heads, t, parts, HEAD).transpose(1, 2, 0, 3).reshape(t, parts * heads * HEAD)


def body(
    block_input,
    ln1_gain,
    ln1_bias,
    qkv_weight,
    qv_bias,
    out_weight,
    out_bias,
    ln2_gain,
    ln2_bias,
    up_weight,
    up_bias,
    down_weight,
    down_bias,
    out_grad,
):
    n_col = lax.axis_size("col")
    width_in = D // n_col
    width_out = D // lax.axis_size("row")
    heads = width_out // HEAD
    order = row_order()
    own = block_input.shape[0] // n_col
    row = lax.axis_index("row").astype(jnp.int32).reshape(1)
    c = lax.axis_index("col")

    x_own = turn_cols(block_input, 0, 1)
    vectors = lax.all_gather(
        jnp.stack([ln1_gain, ln1_bias, ln2_gain, ln2_bias, out_bias, down_bias]), "col", axis=1, tiled=True
    )
    gain1, bias1, gain2, bias2, bias_out, bias_down = [vectors[i] for i in range(6)]
    w_qkv = lax.all_gather(qkv_weight.reshape(width_in, 3 * width_out), "col", axis=0, tiled=True)
    w_out = lax.all_gather(out_weight.reshape(width_out, width_in), "col", axis=1, tiled=True)
    w_up = lax.all_gather(up_weight, "col", axis=0, tiled=True)
    w_down = lax.all_gather(down_weight, "col", axis=0, tiled=True)
    g_own = turn_cols(out_grad, 0, 1)

    x_all = gather_row(x_own)
    centred1, inverse1 = norm_stats(x_all.astype(f32))
    a1 = (centred1 * gain1 + bias1).astype(bf16)
    shifts = jnp.concatenate([qv_bias[0], jnp.zeros_like(qv_bias[0]), qv_bias[1]])
    qkv = (dot_nn(a1, w_qkv) + shifts).astype(bf16)
    qkv_head = to_heads(qkv, 3)
    attended = from_heads(attention_forward(row, qkv_head, order, own), 1, heads)

    resid1 = x_own.astype(f32) + scatter_row(dot_nn(attended, w_out)) + bias_out
    centred2, inverse2 = norm_stats(resid1)
    a2 = gather_row((centred2 * gain2 + bias2).astype(bf16))
    g_all = gather_row(g_own)
    d_act = dot_nn(g_all, w_down)
    pre = dot_nn(a2, w_up) + up_bias
    act = gelu_tanh(pre).astype(bf16)
    d_pre = jax.vjp(gelu_tanh, pre)[1](d_act)[0].astype(bf16)

    d_a2 = scatter_row(dot_nt(d_pre, w_up))
    d_resid1 = g_own.astype(f32) + norm_back(d_a2, centred2, inverse2, gain2)
    gp = d_resid1.astype(bf16)
    gp_all = gather_row(gp)
    d_attended = dot_nt(gp_all, w_out).astype(bf16)
    d_head = to_heads(d_attended, 1)

    block_out = resid1 + scatter_row(dot_nt(act, w_down)) + bias_down
    block_output = turn_cols(block_out.astype(bf16), 1, 0)
    d_down = sum_grad(dot_tn(g_all, act).reshape(n_col, width_in, -1))
    d_up = sum_grad(dot_tn(a2, d_pre).reshape(n_col, width_in, -1))
    d_out = sum_grad(dot_tn(attended, gp_all).reshape(width_out, n_col, width_in).transpose(1, 0, 2))

    d_qkv = from_heads(attention_backward(row, qkv_head, d_head, order, own), 3, heads)
    d_a1_part = dot_nt(d_qkv, w_qkv)
    d_a1 = scatter_row(d_a1_part)
    input_grad = d_resid1 + norm_back(d_a1, centred1[:own], inverse1[:own], gain1)
    input_grad = turn_cols(input_grad.astype(bf16), 1, 0)
    d_qkv_w = sum_grad(dot_tn(a1, d_qkv).reshape(n_col, width_in, -1))

    sums_early = lax.psum(
        jnp.stack([column_sums(d_a2 * centred2), column_sums(d_a2), column_sums(gp), column_sums(g_own)]),
        ("dp", "row", "col"),
    )
    sums_late = lax.psum(jnp.stack([column_sums(d_a1_part * centred1), column_sums(d_a1_part)]), ("dp", "row", "col"))
    mine = lax.dynamic_slice_in_dim(jnp.concatenate([sums_late, sums_early]), c * width_in, width_in, 1)
    d_up_bias = lax.psum(column_sums(d_pre), ("dp", "col"))
    d_qkv_bias = lax.psum(column_sums(d_qkv), ("dp", "col")).reshape(3, width_out)
    d_qv_bias = jnp.stack([d_qkv_bias[0], d_qkv_bias[2]])

    return (
        block_output,
        input_grad,
        mine[0],
        mine[1],
        d_qkv_w.reshape(1, 1, -1),
        d_qv_bias,
        d_out.reshape(1, 1, -1),
        mine[4],
        mine[2],
        mine[3],
        d_up,
        d_up_bias,
        d_down,
        mine[5],
    )


def solution(mesh):
    in_specs = (
        P(("dp", "row"), "col"),
        P("col"),
        P("col"),
        P("col", "row", None),
        P(None, "row"),
        P("row", "col", None),
        P("col"),
        P("col"),
        P("col"),
        P("col", "row"),
        P("row"),
        P("col", "row"),
        P("col"),
        P(("dp", "row"), "col"),
    )
    out_specs = (
        P(("dp", "row"), "col"),
        P(("dp", "row"), "col"),
        P("col"),
        P("col"),
        P("col", "row", None),
        P(None, "row"),
        P("row", "col", None),
        P("col"),
        P("col"),
        P("col"),
        P("col", "row"),
        P("row"),
        P("col", "row"),
        P("col"),
    )
    return jax.shard_map(body, mesh=mesh, in_specs=in_specs, out_specs=out_specs, check_vma=False)
```

time: 622 us -> 341 us (0.55)
  waiting for transfers between devices: 378 us -> 66.7 us
  starting transfers between devices: 0.76 us -> 69.3 us
  matrix products: 40.7 us -> 13.7 us
  other arithmetic: 39.7 us -> 16.3 us
  local copies, waits for them, and re-layouts: 10.4 us -> 24.1 us
  blocking collectives: 137 us -> 127 us
  Pallas kernels: 0 us -> 6.78 us
    reduce_scatter x10 -> x0, waiting for transfers between devices: 249 us -> none  [the longest x4 163 us: sum_over_cols(): lax.psum_scatter(term(jnp.int32(0), share * lax.axis_size('col')), 'col',...]
    all_gather x3 -> x2, waiting for transfers between devices: 101 us -> 8.51 us  [the longest x1 8.51 us: body(): w_down = lax.all_gather(down_weight, 'col', axis=0, tiled=True)]
    ppermute x0 -> x36, starting transfers between devices: none -> 34.7 us  [the longest x12 17.4 us: sum_cols(): lax.ppermute(piece, 'col', [(i, (i + k) % n) for i in range(n)]).astype(f32)]
    all_to_all x0 -> x8, starting transfers between devices: none -> 34.5 us  [turn_cols(): return lax.all_to_all(value, 'col', split, concat, tiled=True)]
    ppermute x0 -> x36, waiting for transfers between devices: none -> 29.5 us  [the longest x24 22.1 us: swap(): return lax.ppermute(value, axis, [(i, i ^ bit) for i in range(n)])]
    all_to_all x0 -> x8, waiting for transfers between devices: none -> 28 us  [turn_cols(): return lax.all_to_all(value, 'col', split, concat, tiled=True)]
    psum x1 -> x0, waiting for transfers between devices: 27.3 us -> none  [body(): lax.psum(d_qkv_weight.astype(jnp.bfloat16), 'dp').astype(jnp.float32)]
    dot_general x30 -> x12, matrix products: 40.7 us -> 13.7 us  [the longest x4 5.89 us: dot_nn(): lax.dot_general(a, b, (((1,), (0,)), ((), ())), preferred_element_type=f32)]
  transfers between devices with their start and end apart: 14 -> 46, of which waited for: 13 -> 18; matrix products, arithmetic and copies ran while one was open for 7% -> 13% of each run, Pallas kernels for 0% -> 2%
where the time goes in v1:
time: 341 us; the launch traced here: 339 us
  blocking collectives  127 us (37%)
  starting transfers between devices  69.3 us (20%)
  waiting for transfers between devices  66.7 us (20%)
  local copies, waits for them, and re-layouts  24.1 us (7%)
  other arithmetic  16.3 us (5%)
  between operations  15.1 us (4%)
  matrix products  13.7 us (4%)
  Pallas kernels  6.78 us (2%)
    psum x1, blocking collectives, body(): lax.psum(jnp.stack([column_sums(d_a1_part * centred1), column_sums(d_a1_p...  39.5 us
    all_gather x1, blocking collectives, body(): lax.all_gather(qkv_weight.reshape(width_in, 3 * width_out), 'col', axis=0...  36.7 us
    all_to_all x8, starting transfers between devices, turn_cols(): return lax.all_to_all(value, 'col', split, concat, tiled=True)  34.5 us
    all_to_all x8, waiting for transfers between devices, turn_cols(): return lax.all_to_all(value, 'col', split, concat, tiled=True)  28 us
    ppermute x24, waiting for transfers between devices, swap(): return lax.ppermute(value, axis, [(i, i ^ bit) for i in range(n)])  22.1 us
    psum x1, blocking collectives, body(): lax.psum(column_sums(d_qkv), ('dp', 'col')).reshape(3, width_out)  22 us
    ppermute x12, starting transfers between devices, sum_cols(): lax.ppermute(piece, 'col', [(i, (i + k) % n) for i in range(n)]).astype(f32)  17.4 us
    ppermute x24, starting transfers between devices, swap(): return lax.ppermute(value, axis, [(i, i ^ bit) for i in range(n)])  17.4 us
  transfers between devices with their start and end apart: 46, of which 18 were waited for; matrix products, arithmetic and copies ran while one was open for 13% of the time, Pallas kernels for 2%

profile of v1, /device:TPU:0, one launch (start us, length us, event | category | flops | bytes accessed | tf_op | source)
XLA Modules:
  0.0 339.4 jit_solution(17155261205889196526)
XLA Ops:
  9.6 6.3 %all-to-all-start = ((bf16[4,64,192]{2,1,0:T(8,128)(2,1)}), bf16[4,64,192]{2,1,0:T(8,128)(2,1)S(1)}, u32[]{:S(2)}, u32[]{:S(2)}) async-start(bf16[4,64,192]{2,1,0:T(8,128)(2,1)} %bitcast), calls=%async_computation | async-start | bytes 262144 | tf_op jit(solution)/shard_map/all_to_all | solution.py:65
  18.4 36.7 %all_gather.16 = bf16[768,576]{1,0:T(8,128)(2,1)S(1)} all-gather(bf16[192,576]{1,0:T(8,128)(2,1)S(1)} %reshape.218), channel_id=1, replica_groups=mesh['dp'=2,'row'=4,'col'=4] {'col'}, dimensions={0}, use_global_device_ids=true | all-gather | bytes 1105920 | tf_op jit(solution)/shard_map/all_gather | solution.py:280
  60.3 13.6 %all-gather = f32[4,192,6]{1,2,0:T(8,128)S(1)} all-gather(f32[1,192,6]{1,2,0:T(8,128)S(1)} %bitcast.170), channel_id=1, replica_groups=mesh['dp'=2,'row'=4,'col'=4] {'col'}, dimensions={0}, use_global_device_ids=true | all-gather | bytes 23040 | tf_op jit(solution)/shard_map/all_gather | solution.py:276
  75.9 5.1 %all-to-all-start.1 = ((bf16[4,256,192]{1,2,0:T(8,128)(2,1)}), bf16[4,256,192]{1,2,0:T(8,128)(2,1)S(1)}, u32[]{:S(2)}, u32[]{:S(2)}) async-start(bf16[4,256,192]{1,2,0:T(8,128)(2,1)} %concatenate.55), calls=%async_computation.1 | async-start | bytes 786432 | tf_op jit(solution)/shard_map/all_to_all | solution.py:65
  81.0 9.4 %all-to-all-done.1 = bf16[4,256,192]{1,2,0:T(8,128)(2,1)S(1)} async-done(((bf16[4,256,192]{1,2,0:T(8,128)(2,1)}), bf16[4,256,192]{1,2,0:T(8,128)(2,1)S(1)}, u32[]{:S(2)}, u32[]{:S(2)}) %all-to-all-start.1) | async-done | bytes 393248 | tf_op jit(solution)/shard_map/all_to_all | solution.py:65
  93.8 3.3 all-to-all-start.2
  98.6 15.6 %all_gather.17 = bf16[192,768]{0,1:T(8,128)(2,1)S(1)} all-gather(bf16[192,192]{0,1:T(8,128)(2,1)S(1)} %copy.82), channel_id=1, replica_groups=mesh['dp'=2,'row'=4,'col'=4] {'col'}, dimensions={1}, use_global_device_ids=true | all-gather | bytes 368640 | tf_op jit(solution)/shard_map/all_gather | solution.py:281
  114.2 3.9 %all-to-all-start.4 = ((bf16[4,64,192]{2,1,0:T(8,128)(2,1)}), bf16[4,64,192]{2,1,0:T(8,128)(2,1)S(1)}, u32[]{:S(2)}, u32[]{:S(2)}) async-start(bf16[4,64,192]{2,1,0:T(8,128)(2,1)} %bitcast.22), calls=%async_computation.4 | async-start | bytes 262144 | tf_op jit(solution)/shard_map/all_to_all | solution.py:65
  119.1 4.8 %all-to-all-done.4 = bf16[4,64,192]{2,1,0:T(8,128)(2,1)S(1)} async-done(((bf16[4,64,192]{2,1,0:T(8,128)(2,1)}), bf16[4,64,192]{2,1,0:T(8,128)(2,1)S(1)}, u32[]{:S(2)}, u32[]{:S(2)}) %all-to-all-start.4) | async-done | bytes 98336 | tf_op jit(solution)/shard_map/all_to_all | solution.py:65
  128.1 3.4 collective-permute-done.3
  132.9 3.5 %collective-permute-done.4 = bf16[64,768]{1,0:T(8,128)(2,1)S(1)} collective-permute-done((bf16[64,768]{1,0:T(8,128)(2,1)S(1)}, bf16[64,768]{1,0:T(8,128)(2,1)S(1)}, u32[]{:S(2)}, u32[]{:S(2)}) %collective-permute-start.4) | collective-permute-done | bytes 98336 | tf_op jit(solution)/shard_map/ppermute | solution.py:31
  143.8 8.5 %all-gather.6.cloned.1.call-done = bf16[768,768]{1,0:T(8,128)(2,1)} async-done(((bf16[192,768]{1,0:T(8,128)(2,1)}), bf16[768,768]{1,0:T(8,128)(2,1)}) %all-gather.6.cloned.1.call-update) | async-done | bytes 1179664 | tf_op jit(solution)/shard_map/all_gather | solution.py:283
  176.0 5.2 %all-to-all-done.3 = bf16[64,4,192]{2,0,1:T(8,128)(2,1)S(1)} async-done(((bf16[64,4,192]{2,0,1:T(8,128)(2,1)}), bf16[64,4,192]{2,0,1:T(8,128)(2,1)S(1)}, u32[]{:S(2)}, u32[]{:S(2)}) %all-to-all-start.3) | async-done | bytes 98336 | tf_op jit(solution)/shard_map/all_to_all | solution.py:65
  198.0 4.6 %all-to-all-start.5 = ((bf16[4,256,64]{1,2,0:T(8,128)(2,1)}), bf16[4,256,64]{1,2,0:T(8,128)(2,1)S(1)}, u32[]{:S(2)}, u32[]{:S(2)}) async-start(bf16[4,256,64]{1,2,0:T(8,128)(2,1)} %concatenate.62), calls=%async_computation.5 | async-start | bytes 262144 | tf_op jit(solution)/shard_map/all_to_all | solution.py:65
  202.6 3.8 %collective-permute-start.29 = (bf16[96,768]{1,0:T(8,128)(2,1)}, bf16[96,768]{1,0:T(8,128)(2,1)S(1)}, u32[]{:S(2)}, u32[]{:S(2)}) collective-permute-start(bf16[96,768]{1,0:T(8,128)(2,1)} %get-tuple-element.88), channel_id=1, source_target_pairs={{0,3},{1,0},{2,1},{3,2},{4,7},{5,4},{6,5},{7,6},{8,11},{9,8},{10,9... | collective-permute-start | bytes 442376 | tf_op jit(solution)/shard_map/ppermute | solution.py:74
  207.5 3.8 %collective-permute-start.24 = (bf16[96,192]{1,0:T(8,128)(2,1)S(1)}, bf16[96,192]{1,0:T(8,128)(2,1)S(1)}, u32[]{:S(2)}, u32[]{:S(2)}) collective-permute-start(bf16[96,192]{1,0:T(8,128)(2,1)S(1)} %get-tuple-element.102), channel_id=1, source_target_pairs={{0,3},{1,0},{2,1},{3,2},{4,7},{5,4},{6,5},{7,6},{8,11},{9,8},{10,9... | collective-permute-start | bytes 110600 | tf_op jit(solution)/shard_map/ppermute | solution.py:74
  222.2 4.4 %shard_map.246 = bf16[4,256,192]{2,1,0:T(8,128)(2,1)S(1)} custom-call(s32[1]{0:T(128)} %bitcast.2.refs_0_, bf16[4,256,192]{2,1,0:T(8,128)(2,1)S(1)} %copy.80.refs_1_, bf16[4,256,64]{2,1,0:T(8,128)(2,1)S(1)} %copy.87.refs_2_), custom_call_target="tpu_custom_call" | custom-call | tf_op jit(solution)/shard_map/pallas_call | solution.py:193
  227.6 3.9 %all-to-all-start.6 = ((bf16[4,256,192]{1,2,0:T(8,128)(2,1)}), bf16[4,256,192]{1,2,0:T(8,128)(2,1)S(1)}, u32[]{:S(2)}, u32[]{:S(2)}) async-start(bf16[4,256,192]{1,2,0:T(8,128)(2,1)} %copy.88), calls=%async_computation.6 | async-start | bytes 786432 | tf_op jit(solution)/shard_map/all_to_all | solution.py:65
  234.1 6.2 %all-to-all-done.6 = bf16[4,256,192]{1,2,0:T(8,128)(2,1)S(1)} async-done(((bf16[4,256,192]{1,2,0:T(8,128)(2,1)}), bf16[4,256,192]{1,2,0:T(8,128)(2,1)S(1)}, u32[]{:S(2)}, u32[]{:S(2)}) %all-to-all-start.6) | async-done | bytes 393248 | tf_op jit(solution)/shard_map/all_to_all | solution.py:65
  242.0 39.5 %all-reduce.2 = (f32[2,768]{1,0:T(2,128)S(1)}, f32[4,768]{1,0:T(4,128)S(1)}) all-reduce(f32[2,768]{1,0:T(2,128)S(1)} %pad_maximum_fusion.11, f32[4,768]{1,0:T(4,128)S(1)} %copy-done.17), channel_id=1, replica_groups=mesh['dp'=2,'row'=4,'col'=4] {'dp','row','col'}, use_global_device_ids=true, to_apply=%region_10.11 | all-reduce | flops 4608 | bytes 36864 | tf_op jit(solution)/shard_map/psum | solution.py:327
  282.4 22.0 %all-reduce.3 = (f32[576]{0:T(1024)S(1)}, f32[768]{0:T(1024)}) all-reduce(f32[576]{0:T(1024)S(1)} %reduce_sum.161, f32[768]{0:T(1024)S(1)} %copy-done.24), channel_id=1, replica_groups=mesh['dp'=2,'row'=4,'col'=4] {'dp','col'}, use_global_device_ids=true, to_apply=%region_17.18 | all-reduce | flops 1344 | bytes 10752 | tf_op jit(solution)/shard_map/psum | solution.py:330
  309.8 5.2 %collective-permute-done.16 = bf16[4,96,576]{2,1,0:T(8,128)(2,1)S(1)} collective-permute-done((bf16[4,96,576]{2,1,0:T(8,128)(2,1)S(1)}, bf16[4,96,576]{2,1,0:T(8,128)(2,1)S(1)}, u32[]{:S(2)}, u32[]{:S(2)}) %collective-permute-start.16) | collective-permute-done | bytes 442400 | tf_op jit(solution)/shard_map/ppermute | solution.py:31
  315.2 3.8 %collective-permute-start.19 = (bf16[96,576]{1,0:T(8,128)(2,1)S(1)}, bf16[96,576]{1,0:T(8,128)(2,1)S(1)}, u32[]{:S(2)}, u32[]{:S(2)}) collective-permute-start(bf16[96,576]{1,0:T(8,128)(2,1)S(1)} %get-tuple-element.91), channel_id=1, source_target_pairs={{0,3},{1,0},{2,1},{3,2},{4,7},{5,4},{6,5},{7,6},{8,11},{9,8},{10,9... | collective-permute-start | bytes 331784 | tf_op jit(solution)/shard_map/ppermute | solution.py:74
  320.0 4.2 %all-to-all-start.7 = ((bf16[64,4,192]{2,0,1:T(8,128)(2,1)}), bf16[64,4,192]{2,0,1:T(8,128)(2,1)S(1)}, u32[]{:S(2)}, u32[]{:S(2)}) async-start(bf16[64,4,192]{2,0,1:T(8,128)(2,1)} %copy.90), calls=%async_computation.7 | async-start | bytes 262144 | tf_op jit(solution)/shard_map/all_to_all | solution.py:65
  (279 shorter events, 103.6 us)
Async XLA Ops:
  7.2 131.2 %all-gather.4.cloned.1.call-start = ((), (), s32[]{:S(2)}) async-start(), calls=%async_computation.8 | async-start | bytes 1474560 | tf_op jit(solution)/shard_map/all_gather | solution.py:282
  9.6 45.6 %all-to-all-start = ((bf16[4,64,192]{2,1,0:T(8,128)(2,1)}), bf16[4,64,192]{2,1,0:T(8,128)(2,1)S(1)}, u32[]{:S(2)}, u32[]{:S(2)}) async-start(bf16[4,64,192]{2,1,0:T(8,128)(2,1)} %bitcast), calls=%async_computation | async-start | bytes 262144 | tf_op jit(solution)/shard_map/all_to_all | solution.py:65
  60.1 14.0 %collective-permute-start.1 = (bf16[128,768]{1,0:T(8,128)(2,1)S(1)}, bf16[128,768]{1,0:T(8,128)(2,1)S(1)}, u32[]{:S(2)}, u32[]{:S(2)}) collective-permute-start(bf16[128,768]{1,0:T(8,128)(2,1)S(1)} %pad_maximum_fusion.3), channel_id=1, source_target_pairs={{0,4},{4,0},{8,12},{12,8},{1,5},{5,1},{9,13},{13,9},{2,6},{6,2},{1... | collective-permute-start | bytes 589832 | tf_op jit(solution)/shard_map/ppermute | solution.py:31
  75.9 14.5 %all-to-all-start.1 = ((bf16[4,256,192]{1,2,0:T(8,128)(2,1)}), bf16[4,256,192]{1,2,0:T(8,128)(2,1)S(1)}, u32[]{:S(2)}, u32[]{:S(2)}) async-start(bf16[4,256,192]{1,2,0:T(8,128)(2,1)} %concatenate.55), calls=%async_computation.1 | async-start | bytes 786432 | tf_op jit(solution)/shard_map/all_to_all | solution.py:65
  93.8 20.3 %all-to-all-start.2 = ((bf16[4,256,64]{1,2,0:T(8,128)(2,1)}), bf16[4,256,64]{1,2,0:T(8,128)(2,1)S(1)}, u32[]{:S(2)}, u32[]{:S(2)}) async-start(bf16[4,256,64]{1,2,0:T(8,128)(2,1)} %copy.81), calls=%async_computation.2 | async-start | bytes 262144 | tf_op jit(solution)/shard_map/all_to_all | solution.py:65
  114.2 9.8 %all-to-all-start.4 = ((bf16[4,64,192]{2,1,0:T(8,128)(2,1)}), bf16[4,64,192]{2,1,0:T(8,128)(2,1)S(1)}, u32[]{:S(2)}, u32[]{:S(2)}) async-start(bf16[4,64,192]{2,1,0:T(8,128)(2,1)} %bitcast.22), calls=%async_computation.4 | async-start | bytes 262144 | tf_op jit(solution)/shard_map/all_to_all | solution.py:65
  118.0 34.3 %all-gather.6.cloned.1.call-start = ((), (), s32[]{:S(2)}) async-start(), calls=%async_computation.9 | async-start | bytes 1474560 | tf_op jit(solution)/shard_map/all_gather | solution.py:283
  159.0 22.9 %collective-permute-start.31 = (bf16[4,96,768]{2,1,0:T(8,128)(2,1)}, bf16[4,96,768]{2,1,0:T(8,128)(2,1)}, u32[]{:S(2)}, u32[]{:S(2)}) collective-permute-start(bf16[4,96,768]{2,1,0:T(8,128)(2,1)} %dynamic-slice_bitcast_fusion), channel_id=1, source_target_pairs={{0,16},{16,0},{1,17},{17,1},{2,18},{18,2},{3,19},{19,3},{4,20},{20... | collective-permute-start | bytes 1769480 | tf_op jit(solution)/shard_map/ppermute | solution.py:31
  162.0 26.0 %collective-permute-start.26 = (bf16[4,96,768]{2,1,0:T(8,128)(2,1)}, bf16[4,96,768]{2,1,0:T(8,128)(2,1)}, u32[]{:S(2)}, u32[]{:S(2)}) collective-permute-start(bf16[4,96,768]{2,1,0:T(8,128)(2,1)} %dynamic-slice_bitcast_fusion.1), channel_id=1, source_target_pairs={{0,16},{16,0},{1,17},{17,1},{2,18},{18,2},{3,19},{19,3},{4,20},{20... | collective-permute-start | bytes 1769480 | tf_op jit(solution)/shard_map/ppermute | solution.py:31
  171.9 9.2 %all-to-all-start.3 = ((bf16[64,4,192]{2,0,1:T(8,128)(2,1)}), bf16[64,4,192]{2,0,1:T(8,128)(2,1)S(1)}, u32[]{:S(2)}, u32[]{:S(2)}) async-start(bf16[64,4,192]{2,0,1:T(8,128)(2,1)} %copy.83), calls=%async_computation.3 | async-start | bytes 262144 | tf_op jit(solution)/shard_map/all_to_all | solution.py:65
  175.9 14.7 %collective-permute-start.13 = (bf16[128,768]{1,0:T(8,128)(2,1)S(1)}, bf16[128,768]{1,0:T(8,128)(2,1)}, u32[]{:S(2)}, u32[]{:S(2)}) collective-permute-start(bf16[128,768]{1,0:T(8,128)(2,1)S(1)} %pad_maximum_fusion.6), channel_id=1, source_target_pairs={{0,4},{4,0},{8,12},{12,8},{1,5},{5,1},{9,13},{13,9},{2,6},{6,2},{1... | collective-permute-start | bytes 589832 | tf_op jit(solution)/shard_map/ppermute | solution.py:31
  184.2 23.2 %collective-permute-start.32 = (bf16[96,768]{1,0:T(8,128)(2,1)}, bf16[96,768]{1,0:T(8,128)(2,1)}, u32[]{:S(2)}, u32[]{:S(2)}) collective-permute-start(bf16[96,768]{1,0:T(8,128)(2,1)} %get-tuple-element.84), channel_id=1, source_target_pairs={{0,1},{1,2},{2,3},{3,0},{4,5},{5,6},{6,7},{7,4},{8,9},{9,10},{10,1... | collective-permute-start | bytes 442376 | tf_op jit(solution)/shard_map/ppermute | solution.py:74
  185.5 22.0 %collective-permute-start.34 = (bf16[96,768]{1,0:T(8,128)(2,1)}, bf16[96,768]{1,0:T(8,128)(2,1)}, u32[]{:S(2)}, u32[]{:S(2)}) collective-permute-start(bf16[96,768]{1,0:T(8,128)(2,1)} %get-tuple-element.85), channel_id=1, source_target_pairs={{0,3},{1,0},{2,1},{3,2},{4,7},{5,4},{6,5},{7,6},{8,11},{9,8},{10,9... | collective-permute-start | bytes 442376 | tf_op jit(solution)/shard_map/ppermute | solution.py:74
  188.0 23.3 %collective-permute-start.33 = (bf16[96,768]{1,0:T(8,128)(2,1)}, bf16[96,768]{1,0:T(8,128)(2,1)}, u32[]{:S(2)}, u32[]{:S(2)}) collective-permute-start(bf16[96,768]{1,0:T(8,128)(2,1)} %get-tuple-element.86), channel_id=1, source_target_pairs={{0,2},{1,3},{2,0},{3,1},{4,6},{5,7},{6,4},{7,5},{8,10},{9,11},{10,... | collective-permute-start | bytes 442376 | tf_op jit(solution)/shard_map/ppermute | solution.py:74
  190.1 27.5 %collective-permute-start.27 = (bf16[96,768]{1,0:T(8,128)(2,1)}, bf16[96,768]{1,0:T(8,128)(2,1)}, u32[]{:S(2)}, u32[]{:S(2)}) collective-permute-start(bf16[96,768]{1,0:T(8,128)(2,1)} %get-tuple-element.87), channel_id=1, source_target_pairs={{0,1},{1,2},{2,3},{3,0},{4,5},{5,6},{6,7},{7,4},{8,9},{9,10},{10,1... | collective-permute-start | bytes 442376 | tf_op jit(solution)/shard_map/ppermute | solution.py:74
  198.0 24.0 %all-to-all-start.5 = ((bf16[4,256,64]{1,2,0:T(8,128)(2,1)}), bf16[4,256,64]{1,2,0:T(8,128)(2,1)S(1)}, u32[]{:S(2)}, u32[]{:S(2)}) async-start(bf16[4,256,64]{1,2,0:T(8,128)(2,1)} %concatenate.62), calls=%async_computation.5 | async-start | bytes 262144 | tf_op jit(solution)/shard_map/all_to_all | solution.py:65
  202.6 15.0 %collective-permute-start.29 = (bf16[96,768]{1,0:T(8,128)(2,1)}, bf16[96,768]{1,0:T(8,128)(2,1)S(1)}, u32[]{:S(2)}, u32[]{:S(2)}) collective-permute-start(bf16[96,768]{1,0:T(8,128)(2,1)} %get-tuple-element.88), channel_id=1, source_target_pairs={{0,3},{1,0},{2,1},{3,2},{4,7},{5,4},{6,5},{7,6},{8,11},{9,8},{10,9... | collective-permute-start | bytes 442376 | tf_op jit(solution)/shard_map/ppermute | solution.py:74
  215.5 16.9 %collective-permute-start.35 = (bf16[96,768]{1,0:T(8,128)(2,1)S(1)}, bf16[96,768]{1,0:T(8,128)(2,1)S(1)}, u32[]{:S(2)}, u32[]{:S(2)}) collective-permute-start(bf16[96,768]{1,0:T(8,128)(2,1)S(1)} %fusion.16), channel_id=1, source_target_pairs={{0,16},{16,0},{1,17},{17,1},{2,18},{18,2},{3,19},{19,3},{4,20},{20... | collective-permute-start | bytes 442376 | tf_op jit(solution)/shard_map/ppermute | solution.py:31
  216.9 14.5 %collective-permute-start.25 = (bf16[96,192]{1,0:T(8,128)(2,1)S(1)}, bf16[96,192]{1,0:T(8,128)(2,1)S(1)}, u32[]{:S(2)}, u32[]{:S(2)}) collective-permute-start(bf16[96,192]{1,0:T(8,128)(2,1)S(1)} %fusion.33), channel_id=1, source_target_pairs={{0,16},{16,0},{1,17},{17,1},{2,18},{18,2},{3,19},{19,3},{4,20},{20... | collective-permute-start | bytes 110600 | tf_op jit(solution)/shard_map/ppermute | solution.py:31
  221.5 11.7 %collective-permute-start.30 = (bf16[96,768]{1,0:T(8,128)(2,1)S(1)}, bf16[96,768]{1,0:T(8,128)(2,1)S(1)}, u32[]{:S(2)}, u32[]{:S(2)}) collective-permute-start(bf16[96,768]{1,0:T(8,128)(2,1)S(1)} %fusion.19), channel_id=1, source_target_pairs={{0,16},{16,0},{1,17},{17,1},{2,18},{18,2},{3,19},{19,3},{4,20},{20... | collective-permute-start | bytes 442376 | tf_op jit(solution)/shard_map/ppermute | solution.py:31
  227.6 12.7 %all-to-all-start.6 = ((bf16[4,256,192]{1,2,0:T(8,128)(2,1)}), bf16[4,256,192]{1,2,0:T(8,128)(2,1)S(1)}, u32[]{:S(2)}, u32[]{:S(2)}) async-start(bf16[4,256,192]{1,2,0:T(8,128)(2,1)} %copy.88), calls=%async_computation.6 | async-start | bytes 786432 | tf_op jit(solution)/shard_map/all_to_all | solution.py:65
  241.2 63.6 %collective-permute-start.14 = (bf16[128,768]{1,0:T(8,128)(2,1)S(1)}, bf16[128,768]{1,0:T(8,128)(2,1)S(1)}, u32[]{:S(2)}, u32[]{:S(2)}) collective-permute-start(bf16[128,768]{1,0:T(8,128)(2,1)S(1)} %slice.244), channel_id=1, source_target_pairs={{0,4},{4,0},{8,12},{12,8},{1,5},{5,1},{9,13},{13,9},{2,6},{6,2},{1... | collective-permute-start | bytes 589832 | tf_op jit(solution)/shard_map/ppermute | solution.py:31
  315.2 9.0 %collective-permute-start.17 = (bf16[96,576]{1,0:T(8,128)(2,1)S(1)}, bf16[96,576]{1,0:T(8,128)(2,1)S(1)}, u32[]{:S(2)}, u32[]{:S(2)}) collective-permute-start(bf16[96,576]{1,0:T(8,128)(2,1)S(1)} %get-tuple-element.90), channel_id=1, source_target_pairs={{0,1},{1,2},{2,3},{3,0},{4,5},{5,6},{6,7},{7,4},{8,9},{9,10},{10,1... | collective-permute-start | bytes 331784 | tf_op jit(solution)/shard_map/ppermute | solution.py:74
  320.0 10.1 %all-to-all-start.7 = ((bf16[64,4,192]{2,0,1:T(8,128)(2,1)}), bf16[64,4,192]{2,0,1:T(8,128)(2,1)S(1)}, u32[]{:S(2)}, u32[]{:S(2)}) async-start(bf16[64,4,192]{2,0,1:T(8,128)(2,1)} %copy.90), calls=%async_computation.7 | async-start | bytes 262144 | tf_op jit(solution)/shard_map/all_to_all | solution.py:65
  (61 other events, 647.9 us)
Sparse Core Ops, SparseCore 0:
  9.6 48.9 all-gather.3
  120.4 31.8 all-gather.5

commit v2 on v1

v2 whole, which is shorter than its diff:
```python
import functools
import math

import jax
import jax.numpy as jnp
from jax import lax
from jax.experimental import pallas as pl
from jax.experimental.pallas import tpu as pltpu
from jax.sharding import PartitionSpec as P

D = 768
HEAD = 64
SCALE = 1.0 / math.sqrt(HEAD)
C0 = math.sqrt(2.0 / math.pi)
C1 = 0.044715
bf16 = jnp.bfloat16
f32 = jnp.float32
VMEM = pl.BlockSpec(memory_space=pltpu.VMEM)
SMEM = pl.BlockSpec(memory_space=pltpu.SMEM)


def dot_nn(a, b):
    return lax.dot_general(a, b, (((1,), (0,)), ((), ())), preferred_element_type=f32)


def dot_nt(a, b):
    return lax.dot_general(a, b, (((1,), (1,)), ((), ())), preferred_element_type=f32)


def dot_tn(a, b):
    return lax.dot_general(a, b, (((0,), (0,)), ((), ())), preferred_element_type=f32)


def call(kernel, outs, scalars, args, scratch=()):
    return pl.pallas_call(
        kernel,
        out_shape=[jax.ShapeDtypeStruct(s, t) for s, t in outs],
        in_specs=[SMEM] + [VMEM] * len(args),
        out_specs=[VMEM] * len(outs),
        scratch_shapes=[pltpu.VMEM(s, t) for s, t in scratch],
        compiler_params=pltpu.CompilerParams(vmem_limit_bytes=40 * 1024 * 1024),
    )(scalars, *args)


def swap(value, axis, bit, low=0, high=None):
    n = lax.axis_size(axis)
    return lax.ppermute(value, axis, [(i, i ^ bit) for i in range(n)])


def swap_some(value, axis, bit, sources, targets):
    n = lax.axis_size(axis)
    return lax.ppermute(value, axis, [(i, i ^ bit) for i in range(n) if i < sources and i ^ bit < targets])


def bits_of(axis, first=1):
    n = lax.axis_size(axis)
    bits = []
    b = first
    while b < n:
        bits.append(b)
        b *= 2
    return bits


def row_order():
    order = [0]
    for b in reversed(bits_of("row")):
        order = order + [o ^ b for o in order]
    return order


def gather_row(value):
    pieces = [value]
    for b in reversed(bits_of("row")):
        pieces = pieces + [swap(p, "row", b) for p in pieces]
    return pieces


def finish_row(keep, send):
    bits = bits_of("row")
    total = keep + swap(send, "row", bits[0]).astype(f32)
    for b in bits[1:]:
        half = total.shape[0] // 2
        total = total[:half] + swap(total[half:].astype(bf16), "row", b).astype(f32)
    return total


def by_column(pieces, c):
    pieces = list(pieces)
    bit = 1
    while bit < len(pieces):
        on = (c & bit) != 0
        pieces = [jnp.where(on, pieces[i ^ bit], pieces[i]) for i in range(len(pieces))]
        bit *= 2
    return pieces


def turn_in(value, c):
    n = lax.axis_size("col")
    t = value.shape[0] // n
    cut = [lax.dynamic_slice_in_dim(value, (c ^ k) * t, t, 0) for k in range(n)]
    return jnp.concatenate([cut[0]] + [swap(cut[k], "col", k) for k in range(1, n)], axis=1)


def turn_out(value, c):
    n = lax.axis_size("col")
    w = value.shape[1] // n
    cut = [value[:, k * w : (k + 1) * w] for k in range(n)]
    pieces = [cut[0]] + [swap(cut[k], "col", k) for k in range(1, n)]
    return jnp.concatenate(by_column(pieces, c), axis=0)


def sum_cols(parts):
    total = parts[0].astype(f32)
    for k in range(1, len(parts)):
        total = total + swap(parts[k].astype(bf16), "col", k).astype(f32)
    return total


def sum_dp(value, first):
    for b in bits_of("dp", first):
        value = (value.astype(f32) + swap(value.astype(bf16), "dp", b).astype(f32)).astype(bf16)
    return value


def sum_halves(mine, other):
    n_col = lax.axis_size("col")
    rows = mine.shape[0] // n_col
    got = swap(other, "dp", 1)
    parts = [
        (mine[k * rows : (k + 1) * rows].astype(f32) + got[k * rows : (k + 1) * rows].astype(f32)).astype(bf16)
        for k in range(n_col)
    ]
    total = sum_dp(sum_cols(parts).astype(bf16), 2)
    return total, swap(total, "dp", 1)


def place(scal, order, k, kk, chunk, n_col):
    at = ((scal[0] ^ order[kk]) * n_col + (scal[1] ^ k)) * chunk
    return pl.ds(pl.multiple_of(at, chunk), chunk)


def load_natural(scal, order, pieces, dst):
    chunk = pieces[0].shape[0] // len(order)
    for k, piece in enumerate(pieces):
        for kk in range(len(order)):
            dst[place(scal, order, k, kk, chunk, len(pieces)), :] = piece[kk * chunk : (kk + 1) * chunk, :]


def store_natural(scal, order, src, pieces):
    chunk = pieces[0].shape[0] // len(order)
    for k, piece in enumerate(pieces):
        for kk in range(len(order)):
            piece[kk * chunk : (kk + 1) * chunk, :] = src[place(scal, order, k, kk, chunk, len(pieces)), :]


def block_probs(q, k, block, i):
    scores = dot_nt(q, k) * SCALE
    rows = lax.broadcasted_iota(jnp.int32, scores.shape, 0) + i * block
    cols = lax.broadcasted_iota(jnp.int32, scores.shape, 1)
    scores = jnp.where(cols <= rows, scores, -1e30)
    top = jnp.max(scores, axis=-1, keepdims=True)
    e = jnp.exp(scores - top)
    return e / jnp.sum(e, axis=-1, keepdims=True)


def forward_kernel(order, n_col, scal, *refs):
    pieces, outs, (nat, res) = refs[:n_col], refs[n_col : 2 * n_col], refs[2 * n_col :]
    load_natural(scal, order, pieces, nat)
    block = nat.shape[0] // len(order)
    k = nat[:, HEAD : 2 * HEAD]
    v = nat[:, 2 * HEAD :]
    for i in range(len(order)):
        upto = (i + 1) * block
        p = block_probs(nat[i * block : upto, :HEAD], k[:upto], block, i)
        res[i * block : upto, :] = dot_nn(p.astype(bf16), v[:upto]).astype(bf16)
    store_natural(scal, order, res, outs)


def backward_kernel(order, n_col, scal, *refs):
    pieces, grads, outs = refs[:n_col], refs[n_col : 2 * n_col], refs[2 * n_col : 3 * n_col]
    nat, dnat, res, dkt, dvt = refs[3 * n_col :]
    load_natural(scal, order, pieces, nat)
    load_natural(scal, order, grads, dnat)
    block = nat.shape[0] // len(order)
    k = nat[:, HEAD : 2 * HEAD]
    v = nat[:, 2 * HEAD :]
    dkt[...] = jnp.zeros_like(dkt)
    dvt[...] = jnp.zeros_like(dvt)
    for i in range(len(order)):
        upto = (i + 1) * block
        q = nat[i * block : upto, :HEAD]
        do = dnat[i * block : upto, :]
        p = block_probs(q, k[:upto], block, i)
        dvt[:, :upto] += dot_tn(do, p.astype(bf16))
        dp = dot_nt(do, v[:upto])
        ds = (p * (dp - jnp.sum(dp * p, axis=-1, keepdims=True))).astype(bf16)
        res[i * block : upto, :HEAD] = (dot_nn(ds, k[:upto]) * SCALE).astype(bf16)
        dkt[:, :upto] += dot_tn(q, ds)
    res[:, HEAD : 2 * HEAD] = (dkt[...].T * SCALE).astype(bf16)
    res[:, 2 * HEAD :] = dvt[...].T.astype(bf16)
    store_natural(scal, order, res, outs)


def norm_stats(v):
    mean = jnp.sum(v, axis=-1, keepdims=True) / D
    var = jnp.sum(v * v, axis=-1, keepdims=True) / D - mean * mean
    inverse = lax.rsqrt(var + 1e-05)
    return (v - mean) * inverse, inverse


def norm_back(grad, centred, inverse, gain):
    scaled = grad * gain
    first = jnp.sum(scaled, axis=-1, keepdims=True) / D
    second = jnp.sum(scaled * centred, axis=-1, keepdims=True) / D
    return inverse * (scaled - first - centred * second)


def stacked(refs):
    return jnp.concatenate([r[...] for r in refs], axis=0)


def qkv_kernel(n_row, n_col, heads, scal, *refs):
    xs, refs = refs[:n_row], refs[n_row:]
    gain, bias, shifts, w_own = refs[:4]
    near, far = refs[4 : 3 + n_col], refs[3 + n_col : 2 + 2 * n_col]
    outs, (a1_out, w_all, cut) = refs[2 + 2 * n_col : 2 + 3 * n_col], refs[2 + 3 * n_col :]
    c, d = scal[1], scal[2]
    rows = w_own.shape[0]
    half = rows // 2
    w_all[:rows, :] = w_own[...]
    for k in range(1, n_col):
        w_all[pl.ds(pl.multiple_of(k * rows + d * half, 32), half), :] = near[k - 1][...]
        w_all[pl.ds(pl.multiple_of(k * rows + (1 - d) * half, 32), half), :] = far[k - 1][...]
    centred, _ = norm_stats(stacked(xs).astype(f32))
    a1 = (centred * gain[...] + bias[...]).astype(bf16)
    a1_out[...] = a1
    qkv = (dot_nn(a1, w_all[...]) + shifts[...]).astype(bf16)
    width = heads * HEAD
    for h in range(n_col):
        if h < heads:
            lo = h * HEAD
            piece = jnp.concatenate([qkv[:, j * width + lo : j * width + lo + HEAD] for j in range(3)], axis=1)
        else:
            piece = jnp.zeros((qkv.shape[0], 3 * HEAD), bf16)
        cut[h ^ c] = piece
    for k in range(n_col):
        outs[k][...] = cut[k]


def halves_out(value, keep, send):
    half = value.shape[0] // 2
    keep[...] = value[:half]
    send[...] = value[half:].astype(bf16)


def out_kernel(n_col, heads, scal, *refs):
    os, ws = refs[:n_col], refs[n_col : 2 * n_col]
    att_out, w_out, keep, send, cut = refs[2 * n_col :]
    c = scal[1]
    for k in range(n_col):
        cut[c ^ k] = os[k][...]
    att = jnp.concatenate([cut[h] for h in range(heads)], axis=1)
    w = jnp.concatenate([r[...] for r in ws], axis=1)
    att_out[...] = att
    w_out[...] = w
    halves_out(dot_nn(att, w), keep, send)


def mlp_kernel(n_row, n_col, scal, *refs):
    a2s, gs, refs = refs[:n_row], refs[n_row : 2 * n_row], refs[2 * n_row :]
    up_bias, up_own, down_own = refs[:3]
    near, far = refs[3 : 2 + n_col], refs[2 + n_col : 1 + 2 * n_col]
    act_out, d_pre_out, bias_sum, a_keep, a_send, y_keep, y_send, wu, wd = refs[1 + 2 * n_col :]
    rows, width = up_own.shape
    half = width // 2
    wu[:rows, :] = up_own[...]
    wd[:rows, :] = down_own[...]
    for k in range(1, n_col):
        at = slice(k * rows, (k + 1) * rows)
        wu[at, :half] = near[k - 1][:rows, :]
        wd[at, :half] = near[k - 1][rows:, :]
        wu[at, half:] = far[k - 1][:rows, :]
        wd[at, half:] = far[k - 1][rows:, :]
    pre = dot_nn(stacked(a2s), wu[...]) + up_bias[...]
    square = pre * pre
    t = jnp.tanh(C0 * (pre + C1 * (square * pre)))
    act = (0.5 * pre * (1.0 + t)).astype(bf16)
    slope = 0.5 * (1.0 + t) + (0.5 * C0) * pre * (1.0 - t * t) * (1.0 + (3.0 * C1) * square)
    d_act = dot_nn(stacked(gs), wd[...])
    d_pre = (d_act * slope).astype(bf16)
    act_out[...] = act
    d_pre_out[...] = d_pre
    bias_sum[...] = jnp.sum(d_pre.astype(f32), axis=0, keepdims=True)
    halves_out(dot_nt(d_pre, wu[...]), a_keep, a_send)
    halves_out(dot_nt(act, wd[...]), y_keep, y_send)


def mlp_grad_kernel(n_row, scal, *refs):
    a2s, gs, refs = refs[:n_row], refs[n_row : 2 * n_row], refs[2 * n_row :]
    act, d_pre, up_mine, up_other, down_mine, down_other = refs
    half = act.shape[1] // 2
    a2, g = stacked(a2s), stacked(gs)
    up_mine[...] = dot_tn(a2, d_pre[:, :half]).astype(bf16)
    up_other[...] = dot_tn(a2, d_pre[:, half:]).astype(bf16)
    down_mine[...] = dot_tn(g, act[:, :half]).astype(bf16)
    down_other[...] = dot_tn(g, act[:, half:]).astype(bf16)


def d_att_kernel(n_row, n_col, heads, scal, *refs):
    gps, (att, w), refs = refs[:n_row], refs[n_row : n_row + 2], refs[n_row + 2 :]
    outs, grads, cut = refs[:n_col], refs[n_col : 2 * n_col], refs[2 * n_col]
    c = scal[1]
    gp = stacked(gps)
    d_att = dot_nt(gp, w[...]).astype(bf16)
    for h in range(n_col):
        if h < heads:
            cut[h ^ c] = d_att[:, h * HEAD : (h + 1) * HEAD]
        else:
            cut[h ^ c] = jnp.zeros((gp.shape[0], HEAD), bf16)
    for k in range(n_col):
        outs[k][...] = cut[k]
    grad = dot_tn(att[...], gp).astype(bf16)
    w_k = grad.shape[1] // n_col
    for k in range(n_col):
        grads[k][...] = grad[:, k * w_k : (k + 1) * w_k]


def d_a1_kernel(n_row, n_col, heads, scal, *refs):
    ds, xs, refs = refs[:n_col], refs[n_col : n_col + n_row], refs[n_col + n_row :]
    a1, w, keep, send, sums, bias_sum, mine, other, cut, full = refs
    c, d = scal[1], scal[2]
    for k in range(n_col):
        cut[c ^ k] = ds[k][...]
    pieces = [cut[h] for h in range(heads)]
    d_qkv = jnp.concatenate([p[:, j * HEAD : (j + 1) * HEAD] for j in range(3) for p in pieces], axis=1)
    part = dot_nt(d_qkv, w[...])
    halves_out(part, keep, send)
    full[...] = dot_tn(a1[...], d_qkv).astype(bf16)
    rows = full.shape[0] // n_col
    half = rows // 2
    for k in range(n_col):
        at = slice(k * half, (k + 1) * half)
        mine[at, :] = full[pl.ds(pl.multiple_of(k * rows + d * half, 32), half), :]
        other[at, :] = full[pl.ds(pl.multiple_of(k * rows + (1 - d) * half, 32), half), :]
    centred, _ = norm_stats(stacked(xs).astype(f32))
    sums[0:1, :] = jnp.sum(part * centred, axis=0, keepdims=True)
    sums[1:2, :] = jnp.sum(part, axis=0, keepdims=True)
    bias_sum[...] = jnp.sum(d_qkv.astype(f32), axis=0, keepdims=True)


def body(
    block_input,
    ln1_gain,
    ln1_bias,
    qkv_weight,
    qv_bias,
    out_weight,
    out_bias,
    ln2_gain,
    ln2_bias,
    up_weight,
    up_bias,
    down_weight,
    down_bias,
    out_grad,
):
    n_col = lax.axis_size("col")
    n_row = lax.axis_size("row")
    width_in = D // n_col
    width_out = D // n_row
    heads = width_out // HEAD
    order = row_order()
    own = block_input.shape[0] // n_col
    tokens = own * n_row
    c = lax.axis_index("col").astype(jnp.int32)
    d = lax.axis_index("dp").astype(jnp.int32) & 1
    scal = jnp.stack([lax.axis_index("row").astype(jnp.int32), c, d])
    cols = range(1, n_col)

    x_own = turn_in(block_input, c)
    x_all = gather_row(x_own)

    vectors = jnp.stack([ln1_gain, ln1_bias, ln2_gain, ln2_bias, out_bias, down_bias])
    for b in bits_of("col"):
        vectors = jnp.concatenate([vectors, swap(vectors, "col", b)], axis=1)
    gain1, bias1, gain2, bias2, bias_out, bias_down = [vectors[i : i + 1] for i in range(6)]
    w_qkv = qkv_weight.reshape(width_in, 3 * width_out)
    half_qkv = lax.dynamic_slice_in_dim(w_qkv, d * (width_in // 2), width_in // 2, 0)
    near_qkv = [swap(half_qkv, "col", k) for k in cols]
    far_qkv = [swap(v, "dp", 1) for v in near_qkv]
    w_out_own = out_weight.reshape(width_out, width_in)
    w_out = [w_out_own] + [swap(w_out_own, "col", k) for k in cols]
    g_own = turn_in(out_grad, c)
    g_all = gather_row(g_own)

    half_ff = up_weight.shape[1] // 2

    def turned(v):
        return jnp.where(d == 0, v, jnp.concatenate([v[:, half_ff:], v[:, :half_ff]], axis=1))

    up_own, down_own, up_shift = turned(up_weight), turned(down_weight), turned(up_bias[None])
    half_mlp = jnp.concatenate([up_own[:, :half_ff], down_own[:, :half_ff]], axis=0)
    near_mlp = [swap(half_mlp, "col", k) for k in cols]
    far_mlp = [swap(v, "dp", 1) for v in near_mlp]

    shifts = jnp.concatenate([qv_bias[0], jnp.zeros_like(qv_bias[0]), qv_bias[1]])[None]
    res = call(
        functools.partial(qkv_kernel, n_row, n_col, heads),
        [((tokens, 3 * HEAD), bf16)] * n_col + [((tokens, D), bf16), ((D, 3 * width_out), bf16)],
        scal,
        [*x_all, gain1, bias1, shifts, w_qkv, *near_qkv, *far_qkv],
        [((n_col, tokens, 3 * HEAD), bf16)],
    )
    qkv_cut, (a1, w_qkv_all) = res[:n_col], res[n_col:]
    qkv_head = [qkv_cut[0]] + [swap_some(qkv_cut[k], "col", k, n_col, heads) for k in cols]
    att_head = call(
        functools.partial(forward_kernel, order, n_col),
        [((tokens, HEAD), bf16)] * n_col,
        scal,
        qkv_head,
        [((tokens * n_col, 3 * HEAD), bf16), ((tokens * n_col, HEAD), bf16)],
    )
    att_cut = [att_head[0]] + [swap_some(att_head[k], "col", k, heads, n_col) for k in cols]
    attended, w_out_all, o_keep, o_send = call(
        functools.partial(out_kernel, n_col, heads),
        [
            ((tokens, width_out), bf16),
            ((width_out, D), bf16),
            ((tokens // 2, D), f32),
            ((tokens // 2, D), bf16),
        ],
        scal,
        [*att_cut, *w_out],
        [((n_col, tokens, HEAD), bf16)],
    )
    resid1 = x_own.astype(f32) + finish_row(o_keep, o_send) + bias_out
    centred2, inverse2 = norm_stats(resid1)
    a2 = gather_row((centred2 * gain2 + bias2).astype(bf16))

    ff = 2 * half_ff
    act, d_pre, up_sum, a_keep, a_send, y_keep, y_send = call(
        functools.partial(mlp_kernel, n_row, n_col),
        [
            ((tokens, ff), bf16),
            ((tokens, ff), bf16),
            ((1, ff), f32),
            ((tokens // 2, D), f32),
            ((tokens // 2, D), bf16),
            ((tokens // 2, D), f32),
            ((tokens // 2, D), bf16),
        ],
        scal,
        [*a2, *g_all, up_shift, up_own, down_own, *near_mlp, *far_mlp],
        [((D, ff), bf16), ((D, ff), bf16)],
    )
    d_a2 = finish_row(a_keep, a_send)
    d_resid1 = g_own.astype(f32) + norm_back(d_a2, centred2, inverse2, gain2)
    gp = d_resid1.astype(bf16)
    gp_all = gather_row(gp)
    res = call(
        functools.partial(d_att_kernel, n_row, n_col, heads),
        [((tokens, HEAD), bf16)] * n_col + [((width_out, width_in), bf16)] * n_col,
        scal,
        [*gp_all, attended, w_out_all],
        [((n_col, tokens, HEAD), bf16)],
    )
    d_att_cut, d_out_parts = res[:n_col], res[n_col:]
    d_att_head = [d_att_cut[0]] + [swap_some(d_att_cut[k], "col", k, n_col, heads) for k in cols]
    d_qkv_head = call(
        functools.partial(backward_kernel, order, n_col),
        [((tokens, 3 * HEAD), bf16)] * n_col,
        scal,
        [*qkv_head, *d_att_head],
        [
            ((tokens * n_col, 3 * HEAD), bf16),
            ((tokens * n_col, HEAD), bf16),
            ((tokens * n_col, 3 * HEAD), bf16),
            ((HEAD, tokens * n_col), f32),
            ((HEAD, tokens * n_col), f32),
        ],
    )
    d_qkv_cut = [d_qkv_head[0]] + [swap_some(d_qkv_head[k], "col", k, heads, n_col) for k in cols]
    d_keep, d_send, ln1_sums, qkv_sum, qkv_mine, qkv_other = call(
        functools.partial(d_a1_kernel, n_row, n_col, heads),
        [
            ((tokens // 2, D), f32),
            ((tokens // 2, D), bf16),
            ((2, D), f32),
            ((1, 3 * width_out), f32),
            ((D // 2, 3 * width_out), bf16),
            ((D // 2, 3 * width_out), bf16),
        ],
        scal,
        [*d_qkv_cut, *x_all, a1, w_qkv_all],
        [((n_col, tokens, 3 * HEAD), bf16), ((D, 3 * width_out), bf16)],
    )

    block_out = resid1 + finish_row(y_keep, y_send) + bias_down
    block_output = turn_out(block_out.astype(bf16), c)

    def two(part, away, axis):
        low = jnp.where(d == 0, part, away)
        high = jnp.where(d == 0, away, part)
        return jnp.concatenate([low, high], axis=axis).astype(f32)

    up_mine, up_other, down_mine, down_other = call(
        functools.partial(mlp_grad_kernel, n_row),
        [((D, half_ff), bf16)] * 4,
        scal,
        [*a2, *g_all, act, d_pre],
    )
    d_down = two(*sum_halves(down_mine, down_other), 1)
    d_up = two(*sum_halves(up_mine, up_other), 1)
    d_out = sum_dp(sum_cols(d_out_parts).astype(bf16), 1).astype(f32)

    d_a1 = finish_row(d_keep, d_send)
    centred1, inverse1 = norm_stats(x_own.astype(f32))
    input_grad = d_resid1 + norm_back(d_a1, centred1, inverse1, gain1)
    input_grad = turn_out(input_grad.astype(bf16), c)
    d_qkv_w = two(*sum_halves(qkv_mine, qkv_other), 0)

    def add(value, axis, bit):
        return value + swap(value, axis, bit)

    feats = jnp.concatenate(
        [
            ln1_sums,
            jnp.sum(d_a2 * centred2, axis=0, keepdims=True),
            jnp.sum(d_a2, axis=0, keepdims=True),
            jnp.sum(gp.astype(f32), axis=0, keepdims=True),
            jnp.sum(g_own.astype(f32), axis=0, keepdims=True),
        ]
    )
    feats = feats.reshape(6, n_col, width_in)
    for b in bits_of("col"):
        pairs = feats.reshape(6, -1, 2, width_in)
        feats = pairs[:, :, 0] + swap(pairs[:, :, 1], "col", b)
    feats = feats.reshape(6, width_in)
    for b in bits_of("row"):
        feats = add(feats, "row", b)
    for b in bits_of("dp"):
        feats = add(feats, "dp", b)
    hidden = jnp.concatenate([turned(up_sum), qkv_sum], axis=1)
    for b in bits_of("col"):
        hidden = add(hidden, "col", b)
    for b in bits_of("dp"):
        hidden = add(hidden, "dp", b)
    d_up_bias = hidden[0, :ff]
    d_qv_bias = jnp.stack([hidden[0, ff : ff + width_out], hidden[0, ff + 2 * width_out :]])

    return (
        block_output,
        input_grad,
        feats[0],
        feats[1],
        d_qkv_w.reshape(1, 1, -1),
        d_qv_bias,
        d_out.reshape(1, 1, -1),
        feats[4],
        feats[2],
        feats[3],
        d_up,
        d_up_bias,
        d_down,
        feats[5],
    )


def solution(mesh):
    in_specs = (
        P(("dp", "row"), "col"),
        P("col"),
        P("col"),
        P("col", "row", None),
        P(None, "row"),
        P("row", "col", None),
        P("col"),
        P("col"),
        P("col"),
        P("col", "row"),
        P("row"),
        P("col", "row"),
        P("col"),
        P(("dp", "row"), "col"),
    )
    out_specs = (
        P(("dp", "row"), "col"),
        P(("dp", "row"), "col"),
        P("col"),
        P("col"),
        P("col", "row", None),
        P(None, "row"),
        P("row", "col", None),
        P("col"),
        P("col"),
        P("col"),
        P("col", "row"),
        P("row"),
        P("col", "row"),
        P("col"),
    )
    return jax.shard_map(body, mesh=mesh, in_specs=in_specs, out_specs=out_specs, check_vma=False)
```

time: 341 us -> 289 us (0.85)
  blocking collectives: 127 us -> 0 us
  starting transfers between devices: 69.3 us -> 126 us
  local copies, waits for them, and re-layouts: 24.1 us -> 38.3 us
  matrix products: 13.7 us -> 0 us
  between operations: 15.1 us -> 1.59 us
  Pallas kernels: 6.78 us -> 19.4 us
  waiting for transfers between devices: 66.7 us -> 77.8 us
  other arithmetic: 16.3 us -> 23.7 us
    ppermute x24 -> x76, starting transfers between devices: 17.4 us -> 95.9 us  [swap(): return lax.ppermute(value, axis, [(i, i ^ bit) for i in range(n)])]
    all_gather x3 -> x0, blocking collectives: 65.9 us -> none  [the longest x1 36.7 us: body(): lax.all_gather(qkv_weight.reshape(width_in, 3 * width_out), 'col', axis=0...]
    psum x2 -> x0, blocking collectives: 61.5 us -> none  [the longest x1 39.5 us: body(): lax.psum(jnp.stack([column_sums(d_a1_part * centred1), column_sums(d_a1_p...]
    ppermute x24 -> x76, waiting for transfers between devices: 22.1 us -> 65.9 us  [swap(): return lax.ppermute(value, axis, [(i, i ^ bit) for i in range(n)])]
    all_to_all x8 -> x0, starting transfers between devices: 34.5 us -> none  [turn_cols(): return lax.all_to_all(value, 'col', split, concat, tiled=True)]
    all_to_all x8 -> x0, waiting for transfers between devices: 28 us -> none  [turn_cols(): return lax.all_to_all(value, 'col', split, concat, tiled=True)]
    unnamed x85 -> x146, local copies, waits for them, and re-layouts: 7.61 us -> 27.9 us
    dot_general x12 -> x0, matrix products: 13.7 us -> none  [the longest x4 5.89 us: dot_nn(): lax.dot_general(a, b, (((1,), (0,)), ((), ())), preferred_element_type=f32)]
  transfers between devices with their start and end apart: 46 -> 88, of which waited for: 18 -> 31; matrix products, arithmetic and copies ran while one was open for 13% -> 13% of each run, Pallas kernels for 2% -> 5%
where the time goes in v2:
time: 289 us; the launch traced here: 287 us
  starting transfers between devices  126 us (44%)
  waiting for transfers between devices  77.8 us (27%)
  local copies, waits for them, and re-layouts  38.3 us (13%)
  other arithmetic  23.7 us (8%)
  Pallas kernels  19.4 us (7%)
    ppermute x76, starting transfers between devices, swap(): return lax.ppermute(value, axis, [(i, i ^ bit) for i in range(n)])  95.9 us
    ppermute x76, waiting for transfers between devices, swap(): return lax.ppermute(value, axis, [(i, i ^ bit) for i in range(n)])  65.9 us
    ppermute x12, starting transfers between devices, swap_some(): lax.ppermute(value, axis, [(i, i ^ bit) for i in range(n) if i < sources...  30.3 us
    unnamed x146, local copies, waits for them, and re-layouts  27.9 us
    pallas_call x8, Pallas kernels, call(): pl.pallas_call(kernel, out_shape=[jax.ShapeDtypeStruct(s, t) for s, t in...  19.4 us
    ppermute x12, waiting for transfers between devices, swap_some(): lax.ppermute(value, axis, [(i, i ^ bit) for i in range(n) if i < sources...  12 us
  transfers between devices with their start and end apart: 88, of which 31 were waited for; matrix products, arithmetic and copies ran while one was open for 13% of the time, Pallas kernels for 5%

profile of v2, /device:TPU:0, one launch (start us, length us, event | category | flops | bytes accessed | tf_op | source)
XLA Modules:
  0.0 287.0 jit_solution(182496489414112724)
XLA Ops:
  3.2 3.1 %collective-permute-start.8 = (bf16[96,576]{1,0:T(8,128)(2,1)S(1)}, bf16[96,576]{1,0:T(8,128)(2,1)S(1)}, u32[]{:S(2)}, u32[]{:S(2)}) collective-permute-start(bf16[96,576]{1,0:T(8,128)(2,1)S(1)} %constant_dynamic-slice_fusion.4), channel_id=1, source_target_pairs={{0,1},{1,0},{2,3},{3,2},{4,5},{5,4},{6,7},{7,6},{8,9},{9,8},{10,11... | collective-permute-start | bytes 331784 | tf_op jit(solution)/shard_map/ppermute | solution.py:47
  15.3 3.6 %collective-permute-start.2 = (bf16[64,192]{1,0:T(8,128)(2,1)S(1)}, bf16[64,192]{1,0:T(8,128)(2,1)S(1)}, u32[]{:S(2)}, u32[]{:S(2)}) collective-permute-start(bf16[64,192]{1,0:T(8,128)(2,1)S(1)} %copy.45), channel_id=1, source_target_pairs={{0,3},{1,2},{2,1},{3,0},{4,7},{5,6},{6,5},{7,4},{8,11},{9,10},{10,... | collective-permute-start | bytes 73736 | tf_op jit(solution)/shard_map/ppermute | solution.py:47
  37.1 4.1 %collective-permute-start.14 = (bf16[256,192]{1,0:T(8,128)(2,1)S(1)}, bf16[256,192]{1,0:T(8,128)(2,1)S(1)}, u32[]{:S(2)}, u32[]{:S(2)}) collective-permute-start(bf16[256,192]{1,0:T(8,128)(2,1)S(1)} %get-tuple-element.58), channel_id=1, source_target_pairs={{0,1},{1,0},{3,2},{4,5},{5,4},{7,6},{8,9},{9,8},{11,10},{12,13},{1... | collective-permute-start | bytes 294920 | tf_op jit(solution)/shard_map/ppermute | solution.py:52
  45.2 4.4 %collective-permute-start.22 = (bf16[192,192]{1,0:T(8,128)(2,1)S(1)}, bf16[192,192]{1,0:T(8,128)(2,1)S(1)}, u32[]{:S(2)}, u32[]{:S(2)}) collective-permute-start(bf16[192,192]{1,0:T(8,128)(2,1)S(1)} %reshape.124.refs_4_), channel_id=1, source_target_pairs={{0,3},{1,2},{2,1},{3,0},{4,7},{5,6},{6,5},{7,4},{8,11},{9,10},{10,... | collective-permute-start | bytes 221192 | tf_op jit(solution)/shard_map/ppermute | solution.py:47
  49.7 6.7 %collective-permute-done.15.refs_2_ = bf16[256,192]{1,0:T(8,128)(2,1)S(1)} collective-permute-done((bf16[256,192]{1,0:T(8,128)(2,1)S(1)}, bf16[256,192]{1,0:T(8,128)(2,1)S(1)}, u32[]{:S(2)}, u32[]{:S(2)}) %collective-permute-start.15) | collective-permute-done | bytes 98336 | tf_op jit(solution)/shard_map/ppermute | solution.py:52
  59.3 5.3 %collective-permute-start.17 = (bf16[256,64]{1,0:T(8,128)(2,1)S(1)}, bf16[256,64]{1,0:T(8,128)(2,1)S(1)}, u32[]{:S(2)}, u32[]{:S(2)}) collective-permute-start(bf16[256,64]{1,0:T(8,128)(2,1)S(1)} %get-tuple-element.62), channel_id=1, source_target_pairs={{0,1},{1,0},{2,3},{4,5},{5,4},{6,7},{8,9},{9,8},{10,11},{12,13},{1... | collective-permute-start | bytes 98312 | tf_op jit(solution)/shard_map/ppermute | solution.py:52
  72.2 4.2 %collective-permute-start.28 = (bf16[64,192]{1,0:T(8,128)(2,1)}, bf16[64,192]{1,0:T(8,128)(2,1)}, u32[]{:S(2)}, u32[]{:S(2)}) collective-permute-start(bf16[64,192]{1,0:T(8,128)(2,1)} %copy.47), channel_id=1, source_target_pairs={{0,1},{1,0},{2,3},{3,2},{4,5},{5,4},{6,7},{7,6},{8,9},{9,8},{10,11... | collective-permute-start | bytes 73736 | tf_op jit(solution)/shard_map/ppermute | solution.py:47
  100.8 11.9 %collective-permute-done.35.refs_12_ = bf16[384,384]{1,0:T(8,128)(2,1)} collective-permute-done((bf16[384,384]{1,0:T(8,128)(2,1)}, bf16[384,384]{1,0:T(8,128)(2,1)}, u32[]{:S(2)}, u32[]{:S(2)}) %collective-permute-start.35) | collective-permute-done | bytes 294944 | tf_op jit(solution)/shard_map/ppermute | solution.py:47
  118.9 2.9 %collective-permute-done.25.refs_1_ = bf16[64,768]{1,0:T(8,128)(2,1)S(1)} collective-permute-done((bf16[64,768]{1,0:T(8,128)(2,1)S(1)}, bf16[64,768]{1,0:T(8,128)(2,1)S(1)}, u32[]{:S(2)}, u32[]{:S(2)}) %collective-permute-start.25) | collective-permute-done | bytes 98336 | tf_op jit(solution)/shard_map/ppermute | solution.py:47
  123.8 5.5 %collective-permute-done.38.refs_15_ = bf16[384,384]{1,0:T(8,128)(2,1)} collective-permute-done((bf16[384,384]{1,0:T(8,128)(2,1)}, bf16[384,384]{1,0:T(8,128)(2,1)}, u32[]{:S(2)}, u32[]{:S(2)}) %collective-permute-start.38) | collective-permute-done | bytes 294944 | tf_op jit(solution)/shard_map/ppermute | solution.py:47
  129.3 3.8 %collective-permute-done.39.refs_16_ = bf16[384,384]{1,0:T(8,128)(2,1)} collective-permute-done((bf16[384,384]{1,0:T(8,128)(2,1)}, bf16[384,384]{1,0:T(8,128)(2,1)}, u32[]{:S(2)}, u32[]{:S(2)}) %collective-permute-start.39) | collective-permute-done | bytes 294944 | tf_op jit(solution)/shard_map/ppermute | solution.py:47
  133.2 3.1 %shard_map.248 = (bf16[256,768]{1,0:T(8,128)(2,1)S(1)}, bf16[256,768]{1,0:T(8,128)(2,1)S(1)}, f32[1,768]{1,0:T(1,128)S(1)}, f32[128,768]{1,0:T(8,128)S(1)}, bf16...) custom-call(s32[3]{0:T(128)S(1)} %pad_add_fusion.scal, ...), custom_call_target="tpu_custom_call" | custom-call | tf_op jit(solution)/shard_map/pallas_call | solution.py:35
  147.7 3.5 %collective-permute-done.46 = bf16[64,768]{1,0:T(8,128)(2,1)S(1)} collective-permute-done((bf16[64,768]{1,0:T(8,128)(2,1)S(1)}, bf16[64,768]{1,0:T(8,128)(2,1)S(1)}, u32[]{:S(2)}, u32[]{:S(2)}) %collective-permute-start.46) | collective-permute-done | bytes 98336 | tf_op jit(solution)/shard_map/ppermute | solution.py:47
  175.3 3.5 %collective-permute-start.75 = (bf16[192,192]{1,0:T(8,128)(2,1)}, bf16[192,192]{1,0:T(8,128)(2,1)}, u32[]{:S(2)}, u32[]{:S(2)}) collective-permute-start(bf16[192,192]{1,0:T(8,128)(2,1)} %get-tuple-element.92), channel_id=1, source_target_pairs={{0,2},{1,3},{2,0},{3,1},{4,6},{5,7},{6,4},{7,5},{8,10},{9,11},{10,... | collective-permute-start | bytes 221192 | tf_op jit(solution)/shard_map/ppermute | solution.py:47
  183.2 4.5 %collective-permute-done.52.refs_7_ = bf16[256,64]{1,0:T(8,128)(2,1)S(1)} collective-permute-done((bf16[256,64]{1,0:T(8,128)(2,1)}, bf16[256,64]{1,0:T(8,128)(2,1)S(1)}, u32[]{:S(2)}, u32[]{:S(2)}) %collective-permute-start.52) | collective-permute-done | bytes 32800 | tf_op jit(solution)/shard_map/ppermute | solution.py:52
  188.4 5.0 %shard_map.250 = (bf16[256,192]{1,0:T(8,128)(2,1)S(1)}, bf16[256,192]{1,0:T(8,128)(2,1)S(1)}, bf16[256,192]{1,0:T(8,128)(2,1)S(1)}, bf16[256,192]{1,0:T(8,128)(2,1)S(1)}) custom-call(s32[3]{0:T(128)S(1)} %pad_add_fusion.scal, bf16[256,192]{1,0:T(8,128)(2,1)S(1)} %get-tuple-element.57.refs_0_, bf16[256,192]{1,0:T(8,128)(2,1)S(1)} %collective-permute-done.14.refs_1_, ...), custom_call_target="tpu_custom_call" | custom-call | tf_op jit(solution)/shard_map/pallas_call | solution.py:35
  193.4 5.7 %collective-permute-start.53 = (bf16[256,192]{1,0:T(8,128)(2,1)S(1)}, bf16[256,192]{1,0:T(8,128)(2,1)S(1)}, u32[]{:S(2)}, u32[]{:S(2)}) collective-permute-start(bf16[256,192]{1,0:T(8,128)(2,1)S(1)} %get-tuple-element.78), channel_id=1, source_target_pairs={{0,1},{1,0},{2,3},{4,5},{5,4},{6,7},{8,9},{9,8},{10,11},{12,13},{1... | collective-permute-start | bytes 294920 | tf_op jit(solution)/shard_map/ppermute | solution.py:52
  207.0 4.1 %collective-permute-start.84 = (bf16[192,384]{1,0:T(8,128)(2,1)}, bf16[192,384]{1,0:T(8,128)(2,1)}, u32[]{:S(2)}, u32[]{:S(2)}) collective-permute-start(bf16[192,384]{1,0:T(8,128)(2,1)} %get-tuple-element.139), channel_id=1, source_target_pairs={{0,1},{1,0},{2,3},{3,2},{4,5},{5,4},{6,7},{7,6},{8,9},{9,8},{10,11... | collective-permute-start | bytes 442376 | tf_op jit(solution)/shard_map/ppermute | solution.py:47
  244.2 3.0 %collective-permute-start.81 = (bf16[192,384]{1,0:T(8,128)(2,1)}, bf16[192,384]{1,0:T(8,128)(2,1)S(1)}, u32[]{:S(2)}, u32[]{:S(2)}) collective-permute-start(bf16[192,384]{1,0:T(8,128)(2,1)} %get-tuple-element.143), channel_id=1, source_target_pairs={{0,3},{1,2},{2,1},{3,0},{4,7},{5,6},{6,5},{7,4},{8,11},{9,10},{10,... | collective-permute-start | bytes 442376 | tf_op jit(solution)/shard_map/ppermute | solution.py:47
  250.4 4.2 %collective-permute-done.80 = bf16[192,384]{1,0:T(8,128)(2,1)S(1)} collective-permute-done((bf16[192,384]{1,0:T(8,128)(2,1)}, bf16[192,384]{1,0:T(8,128)(2,1)S(1)}, u32[]{:S(2)}, u32[]{:S(2)}) %collective-permute-start.80) | collective-permute-done | bytes 147488 | tf_op jit(solution)/shard_map/ppermute | solution.py:47
  258.2 4.0 %collective-permute-done.87 = bf16[192,384]{1,0:T(8,128)(2,1)S(1)} collective-permute-done((bf16[192,384]{1,0:T(8,128)(2,1)S(1)}, bf16[192,384]{1,0:T(8,128)(2,1)S(1)}, u32[]{:S(2)}, u32[]{:S(2)}) %collective-permute-start.87) | collective-permute-done | bytes 147488 | tf_op jit(solution)/shard_map/ppermute | solution.py:47
  267.6 3.4 %collective-permute-start.60 = (bf16[64,192]{1,0:T(8,128)(2,1)S(1)}, bf16[64,192]{1,0:T(8,128)(2,1)S(1)}, u32[]{:S(2)}, u32[]{:S(2)}) collective-permute-start(bf16[64,192]{1,0:T(8,128)(2,1)S(1)} %get-tuple-element.167), channel_id=1, source_target_pairs={{0,1},{1,0},{2,3},{3,2},{4,5},{5,4},{6,7},{7,6},{8,9},{9,8},{10,11... | collective-permute-start | bytes 73736 | tf_op jit(solution)/shard_map/ppermute | solution.py:47
  277.3 3.2 %collective-permute-done.68 = bf16[96,576]{1,0:T(8,128)(2,1)S(1)} collective-permute-done((bf16[96,576]{1,0:T(8,128)(2,1)S(1)}, bf16[96,576]{1,0:T(8,128)(2,1)S(1)}, u32[]{:S(2)}, u32[]{:S(2)}) %collective-permute-start.68) | collective-permute-done | bytes 110624 | tf_op jit(solution)/shard_map/ppermute | solution.py:47
  282.5 3.1 %collective-permute-done.70 = bf16[96,576]{1,0:T(8,128)(2,1)S(1)} collective-permute-done((bf16[96,576]{1,0:T(8,128)(2,1)S(1)}, bf16[96,576]{1,0:T(8,128)(2,1)S(1)}, u32[]{:S(2)}, u32[]{:S(2)}) %collective-permute-start.70) | collective-permute-done | bytes 110624 | tf_op jit(solution)/shard_map/ppermute | solution.py:47
  (397 shorter events, 179.6 us)
Async XLA Ops:
  3.2 20.9 %collective-permute-start.8 = (bf16[96,576]{1,0:T(8,128)(2,1)S(1)}, bf16[96,576]{1,0:T(8,128)(2,1)S(1)}, u32[]{:S(2)}, u32[]{:S(2)}) collective-permute-start(bf16[96,576]{1,0:T(8,128)(2,1)S(1)} %constant_dynamic-slice_fusion.4), channel_id=1, source_target_pairs={{0,1},{1,0},{2,3},{3,2},{4,5},{5,4},{6,7},{7,6},{8,9},{9,8},{10,11... | collective-permute-start | bytes 331784 | tf_op jit(solution)/shard_map/ppermute | solution.py:47
  6.3 19.4 %collective-permute-start.9 = (bf16[96,576]{1,0:T(8,128)(2,1)S(1)}, bf16[96,576]{1,0:T(8,128)(2,1)S(1)}, u32[]{:S(2)}, u32[]{:S(2)}) collective-permute-start(bf16[96,576]{1,0:T(8,128)(2,1)S(1)} %constant_dynamic-slice_fusion.4), channel_id=1, source_target_pairs={{0,2},{1,3},{2,0},{3,1},{4,6},{5,7},{6,4},{7,5},{8,10},{9,11},{10,... | collective-permute-start | bytes 331784 | tf_op jit(solution)/shard_map/ppermute | solution.py:47
  28.3 38.1 %collective-permute-start.20 = (bf16[192,192]{1,0:T(8,128)(2,1)S(1)}, bf16[192,192]{1,0:T(8,128)(2,1)S(1)}, u32[]{:S(2)}, u32[]{:S(2)}) collective-permute-start(bf16[192,192]{1,0:T(8,128)(2,1)S(1)} %reshape.124.refs_4_), channel_id=1, source_target_pairs={{0,1},{1,0},{2,3},{3,2},{4,5},{5,4},{6,7},{7,6},{8,9},{9,8},{10,11... | collective-permute-start | bytes 221192 | tf_op jit(solution)/shard_map/ppermute | solution.py:47
  30.6 41.7 %collective-permute-start.21 = (bf16[192,192]{1,0:T(8,128)(2,1)S(1)}, bf16[192,192]{1,0:T(8,128)(2,1)S(1)}, u32[]{:S(2)}, u32[]{:S(2)}) collective-permute-start(bf16[192,192]{1,0:T(8,128)(2,1)S(1)} %reshape.124.refs_4_), channel_id=1, source_target_pairs={{0,2},{1,3},{2,0},{3,1},{4,6},{5,7},{6,4},{7,5},{8,10},{9,11},{10,... | collective-permute-start | bytes 221192 | tf_op jit(solution)/shard_map/ppermute | solution.py:47
  45.2 31.2 %collective-permute-start.22 = (bf16[192,192]{1,0:T(8,128)(2,1)S(1)}, bf16[192,192]{1,0:T(8,128)(2,1)S(1)}, u32[]{:S(2)}, u32[]{:S(2)}) collective-permute-start(bf16[192,192]{1,0:T(8,128)(2,1)S(1)} %reshape.124.refs_4_), channel_id=1, source_target_pairs={{0,3},{1,2},{2,1},{3,0},{4,7},{5,6},{6,5},{7,4},{8,11},{9,10},{10,... | collective-permute-start | bytes 221192 | tf_op jit(solution)/shard_map/ppermute | solution.py:47
  59.3 17.8 %collective-permute-start.17 = (bf16[256,64]{1,0:T(8,128)(2,1)S(1)}, bf16[256,64]{1,0:T(8,128)(2,1)S(1)}, u32[]{:S(2)}, u32[]{:S(2)}) collective-permute-start(bf16[256,64]{1,0:T(8,128)(2,1)S(1)} %get-tuple-element.62), channel_id=1, source_target_pairs={{0,1},{1,0},{2,3},{4,5},{5,4},{6,7},{8,9},{9,8},{10,11},{12,13},{1... | collective-permute-start | bytes 98312 | tf_op jit(solution)/shard_map/ppermute | solution.py:52
  72.2 16.7 %collective-permute-start.28 = (bf16[64,192]{1,0:T(8,128)(2,1)}, bf16[64,192]{1,0:T(8,128)(2,1)}, u32[]{:S(2)}, u32[]{:S(2)}) collective-permute-start(bf16[64,192]{1,0:T(8,128)(2,1)} %copy.47), channel_id=1, source_target_pairs={{0,1},{1,0},{2,3},{3,2},{4,5},{5,4},{6,7},{7,6},{8,9},{9,8},{10,11... | collective-permute-start | bytes 73736 | tf_op jit(solution)/shard_map/ppermute | solution.py:47
  89.0 23.8 %collective-permute-start.35 = (bf16[384,384]{1,0:T(8,128)(2,1)}, bf16[384,384]{1,0:T(8,128)(2,1)}, u32[]{:S(2)}, u32[]{:S(2)}) collective-permute-start(bf16[384,384]{1,0:T(8,128)(2,1)} %pad_maximum_fusion), channel_id=1, source_target_pairs={{0,2},{1,3},{2,0},{3,1},{4,6},{5,7},{6,4},{7,5},{8,10},{9,11},{10,... | collective-permute-start | bytes 884744 | tf_op jit(solution)/shard_map/ppermute | solution.py:47
  89.9 24.2 %collective-permute-start.36 = (bf16[384,384]{1,0:T(8,128)(2,1)}, bf16[384,384]{1,0:T(8,128)(2,1)}, u32[]{:S(2)}, u32[]{:S(2)}) collective-permute-start(bf16[384,384]{1,0:T(8,128)(2,1)} %pad_maximum_fusion), channel_id=1, source_target_pairs={{0,3},{1,2},{2,1},{3,0},{4,7},{5,6},{6,5},{7,4},{8,11},{9,10},{10,... | collective-permute-start | bytes 884744 | tf_op jit(solution)/shard_map/ppermute | solution.py:47
  95.8 19.0 %collective-permute-start.24 = (bf16[64,768]{1,0:T(8,128)(2,1)S(1)}, bf16[64,768]{1,0:T(8,128)(2,1)S(1)}, u32[]{:S(2)}, u32[]{:S(2)}) collective-permute-start(bf16[64,768]{1,0:T(8,128)(2,1)S(1)} %slice.421), channel_id=1, source_target_pairs={{0,8},{4,12},{8,0},{12,4},{1,9},{5,13},{9,1},{13,5},{2,10},{6,14},... | collective-permute-start | bytes 294920 | tf_op jit(solution)/shard_map/ppermute | solution.py:47
  97.9 19.2 %collective-permute-start.32 = (bf16[64,768]{1,0:T(8,128)(2,1)S(1)}, bf16[64,768]{1,0:T(8,128)(2,1)S(1)}, u32[]{:S(2)}, u32[]{:S(2)}) collective-permute-start(bf16[64,768]{1,0:T(8,128)(2,1)S(1)} %get-tuple-element.131.refs_4_), channel_id=1, source_target_pairs={{0,4},{4,0},{8,12},{12,8},{1,5},{5,1},{9,13},{13,9},{2,6},{6,2},{1... | collective-permute-start | bytes 294920 | tf_op jit(solution)/shard_map/ppermute | solution.py:47
  100.8 18.0 %collective-permute-start.33 = (bf16[64,768]{1,0:T(8,128)(2,1)S(1)}, bf16[64,768]{1,0:T(8,128)(2,1)S(1)}, u32[]{:S(2)}, u32[]{:S(2)}) collective-permute-start(bf16[64,768]{1,0:T(8,128)(2,1)S(1)} %collective-permute-done.31.refs_5_), channel_id=1, source_target_pairs={{0,4},{4,0},{8,12},{12,8},{1,5},{5,1},{9,13},{13,9},{2,6},{6,2},{1... | collective-permute-start | bytes 294920 | tf_op jit(solution)/shard_map/ppermute | solution.py:47
  114.8 18.4 %collective-permute-start.39 = (bf16[384,384]{1,0:T(8,128)(2,1)}, bf16[384,384]{1,0:T(8,128)(2,1)}, u32[]{:S(2)}, u32[]{:S(2)}) collective-permute-start(bf16[384,384]{1,0:T(8,128)(2,1)} %collective-permute-done.36.refs_13_), channel_id=1, source_target_pairs={{0,16},{16,0},{1,17},{17,1},{2,18},{18,2},{3,19},{19,3},{4,20},{20... | collective-permute-start | bytes 884744 | tf_op jit(solution)/shard_map/ppermute | solution.py:47
  142.3 61.3 %collective-permute-start.83 = (bf16[768,384]{1,0:T(8,128)(2,1)}, bf16[768,384]{1,0:T(8,128)(2,1)}, u32[]{:S(2)}, u32[]{:S(2)}) collective-permute-start(bf16[768,384]{1,0:T(8,128)(2,1)} %get-tuple-element.99), channel_id=1, source_target_pairs={{0,16},{16,0},{1,17},{17,1},{2,18},{18,2},{3,19},{19,3},{4,20},{20... | collective-permute-start | bytes 1769480 | tf_op jit(solution)/shard_map/ppermute | solution.py:47
  156.2 16.8 %collective-permute-start.43 = (bf16[64,192]{1,0:T(8,128)(2,1)}, bf16[64,192]{1,0:T(8,128)(2,1)}, u32[]{:S(2)}, u32[]{:S(2)}) collective-permute-start(bf16[64,192]{1,0:T(8,128)(2,1)} %get-tuple-element.171), channel_id=1, source_target_pairs={{0,2},{1,3},{2,0},{3,1},{4,6},{5,7},{6,4},{7,5},{8,10},{9,11},{10,... | collective-permute-start | bytes 73736 | tf_op jit(solution)/shard_map/ppermute | solution.py:47
  173.8 19.5 %collective-permute-start.74 = (bf16[192,192]{1,0:T(8,128)(2,1)}, bf16[192,192]{1,0:T(8,128)(2,1)}, u32[]{:S(2)}, u32[]{:S(2)}) collective-permute-start(bf16[192,192]{1,0:T(8,128)(2,1)} %get-tuple-element.91), channel_id=1, source_target_pairs={{0,1},{1,0},{2,3},{3,2},{4,5},{5,4},{6,7},{7,6},{8,9},{9,8},{10,11... | collective-permute-start | bytes 221192 | tf_op jit(solution)/shard_map/ppermute | solution.py:47
  175.3 23.8 %collective-permute-start.75 = (bf16[192,192]{1,0:T(8,128)(2,1)}, bf16[192,192]{1,0:T(8,128)(2,1)}, u32[]{:S(2)}, u32[]{:S(2)}) collective-permute-start(bf16[192,192]{1,0:T(8,128)(2,1)} %get-tuple-element.92), channel_id=1, source_target_pairs={{0,2},{1,3},{2,0},{3,1},{4,6},{5,7},{6,4},{7,5},{8,10},{9,11},{10,... | collective-permute-start | bytes 221192 | tf_op jit(solution)/shard_map/ppermute | solution.py:47
  178.8 22.2 %collective-permute-start.76 = (bf16[192,192]{1,0:T(8,128)(2,1)}, bf16[192,192]{1,0:T(8,128)(2,1)}, u32[]{:S(2)}, u32[]{:S(2)}) collective-permute-start(bf16[192,192]{1,0:T(8,128)(2,1)} %get-tuple-element.93), channel_id=1, source_target_pairs={{0,3},{1,2},{2,1},{3,0},{4,7},{5,6},{6,5},{7,4},{8,11},{9,10},{10,... | collective-permute-start | bytes 221192 | tf_op jit(solution)/shard_map/ppermute | solution.py:47
  187.7 36.7 %collective-permute-start.78 = (bf16[768,384]{1,0:T(8,128)(2,1)}, bf16[768,384]{1,0:T(8,128)(2,1)}, u32[]{:S(2)}, u32[]{:S(2)}) collective-permute-start(bf16[768,384]{1,0:T(8,128)(2,1)} %copy-done.30), channel_id=1, source_target_pairs={{0,16},{16,0},{1,17},{17,1},{2,18},{18,2},{3,19},{19,3},{4,20},{20... | collective-permute-start | bytes 1769480 | tf_op jit(solution)/shard_map/ppermute | solution.py:47
  203.6 34.9 %collective-permute-start.77 = (bf16[192,192]{1,0:T(8,128)(2,1)S(1)}, bf16[192,192]{1,0:T(8,128)(2,1)}, u32[]{:S(2)}, u32[]{:S(2)}) collective-permute-start(bf16[192,192]{1,0:T(8,128)(2,1)S(1)} %add_convert_fusion.16), channel_id=1, source_target_pairs={{0,16},{16,0},{1,17},{17,1},{2,18},{18,2},{3,19},{19,3},{4,20},{20... | collective-permute-start | bytes 221192 | tf_op jit(solution)/shard_map/ppermute | solution.py:47
  207.0 37.2 %collective-permute-start.84 = (bf16[192,384]{1,0:T(8,128)(2,1)}, bf16[192,384]{1,0:T(8,128)(2,1)}, u32[]{:S(2)}, u32[]{:S(2)}) collective-permute-start(bf16[192,384]{1,0:T(8,128)(2,1)} %get-tuple-element.139), channel_id=1, source_target_pairs={{0,1},{1,0},{2,3},{3,2},{4,5},{5,4},{6,7},{7,6},{8,9},{9,8},{10,11... | collective-permute-start | bytes 442376 | tf_op jit(solution)/shard_map/ppermute | solution.py:47
  211.1 36.1 %collective-permute-start.85 = (bf16[192,384]{1,0:T(8,128)(2,1)}, bf16[192,384]{1,0:T(8,128)(2,1)}, u32[]{:S(2)}, u32[]{:S(2)}) collective-permute-start(bf16[192,384]{1,0:T(8,128)(2,1)} %get-tuple-element.141), channel_id=1, source_target_pairs={{0,2},{1,3},{2,0},{3,1},{4,6},{5,7},{6,4},{7,5},{8,10},{9,11},{10,... | collective-permute-start | bytes 442376 | tf_op jit(solution)/shard_map/ppermute | solution.py:47
  226.9 21.4 %collective-permute-start.86 = (bf16[192,384]{1,0:T(8,128)(2,1)S(1)}, bf16[192,384]{1,0:T(8,128)(2,1)S(1)}, u32[]{:S(2)}, u32[]{:S(2)}) collective-permute-start(bf16[192,384]{1,0:T(8,128)(2,1)S(1)} %copy-done.46), channel_id=1, source_target_pairs={{0,3},{1,2},{2,1},{3,0},{4,7},{5,6},{6,5},{7,4},{8,11},{9,10},{10,... | collective-permute-start | bytes 442376 | tf_op jit(solution)/shard_map/ppermute | solution.py:47
  247.2 23.8 %collective-permute-start.66 = (bf16[384,576]{1,0:T(8,128)(2,1)S(1)}, bf16[384,576]{1,0:T(8,128)(2,1)S(1)}, u32[]{:S(2)}, u32[]{:S(2)}) collective-permute-start(bf16[384,576]{1,0:T(8,128)(2,1)S(1)} %copy-done.32), channel_id=1, source_target_pairs={{0,16},{16,0},{1,17},{17,1},{2,18},{18,2},{3,19},{19,3},{4,20},{20... | collective-permute-start | bytes 1327112 | tf_op jit(solution)/shard_map/ppermute | solution.py:47
  (129 other events, 766.0 us)

commit v3 on v1

v3 whole, which is shorter than its diff:
```python
import functools
import math

import jax
import jax.numpy as jnp
from jax import lax
from jax.experimental import pallas as pl
from jax.experimental.pallas import tpu as pltpu
from jax.sharding import PartitionSpec as P

D = 768
HEAD = 64
SCALE = 1.0 / math.sqrt(HEAD)
C0 = math.sqrt(2.0 / math.pi)
C1 = 0.044715
bf16 = jnp.bfloat16
f32 = jnp.float32
VMEM = pl.BlockSpec(memory_space=pltpu.VMEM)
SMEM = pl.BlockSpec(memory_space=pltpu.SMEM)


def dot_nn(a, b):
    return lax.dot_general(a, b, (((1,), (0,)), ((), ())), preferred_element_type=f32)


def dot_nt(a, b):
    return lax.dot_general(a, b, (((1,), (1,)), ((), ())), preferred_element_type=f32)


def dot_tn(a, b):
    return lax.dot_general(a, b, (((0,), (0,)), ((), ())), preferred_element_type=f32)


def call(kernel, outs, scalars, args, scratch=()):
    first = [] if scalars is None else [scalars]
    return pl.pallas_call(
        kernel,
        out_shape=[jax.ShapeDtypeStruct(s, t) for s, t in outs],
        in_specs=[SMEM] * len(first) + [VMEM] * len(args),
        out_specs=[VMEM] * len(outs),
        scratch_shapes=[pltpu.VMEM(s, t) for s, t in scratch],
        compiler_params=pltpu.CompilerParams(vmem_limit_bytes=20 * 1024 * 1024),
    )(*first, *args)


def swap(value, axis, bit):
    n = lax.axis_size(axis)
    return lax.ppermute(value, axis, [(i, i ^ bit) for i in range(n)])


def turn(value, split=0, concat=0):
    return lax.all_to_all(value, "col", split, concat, tiled=True)


def bits_of(axis, first=1):
    n = lax.axis_size(axis)
    bits = []
    b = first
    while b < n:
        bits.append(b)
        b *= 2
    return bits


def row_order():
    order = [0]
    for b in reversed(bits_of("row")):
        order = order + [o ^ b for o in order]
    return order


def gather_row(value):
    pieces = [value]
    for b in reversed(bits_of("row")):
        pieces = pieces + [swap(p, "row", b) for p in pieces]
    return pieces


def finish_row(keep, send):
    bits = bits_of("row")
    for b in bits[:-1]:
        keep, send = add_halves(keep, swap(send, "row", b))
    return keep, swap(send, "row", bits[-1])


def add_halves(keep, got):
    rows, width = keep.shape
    return call(halves_kernel, [((rows // 2, width), f32), ((rows // 2, width), bf16)], None, [keep, got])


def three_parts(v):
    high = lax.optimization_barrier(v.astype(bf16))
    rest = v - high.astype(f32)
    middle = lax.optimization_barrier(rest.astype(bf16))
    low = (rest - middle.astype(f32)).astype(bf16)
    return jnp.concatenate([high, middle, low], axis=0)


def place(scal, order, col, kk, chunk, n_col, second):
    half = chunk // 2
    at = ((scal[0] ^ order[kk]) * n_col + col) * chunk + second * half
    return pl.ds(pl.multiple_of(at, half), half)


def load_natural(scal, order, src, dst):
    n_col, rows, width = src.shape
    half = rows // len(order)
    for col in range(n_col):
        for kk in range(len(order)):
            both = src[col, kk * half : (kk + 1) * half, :]
            for second in range(2):
                at = place(scal, order, col, kk, 2 * half, n_col, second)
                dst[at, :] = both[:, second * (width // 2) : (second + 1) * (width // 2)]


def store_natural(scal, order, src, dst):
    n_col, rows, _ = dst.shape
    half = rows // len(order)
    for col in range(n_col):
        for kk in range(len(order)):
            both = [src[place(scal, order, col, kk, 2 * half, n_col, second), :] for second in range(2)]
            dst[col, kk * half : (kk + 1) * half, :] = jnp.concatenate(both, axis=1)


def beside(value, chunk):
    half = chunk // 2
    starts = range(0, value.shape[0], chunk)
    first = jnp.concatenate([value[i : i + half] for i in starts], axis=0)
    second = jnp.concatenate([value[i + half : i + chunk] for i in starts], axis=0)
    return jnp.concatenate([first, second], axis=1)


def under(value, chunk):
    half = chunk // 2
    width = value.shape[1] // 2
    parts = []
    for i in range(0, value.shape[0], half):
        parts += [value[i : i + half, :width], value[i : i + half, width:]]
    return jnp.concatenate(parts, axis=0)


def block_probs(q, k, block, i):
    scores = dot_nt(q, k) * SCALE
    rows = lax.broadcasted_iota(jnp.int32, scores.shape, 0) + i * block
    cols = lax.broadcasted_iota(jnp.int32, scores.shape, 1)
    scores = jnp.where(cols <= rows, scores, -1e30)
    top = jnp.max(scores, axis=-1, keepdims=True)
    e = jnp.exp(scores - top)
    return e / jnp.sum(e, axis=-1, keepdims=True)


def forward_kernel(order, scal, qkv_ref, out_ref, nat, res):
    load_natural(scal, order, qkv_ref, nat)
    block = nat.shape[0] // len(order)
    k = nat[:, HEAD : 2 * HEAD]
    v = nat[:, 2 * HEAD :]
    for i in range(len(order)):
        upto = (i + 1) * block
        p = block_probs(nat[i * block : upto, :HEAD], k[:upto], block, i)
        res[i * block : upto, :] = dot_nn(p.astype(bf16), v[:upto]).astype(bf16)
    store_natural(scal, order, res, out_ref)


def backward_kernel(order, scal, qkv_ref, do_ref, out_ref, nat, dnat, res, dkt, dvt):
    load_natural(scal, order, qkv_ref, nat)
    load_natural(scal, order, do_ref, dnat)
    block = nat.shape[0] // len(order)
    k = nat[:, HEAD : 2 * HEAD]
    v = nat[:, 2 * HEAD :]
    dkt[...] = jnp.zeros_like(dkt)
    dvt[...] = jnp.zeros_like(dvt)
    for i in range(len(order)):
        upto = (i + 1) * block
        q = nat[i * block : upto, :HEAD]
        do = dnat[i * block : upto, :]
        p = block_probs(q, k[:upto], block, i)
        dvt[:, :upto] += dot_tn(do, p.astype(bf16))
        dp = dot_nt(do, v[:upto])
        ds = (p * (dp - jnp.sum(dp * p, axis=-1, keepdims=True))).astype(bf16)
        res[i * block : upto, :HEAD] = (dot_nn(ds, k[:upto]) * SCALE).astype(bf16)
        dkt[:, :upto] += dot_tn(q, ds)
    res[:, HEAD : 2 * HEAD] = (dkt[...].T * SCALE).astype(bf16)
    res[:, 2 * HEAD :] = dvt[...].T.astype(bf16)
    store_natural(scal, order, res, out_ref)


def norm_stats(v):
    mean = jnp.sum(v, axis=-1, keepdims=True) / D
    var = jnp.sum(v * v, axis=-1, keepdims=True) / D - mean * mean
    inverse = lax.rsqrt(var + 1e-05)
    return (v - mean) * inverse, inverse


def norm_back(grad, centred, inverse, gain):
    scaled = grad * gain
    first = jnp.sum(scaled, axis=-1, keepdims=True) / D
    second = jnp.sum(scaled * centred, axis=-1, keepdims=True) / D
    return inverse * (scaled - first - centred * second)


def stacked(refs, rows=slice(None)):
    return jnp.concatenate([r[rows, :] for r in refs], axis=0)


def halves_kernel(keep_ref, got_ref, keep, send):
    half = keep_ref.shape[0] // 2
    keep[...] = keep_ref[:half, :] + got_ref[:half, :].astype(f32)
    send[...] = (keep_ref[half:, :] + got_ref[half:, :].astype(f32)).astype(bf16)


def halves_out(value, keep, send):
    half = value.shape[0] // 2
    keep[...] = value[:half]
    send[...] = value[half:].astype(bf16)


def token_kernel(got, xg, vec):
    n_col, rows, width = got.shape
    two = xg.shape[0]
    for j in range(n_col):
        at = slice(j * width, (j + 1) * width)
        xg[:, at] = got[j, :two, :]
        v = got[j, two:, :].astype(f32)
        vec[:, at] = v[:8] + v[8:16] + v[16:24]


def qkv_kernel(heads, tokens, n_row, n_col, scal, *refs):
    xgs, (vec, shifts, own_qkv, own_out), refs = refs[:n_row], refs[n_row : n_row + 4], refs[n_row + 4 :]
    near, far, (cut, a1_out, w_all, w_out) = refs[: n_col - 1], refs[n_col - 1 : 2 * n_col - 2], refs[2 * n_col - 2 :]
    c, d = scal[1], scal[2]
    rows, width3 = own_qkv.shape
    half = rows // 2
    w_all[pl.ds(pl.multiple_of(c * rows, 64), rows), :] = own_qkv[...]
    w_out[c] = own_out[...]
    for k in range(1, n_col):
        for part, ref in ((d, near[k - 1]), (1 - d, far[k - 1])):
            w_all[pl.ds(pl.multiple_of(((c ^ k) * 2 + part) * half, 32), half), :] = ref[:, :width3]
            w_out[c ^ k, pl.ds(pl.multiple_of(part * half, 32), half), :] = ref[:, width3:]
    x = stacked(xgs, slice(0, tokens // n_row))
    centred, _ = norm_stats(x.astype(f32))
    a1 = (centred * vec[0:1, :] + vec[1:2, :]).astype(bf16)
    a1_out[...] = a1
    qkv = (dot_nn(a1, w_all[...]) + shifts[...]).astype(bf16)
    width = heads * HEAD
    for h in range(n_col):
        if h < heads:
            lo = h * HEAD
            piece = jnp.concatenate([qkv[:, j * width + lo : j * width + lo + HEAD] for j in range(3)], axis=1)
            cut[h] = beside(piece, tokens // n_row)
        else:
            cut[h] = jnp.zeros((tokens // 2, 6 * HEAD), bf16)


def out_kernel(heads, chunk, o, w, att_out, keep, send):
    att = jnp.concatenate([under(o[h], chunk) for h in range(heads)], axis=1)
    att_out[...] = att
    w_all = jnp.concatenate([w[j] for j in range(w.shape[0])], axis=1)
    halves_out(dot_nn(att, w_all), keep, send)


def norm2_kernel(keep, got, xg, vec, resid_out, a2_out):
    own = keep.shape[0]
    resid = xg[:own, :].astype(f32) + (keep[...] + got[...].astype(f32)) + vec[4:5, :]
    resid_out[...] = resid
    centred, _ = norm_stats(resid)
    a2_out[...] = (centred * vec[2:3, :] + vec[3:4, :]).astype(bf16)


def mlp_kernel(n_row, n_col, scal, *refs):
    a2s, gs, refs = refs[:n_row], refs[n_row : 2 * n_row], refs[2 * n_row :]
    up_bias, up_own, down_own = refs[:3]
    near, far = refs[3 : 2 + n_col], refs[2 + n_col : 1 + 2 * n_col]
    act_out, d_pre_out, bias_sum, a_keep, a_send, y_keep, y_send, wu, wd = refs[1 + 2 * n_col :]
    c, d = scal[1], scal[2]
    rows, width = up_own.shape
    half = width // 2
    mine = pl.ds(pl.multiple_of(d * half, 128), half)
    other = pl.ds(pl.multiple_of((1 - d) * half, 128), half)
    here = pl.ds(pl.multiple_of(c * rows, 64), rows)
    for w, own in ((wu, up_own), (wd, down_own)):
        w[here, :half] = own[:, mine]
        w[here, half:] = own[:, other]
    for k in range(1, n_col):
        there = pl.ds(pl.multiple_of((c ^ k) * rows, 64), rows)
        wu[there, :half] = near[k - 1][:rows, :]
        wd[there, :half] = near[k - 1][rows:, :]
        wu[there, half:] = far[k - 1][:rows, :]
        wd[there, half:] = far[k - 1][rows:, :]
    own = a2s[0].shape[0]
    shift = jnp.concatenate([up_bias[:, mine], up_bias[:, other]], axis=1)
    pre = dot_nn(stacked(a2s), wu[...]) + shift
    square = pre * pre
    t = jnp.tanh(C0 * (pre + C1 * (square * pre)))
    act = (0.5 * pre * (1.0 + t)).astype(bf16)
    slope = 0.5 * (1.0 + t) + (0.5 * C0) * pre * (1.0 - t * t) * (1.0 + (3.0 * C1) * square)
    d_act = dot_nn(stacked(gs, slice(own, 2 * own)), wd[...])
    d_pre = (d_act * slope).astype(bf16)
    act_out[...] = act
    d_pre_out[...] = d_pre
    total = jnp.sum(d_pre.astype(f32), axis=0, keepdims=True)
    bias_sum[:, mine] = total[:, :half]
    bias_sum[:, other] = total[:, half:]
    halves_out(dot_nt(d_pre, wu[...]), a_keep, a_send)
    halves_out(dot_nt(act, wd[...]), y_keep, y_send)


def mlp_grad_kernel(n_row, n_col, *refs):
    a2s, gs, refs = refs[:n_row], refs[n_row : 2 * n_row], refs[2 * n_row :]
    act, d_pre, mine, other = refs
    half = act.shape[1] // 2
    own = a2s[0].shape[0]
    a2, g = stacked(a2s), stacked(gs, slice(own, 2 * own))
    rows = a2.shape[1] // n_col
    for value, right, at in ((a2, d_pre, 0), (g, act, rows)):
        grad = dot_tn(value, right[...]).astype(bf16)
        for j in range(n_col):
            to = slice(2 * j * rows + at, 2 * j * rows + at + rows)
            mine[to, :] = grad[j * rows : (j + 1) * rows, :half]
            other[to, :] = grad[j * rows : (j + 1) * rows, half:]


def norm2_back_kernel(keep, got, xg, vec, resid_ref, gp_out, d_resid_out, sums):
    own = keep.shape[0]
    d_a2 = keep[...] + got[...].astype(f32)
    centred, inverse = norm_stats(resid_ref[...])
    g = xg[own:, :].astype(f32)
    d_resid = g + norm_back(d_a2, centred, inverse, vec[2:3, :])
    gp = d_resid.astype(bf16)
    d_resid_out[...] = d_resid
    gp_out[...] = gp
    for i, v in enumerate((d_a2 * centred, d_a2, gp.astype(f32), g)):
        sums[i : i + 1, :] = jnp.sum(v, axis=0, keepdims=True)


def d_att_kernel(n_row, heads, scal, *refs):
    gps, (att, w, cut, mine, other, full) = refs[:n_row], refs[n_row:]
    d = scal[2]
    gp = stacked(gps)
    n_col, rows, width = w.shape
    w_all = jnp.concatenate([w[j] for j in range(n_col)], axis=1)
    d_att = dot_nt(gp, w_all).astype(bf16)
    for h in range(n_col):
        if h < heads:
            cut[h] = beside(d_att[:, h * HEAD : (h + 1) * HEAD], gps[0].shape[0])
        else:
            cut[h] = jnp.zeros((gp.shape[0] // 2, 2 * HEAD), bf16)
    full[...] = dot_tn(att[...], gp).astype(bf16)
    half = rows // 2
    for to, part in ((mine, d), (other, 1 - d)):
        piece = full[pl.ds(pl.multiple_of(part * half, 32), half), :]
        for j in range(n_col):
            to[j * (half // 2) : (j + 1) * (half // 2), :] = beside(piece[:, j * width : (j + 1) * width], half)


def d_a1_kernel(n_row, heads, scal, *refs):
    xgs, (ds, a1, w), refs = refs[:n_row], refs[n_row : n_row + 3], refs[n_row + 3 :]
    keep, send, sums, mine, other, full = refs
    d = scal[2]
    tokens = a1.shape[0]
    pieces = [under(ds[h], tokens // n_row) for h in range(heads)]
    d_qkv = jnp.concatenate([p[:, j * HEAD : (j + 1) * HEAD] for j in range(3) for p in pieces], axis=1)
    part = dot_nt(d_qkv, w[...])
    halves_out(part, keep, send)
    full[...] = dot_tn(a1[...], d_qkv).astype(bf16)
    n_col = ds.shape[0]
    half = full.shape[0] // (2 * n_col)
    for j in range(n_col):
        at = slice(j * half, (j + 1) * half)
        mine[at, :] = full[pl.ds(pl.multiple_of((2 * j + d) * half, 32), half), :]
        other[at, :] = full[pl.ds(pl.multiple_of((2 * j + 1 - d) * half, 32), half), :]
    centred, _ = norm_stats(stacked(xgs, slice(0, tokens // n_row)).astype(f32))
    sums[...] = jnp.zeros_like(sums)
    sums[0:1, :] = jnp.sum(part * centred, axis=0, keepdims=True)
    sums[1:2, :] = jnp.sum(part, axis=0, keepdims=True)
    sums[2:3, : d_qkv.shape[1]] = jnp.sum(d_qkv.astype(f32), axis=0, keepdims=True)


def final_kernel(a_keep, a_got, y_keep, y_got, xg, vec, resid, d_resid, out):
    n_col, rows, width = out.shape
    own = rows // 2
    d_a1 = a_keep[...] + a_got[...].astype(f32)
    centred, inverse = norm_stats(xg[:own, :].astype(f32))
    d_x = (d_resid[...] + norm_back(d_a1, centred, inverse, vec[0:1, :])).astype(bf16)
    y = (resid[...] + (y_keep[...] + y_got[...].astype(f32)) + vec[5:6, :]).astype(bf16)
    for j in range(n_col):
        out[j, :own, :] = d_x[:, j * width : (j + 1) * width]
        out[j, own:, :] = y[:, j * width : (j + 1) * width]


def part_kernel(n_in, scal, *refs):
    mine, got, outs = refs[:n_in], refs[n_in : 2 * n_in], refs[2 * n_in :]
    n_col = len(outs)
    at = 0
    for m, g in zip(mine, got):
        rows = m.shape[0] // n_col
        for k in range(n_col):
            there = pl.ds(pl.multiple_of((scal[1] ^ k) * rows, 16), rows)
            total = m[there, :].astype(f32) + g[there, :].astype(f32)
            outs[k][at : at + rows, :] = total.astype(outs[k].dtype)
        at += rows


def add_kernel(*refs):
    total = refs[0][...].astype(f32)
    for r in refs[1:-1]:
        total = total + r[...].astype(f32)
    refs[-1][...] = total.astype(refs[-1].dtype)


def mlp_out_kernel(scal, part, away, up, down, out):
    d = scal[2]
    rows, width = up.shape
    half = width // 2
    for ref, index in ((part, d), (away, 1 - d)):
        lanes = pl.ds(pl.multiple_of(index * half, 128), half)
        up[:, lanes] = ref[:rows, :].astype(f32)
        down[:, lanes] = ref[rows : 2 * rows, :].astype(f32)
        piece = under(ref[2 * rows :, :].astype(f32), rows // 2)
        out[pl.ds(pl.multiple_of(index * (rows // 2), 32), rows // 2), :] = piece


def qkv_out_kernel(scal, part, away, out):
    half = part.shape[0]
    out[pl.ds(pl.multiple_of(scal[2] * half, 32), half), :] = part[...].astype(f32)
    out[pl.ds(pl.multiple_of((1 - scal[2]) * half, 32), half), :] = away[...].astype(f32)


def sum_parts(pairs, scal):
    n_col = lax.axis_size("col")
    mine = [m for m, _ in pairs]
    got = [swap(o, "dp", 1) for _, o in pairs]
    rows = sum(m.shape[0] for m in mine) // n_col
    width = mine[0].shape[1]
    parts = call(
        functools.partial(part_kernel, len(mine)),
        [((rows, width), f32)] + [((rows, width), bf16)] * (n_col - 1),
        scal,
        [*mine, *got],
    )
    got = [swap(parts[k], "col", k) for k in range(1, n_col)]
    total = call(add_kernel, [((rows, width), bf16)], None, [parts[0], *got])[0]
    for b in bits_of("dp", 2):
        total = call(add_kernel, [((rows, width), bf16)], None, [total, swap(total, "dp", b)])[0]
    return total, swap(total, "dp", 1)


def body(
    block_input,
    ln1_gain,
    ln1_bias,
    qkv_weight,
    qv_bias,
    out_weight,
    out_bias,
    ln2_gain,
    ln2_bias,
    up_weight,
    up_bias,
    down_weight,
    down_bias,
    out_grad,
):
    n_col = lax.axis_size("col")
    n_row = lax.axis_size("row")
    width_in = D // n_col
    width_out = D // n_row
    heads = width_out // HEAD
    order = row_order()
    own = block_input.shape[0] // n_col
    tokens = own * n_row
    half_ff = up_weight.shape[1] // 2
    ff = 2 * half_ff
    cols = range(1, n_col)
    c = lax.axis_index("col").astype(jnp.int32)
    d = lax.axis_index("dp").astype(jnp.int32) & 1
    scal = jnp.stack([lax.axis_index("row").astype(jnp.int32), c, d])
    token_sum = [((tokens // 2, D), f32), ((tokens // 2, D), bf16)]

    zero = jnp.zeros_like(ln1_gain)
    vectors = three_parts(jnp.stack([ln1_gain, ln1_bias, ln2_gain, ln2_bias, out_bias, down_bias, zero, zero]))
    message = jnp.concatenate(
        [
            block_input.reshape(n_col, own, width_in),
            out_grad.reshape(n_col, own, width_in),
            jnp.broadcast_to(jnp.pad(vectors, ((0, 8), (0, 0)))[None], (n_col, 32, width_in)),
        ],
        axis=1,
    )
    got = turn(message.reshape(-1, width_in)).reshape(message.shape)
    xg_own, vec = call(token_kernel, [((2 * own, D), bf16), ((8, D), f32)], None, [got])

    own_qkv = qkv_weight.reshape(width_in, 3 * width_out)
    own_out = out_weight.reshape(width_out, width_in)
    both = jnp.concatenate([own_qkv, own_out], axis=1)
    half_a = lax.dynamic_slice_in_dim(both, d * (width_in // 2), width_in // 2, 0)
    near_a = [swap(half_a, "col", k) for k in cols]
    near_a, up_w, down_w = lax.optimization_barrier((near_a, up_weight, down_weight))
    far_a = [swap(v, "dp", 1) for v in near_a]
    half_m = jnp.concatenate(
        [lax.dynamic_slice_in_dim(w, d * half_ff, half_ff, 1) for w in (up_w, down_w)], axis=0
    )
    near_m = [swap(half_m, "col", k) for k in cols]
    far_m = [swap(v, "dp", 1) for v in near_m]

    xg = gather_row(xg_own)
    shifts = jnp.concatenate([qv_bias[0], jnp.zeros_like(qv_bias[0]), qv_bias[1]])[None]
    qkv_cut, a1, w_qkv, w_out = call(
        functools.partial(qkv_kernel, heads, tokens, n_row, n_col),
        [
            ((n_col, tokens // 2, 6 * HEAD), bf16),
            ((tokens, D), bf16),
            ((D, 3 * width_out), bf16),
            ((n_col, width_out, width_in), bf16),
        ],
        scal,
        [*xg, vec, shifts, own_qkv, own_out, *near_a, *far_a],
    )
    qkv_head = turn(qkv_cut)
    att_head = call(
        functools.partial(forward_kernel, order),
        [((n_col, tokens // 2, 2 * HEAD), bf16)],
        scal,
        [qkv_head],
        [((tokens * n_col, 3 * HEAD), bf16), ((tokens * n_col, HEAD), bf16)],
    )[0]
    attended, o_keep, o_send = call(
        functools.partial(out_kernel, heads, own),
        [((tokens, width_out), bf16)] + token_sum,
        None,
        [turn(att_head), w_out],
    )
    resid1, a2_own = call(
        norm2_kernel, [((own, D), f32), ((own, D), bf16)], None, [*finish_row(o_keep, o_send), xg_own, vec]
    )
    a2 = gather_row(a2_own)
    act, d_pre, up_sum, a_keep, a_send, y_keep, y_send = call(
        functools.partial(mlp_kernel, n_row, n_col),
        [((tokens, ff), bf16), ((tokens, ff), bf16), ((1, ff), f32)] + token_sum + token_sum,
        scal,
        [*a2, *xg, up_bias[None], up_weight, down_weight, *near_m, *far_m],
        [((D, ff), bf16), ((D, ff), bf16)],
    )
    gp, d_resid1, sums2 = call(
        norm2_back_kernel,
        [((own, D), bf16), ((own, D), f32), ((4, D), f32)],
        None,
        [*finish_row(a_keep, a_send), xg_own, vec, resid1],
    )
    gp_all = gather_row(gp)
    mlp_mine, mlp_other = call(
        functools.partial(mlp_grad_kernel, n_row, n_col),
        [((2 * D, half_ff), bf16)] * 2,
        None,
        [*a2, *xg, act, d_pre],
    )
    d_att_cut, out_mine, out_other = call(
        functools.partial(d_att_kernel, n_row, heads),
        [((n_col, tokens // 2, 2 * HEAD), bf16)] + [((n_col * width_out // 4, 2 * width_in), bf16)] * 2,
        scal,
        [*gp_all, attended, w_out],
        [((width_out, D), bf16)],
    )
    d_qkv_head = call(
        functools.partial(backward_kernel, order),
        [((n_col, tokens // 2, 6 * HEAD), bf16)],
        scal,
        [qkv_head, turn(d_att_cut)],
        [
            ((tokens * n_col, 3 * HEAD), bf16),
            ((tokens * n_col, HEAD), bf16),
            ((tokens * n_col, 3 * HEAD), bf16),
            ((HEAD, tokens * n_col), f32),
            ((HEAD, tokens * n_col), f32),
        ],
    )[0]
    d_keep, d_send, sums1, qkv_mine, qkv_other = call(
        functools.partial(d_a1_kernel, n_row, heads),
        token_sum + [((3, D), f32)] + [((D // 2, 3 * width_out), bf16)] * 2,
        scal,
        [*xg, turn(d_qkv_head), a1, w_qkv],
        [((D, 3 * width_out), bf16)],
    )

    d_up, d_down, d_out = call(
        mlp_out_kernel,
        [((width_in, ff), f32), ((width_in, ff), f32), ((width_out, width_in), f32)],
        scal,
        sum_parts([(mlp_mine, mlp_other), (out_mine, out_other)], scal),
    )
    d_qkv = call(qkv_out_kernel, [((width_in, 3 * width_out), f32)], scal, sum_parts([(qkv_mine, qkv_other)], scal))[0]

    outs = call(
        final_kernel,
        [((n_col, 2 * own, width_in), bf16)],
        None,
        [*finish_row(d_keep, d_send), *finish_row(y_keep, y_send), xg_own, vec, resid1, d_resid1],
    )[0]
    outs = turn(outs)
    input_grad = outs[:, :own].reshape(-1, width_in)
    block_output = outs[:, own:].reshape(-1, width_in)

    sums = jnp.concatenate([sums1[:2], sums2, up_sum.reshape(-1, D), sums1[2:]])
    for axis in ("col", "dp"):
        for b in bits_of(axis):
            sums = sums + swap(sums, axis, b)
    feats = sums[:6]
    for b in bits_of("row"):
        feats = feats + swap(feats, "row", b)
    feats = lax.dynamic_slice_in_dim(feats, c * width_in, width_in, 1)
    d_qv_bias = jnp.stack([sums[-1, :width_out], sums[-1, 2 * width_out : 3 * width_out]])

    return (
        block_output,
        input_grad,
        feats[0],
        feats[1],
        d_qkv.reshape(1, 1, -1),
        d_qv_bias,
        d_out.reshape(1, 1, -1),
        feats[4],
        feats[2],
        feats[3],
        d_up,
        sums[6:-1].reshape(ff),
        d_down,
        feats[5],
    )


def solution(mesh):
    in_specs = (
        P(("dp", "row"), "col"),
        P("col"),
        P("col"),
        P("col", "row", None),
        P(None, "row"),
        P("row", "col", None),
        P("col"),
        P("col"),
        P("col"),
        P("col", "row"),
        P("row"),
        P("col", "row"),
        P("col"),
        P(("dp", "row"), "col"),
    )
    out_specs = (
        P(("dp", "row"), "col"),
        P(("dp", "row"), "col"),
        P("col"),
        P("col"),
        P("col", "row", None),
        P(None, "row"),
        P("row", "col", None),
        P("col"),
        P("col"),
        P("col"),
        P("col", "row"),
        P("row"),
        P("col", "row"),
        P("col"),
    )
    return jax.shard_map(body, mesh=mesh, in_specs=in_specs, out_specs=out_specs, check_vma=False)
```

time: 341 us -> 238 us (0.70)
  blocking collectives: 127 us -> 14 us
  waiting for transfers between devices: 66.7 us -> 104 us
  Pallas kernels: 6.78 us -> 26.3 us
  between operations: 15.1 us -> 1.18 us
  matrix products: 13.7 us -> 0 us
  other arithmetic: 16.3 us -> 3.58 us
  local copies, waits for them, and re-layouts: 24.1 us -> 18.3 us
    all_gather x3 -> x0, blocking collectives: 65.9 us -> none  [the longest x1 36.7 us: body(): lax.all_gather(qkv_weight.reshape(width_in, 3 * width_out), 'col', axis=0...]
    psum x2 -> x0, blocking collectives: 61.5 us -> none  [the longest x1 39.5 us: body(): lax.psum(jnp.stack([column_sums(d_a1_part * centred1), column_sums(d_a1_p...]
    ppermute x24 -> x45, waiting for transfers between devices: 22.1 us -> 70 us  [swap(): return lax.ppermute(value, axis, [(i, i ^ bit) for i in range(n)])]
    ppermute x24 -> x45, starting transfers between devices: 17.4 us -> 45.6 us  [swap(): return lax.ppermute(value, axis, [(i, i ^ bit) for i in range(n)])]
    pallas_call x2 -> x22, Pallas kernels: 6.78 us -> 26.3 us  [call(): pl.pallas_call(kernel, out_shape=[jax.ShapeDtypeStruct(s, t) for s, t in...]
    ppermute x12 -> x0, starting transfers between devices: 17.4 us -> none  [sum_cols(): lax.ppermute(piece, 'col', [(i, (i + k) % n) for i in range(n)]).astype(f32)]
    all_to_all x0 -> x1, blocking collectives: none -> 14 us  [turn(): return lax.all_to_all(value, 'col', split, concat, tiled=True)]
    dot_general x12 -> x0, matrix products: 13.7 us -> none  [the longest x4 5.89 us: dot_nn(): lax.dot_general(a, b, (((1,), (0,)), ((), ())), preferred_element_type=f32)]
  transfers between devices with their start and end apart: 46 -> 50, of which waited for: 18 -> 25; matrix products, arithmetic and copies ran while one was open for 13% -> 3% of each run, Pallas kernels for 2% -> 6%
where the time goes in v3:
time: 238 us; the launch traced here: 237 us
  waiting for transfers between devices  104 us (44%)
  starting transfers between devices  69.1 us (29%)
  Pallas kernels  26.3 us (11%)
  local copies, waits for them, and re-layouts  18.3 us (8%)
  blocking collectives  14 us (6%)
  other arithmetic  3.58 us (2%)
    ppermute x45, waiting for transfers between devices, swap(): return lax.ppermute(value, axis, [(i, i ^ bit) for i in range(n)])  70 us
    ppermute x45, starting transfers between devices, swap(): return lax.ppermute(value, axis, [(i, i ^ bit) for i in range(n)])  45.6 us
    all_to_all x5, waiting for transfers between devices, turn(): return lax.all_to_all(value, 'col', split, concat, tiled=True)  34.3 us
    pallas_call x22, Pallas kernels, call(): pl.pallas_call(kernel, out_shape=[jax.ShapeDtypeStruct(s, t) for s, t in...  26.3 us
    all_to_all x5, starting transfers between devices, turn(): return lax.all_to_all(value, 'col', split, concat, tiled=True)  23.5 us
    all_to_all x1, blocking collectives, turn(): return lax.all_to_all(value, 'col', split, concat, tiled=True)  14 us
    unnamed x72, local copies, waits for them, and re-layouts  12.5 us
  transfers between devices with their start and end apart: 50, of which 25 were waited for; matrix products, arithmetic and copies ran while one was open for 3% of the time, Pallas kernels for 6%

profile of v3, /device:TPU:0, one launch (start us, length us, event | category | flops | bytes accessed | tf_op | source)
XLA Modules:
  0.0 236.8 jit_solution(7993834734083836313)
XLA Ops:
  4.4 6.3 %all-to-all-start = ((bf16[4,160,192]{2,1,0:T(8,128)(2,1)}), bf16[4,160,192]{2,1,0:T(8,128)(2,1)S(1)}, u32[]{:S(2)}, u32[]{:S(2)}) async-start(bf16[4,160,192]{2,1,0:T(8,128)(2,1)} %pad_maximum_fusion), calls=%async_computation | async-start | bytes 655360 | tf_op jit(solution)/shard_map/all_to_all | solution.py:52
  12.9 3.0 %collective-permute-start.4 = (bf16[96,768]{1,0:T(8,128)(2,1)S(1)}, bf16[96,768]{1,0:T(8,128)(2,1)S(1)}, u32[]{:S(2)}, u32[]{:S(2)}) collective-permute-start(bf16[96,768]{1,0:T(8,128)(2,1)S(1)} %fusion), channel_id=1, source_target_pairs={{0,2},{1,3},{2,0},{3,1},{4,6},{5,7},{6,4},{7,5},{8,10},{9,11},{10,... | collective-permute-start | bytes 442376 | tf_op jit(solution)/shard_map/ppermute | solution.py:48
  17.4 8.0 %all-to-all-done.got = bf16[4,160,192]{2,1,0:T(8,128)(2,1)S(1)} async-done(((bf16[4,160,192]{2,1,0:T(8,128)(2,1)}), bf16[4,160,192]{2,1,0:T(8,128)(2,1)S(1)}, u32[]{:S(2)}, u32[]{:S(2)}) %all-to-all-start) | async-done | bytes 245792 | tf_op jit(solution)/shard_map/all_to_all | solution.py:52
  27.1 4.4 %collective-permute-done.4.refs_9_ = bf16[96,768]{1,0:T(8,128)(2,1)S(1)} collective-permute-done((bf16[96,768]{1,0:T(8,128)(2,1)S(1)}, bf16[96,768]{1,0:T(8,128)(2,1)S(1)}, u32[]{:S(2)}, u32[]{:S(2)}) %collective-permute-start.4) | collective-permute-done | bytes 147488 | tf_op jit(solution)/shard_map/ppermute | solution.py:48
  44.1 6.3 %all-to-all-start.1 = ((bf16[4,128,384]{2,1,0:T(8,128)(2,1)}), bf16[4,128,384]{2,1,0:T(8,128)(2,1)S(1)}, u32[]{:S(2)}, u32[]{:S(2)}) async-start(bf16[4,128,384]{2,1,0:T(8,128)(2,1)} %get-tuple-element.74), calls=%async_computation.1 | async-start | bytes 786432 | tf_op jit(solution)/shard_map/all_to_all | solution.py:52
  50.5 10.1 %all-to-all-done.1.qkv_ref = bf16[4,128,384]{2,1,0:T(8,128)(2,1)S(1)} async-done(((bf16[4,128,384]{2,1,0:T(8,128)(2,1)}), bf16[4,128,384]{2,1,0:T(8,128)(2,1)S(1)}, u32[]{:S(2)}, u32[]{:S(2)}) %all-to-all-start.1) | async-done | bytes 393248 | tf_op jit(solution)/shard_map/all_to_all | solution.py:52
  60.6 3.8 %shard_map.247 = bf16[4,128,128]{2,1,0:T(8,128)(2,1)} custom-call(s32[3]{0:T(128)S(1)} %pad_add_fusion.scal, bf16[4,128,384]{2,1,0:T(8,128)(2,1)S(1)} %all-to-all-done.1.qkv_ref), custom_call_target="tpu_custom_call" | custom-call | tf_op jit(solution)/shard_map/pallas_call | solution.py:36
  64.4 3.3 %all-to-all-start.2 = ((bf16[4,128,128]{2,1,0:T(8,128)(2,1)}), bf16[4,128,128]{2,1,0:T(8,128)(2,1)S(1)}, u32[]{:S(2)}, u32[]{:S(2)}) async-start(bf16[4,128,128]{2,1,0:T(8,128)(2,1)} %shard_map.247), calls=%async_computation.2 | async-start | bytes 262144 | tf_op jit(solution)/shard_map/all_to_all | solution.py:52
  67.8 3.8 %collective-permute-start.16 = (bf16[384,384]{1,0:T(8,128)(2,1)S(1)}, bf16[384,384]{1,0:T(8,128)(2,1)S(1)}, u32[]{:S(2)}, u32[]{:S(2)}) collective-permute-start(bf16[384,384]{1,0:T(8,128)(2,1)S(1)} %pad_maximum_fusion.1), channel_id=1, source_target_pairs={{0,3},{1,2},{2,1},{3,0},{4,7},{5,6},{6,5},{7,4},{8,11},{9,10},{10,... | collective-permute-start | bytes 884744 | tf_op jit(solution)/shard_map/ppermute | solution.py:48
  72.3 14.2 %all-to-all-done.2.o = bf16[4,128,128]{2,1,0:T(8,128)(2,1)S(1)} async-done(((bf16[4,128,128]{2,1,0:T(8,128)(2,1)}), bf16[4,128,128]{2,1,0:T(8,128)(2,1)S(1)}, u32[]{:S(2)}, u32[]{:S(2)}) %all-to-all-start.2) | async-done | bytes 131104 | tf_op jit(solution)/shard_map/all_to_all | solution.py:52
  90.1 8.4 %collective-permute-done.15.refs_12_ = bf16[384,384]{1,0:T(8,128)(2,1)S(1)} collective-permute-done((bf16[384,384]{1,0:T(8,128)(2,1)S(1)}, bf16[384,384]{1,0:T(8,128)(2,1)S(1)}, u32[]{:S(2)}, u32[]{:S(2)}) %collective-permute-start.15) | collective-permute-done | bytes 294944 | tf_op jit(solution)/shard_map/ppermute | solution.py:48
  102.4 3.1 %collective-permute-done.11.refs_1_ = bf16[64,768]{1,0:T(8,128)(2,1)S(1)} collective-permute-done((bf16[64,768]{1,0:T(8,128)(2,1)S(1)}, bf16[64,768]{1,0:T(8,128)(2,1)S(1)}, u32[]{:S(2)}, u32[]{:S(2)}) %collective-permute-start.11) | collective-permute-done | bytes 98336 | tf_op jit(solution)/shard_map/ppermute | solution.py:48
  105.5 3.0 %collective-permute-done.18.refs_15_ = bf16[384,384]{1,0:T(8,128)(2,1)S(1)} collective-permute-done((bf16[384,384]{1,0:T(8,128)(2,1)S(1)}, bf16[384,384]{1,0:T(8,128)(2,1)S(1)}, u32[]{:S(2)}, u32[]{:S(2)}) %collective-permute-start.18) | collective-permute-done | bytes 294944 | tf_op jit(solution)/shard_map/ppermute | solution.py:48
  108.5 4.1 %collective-permute-done.17.refs_14_ = bf16[384,384]{1,0:T(8,128)(2,1)S(1)} collective-permute-done((bf16[384,384]{1,0:T(8,128)(2,1)}, bf16[384,384]{1,0:T(8,128)(2,1)S(1)}, u32[]{:S(2)}, u32[]{:S(2)}) %collective-permute-start.17) | collective-permute-done | bytes 294944 | tf_op jit(solution)/shard_map/ppermute | solution.py:48
  114.5 3.4 %shard_map.251 = (bf16[256,768]{1,0:T(8,128)(2,1)S(1)}, bf16[256,768]{1,0:T(8,128)(2,1)S(1)}, f32[1,768]{1,0:T(1,128)S(1)}, f32[128,768]{1,0:T(8,128)S(1)}, bf16...) custom-call(s32[3]{0:T(128)S(1)} %pad_add_fusion.scal, ...), custom_call_target="tpu_custom_call" | custom-call | tf_op jit(solution)/shard_map/pallas_call | solution.py:36
  121.1 3.3 %collective-permute-done.21.got = bf16[64,768]{1,0:T(8,128)(2,1)S(1)} collective-permute-done((bf16[64,768]{1,0:T(8,128)(2,1)S(1)}, bf16[64,768]{1,0:T(8,128)(2,1)S(1)}, u32[]{:S(2)}, u32[]{:S(2)}) %collective-permute-start.21) | collective-permute-done | bytes 98336 | tf_op jit(solution)/shard_map/ppermute | solution.py:48
  126.9 3.1 %collective-permute-done.22.refs_1_ = bf16[64,768]{1,0:T(8,128)(2,1)S(1)} collective-permute-done((bf16[64,768]{1,0:T(8,128)(2,1)S(1)}, bf16[64,768]{1,0:T(8,128)(2,1)S(1)}, u32[]{:S(2)}, u32[]{:S(2)}) %collective-permute-start.22) | collective-permute-done | bytes 98336 | tf_op jit(solution)/shard_map/ppermute | solution.py:48
  133.7 4.1 %all-to-all-start.3 = ((bf16[4,128,128]{2,1,0:T(8,128)(2,1)}), bf16[4,128,128]{2,1,0:T(8,128)(2,1)}, u32[]{:S(2)}, u32[]{:S(2)}) async-start(bf16[4,128,128]{2,1,0:T(8,128)(2,1)} %get-tuple-element.90), calls=%async_computation.3 | async-start | bytes 262144 | tf_op jit(solution)/shard_map/all_to_all | solution.py:52
  144.1 5.7 %shard_map.255 = bf16[4,128,384]{2,1,0:T(8,128)(2,1)S(1)} custom-call(s32[3]{0:T(128)S(1)} %pad_add_fusion.scal, bf16[4,128,384]{2,1,0:T(8,128)(2,1)S(1)} %all-to-all-done.1.qkv_ref, bf16[4,128,128]{2,1,0:T(8,128)(2,1)} %all-to-all-done.3.do_ref), custom_call_target="tpu_custom_call" | custom-call | tf_op jit(solution)/shard_map/pallas_call | solution.py:36
  149.8 14.0 %all_to_all.31.refs_4_ = bf16[4,128,384]{2,1,0:T(8,128)(2,1)S(1)} all-to-all(bf16[4,128,384]{2,1,0:T(8,128)(2,1)S(1)} %shard_map.255), channel_id=1, replica_groups=mesh['dp'=2,'row'=4,'col'=4] {'col'}, dimensions={0} | all-to-all | bytes 786432 | tf_op jit(solution)/shard_map/all_to_all | solution.py:52
  172.7 4.5 %collective-permute-done.30 = f32[8,768]{1,0:T(8,128)S(1)} collective-permute-done((f32[8,768]{1,0:T(8,128)S(1)}, f32[8,768]{1,0:T(8,128)S(1)}, u32[]{:S(2)}, u32[]{:S(2)}) %collective-permute-start.30) | collective-permute-done | bytes 24608 | tf_op jit(solution)/shard_map/ppermute | solution.py:48
  193.1 13.2 %collective-permute-done.42.refs_2_ = bf16[432,384]{1,0:T(8,128)(2,1)S(1)} collective-permute-done((bf16[432,384]{1,0:T(8,128)(2,1)S(1)}, bf16[432,384]{1,0:T(8,128)(2,1)S(1)}, u32[]{:S(2)}, u32[]{:S(2)}) %collective-permute-start.42) | collective-permute-done | bytes 331808 | tf_op jit(solution)/shard_map/ppermute | solution.py:48
  212.1 3.4 %all-to-all-start.5 = ((bf16[4,128,192]{1,2,0:T(8,128)(2,1)}), bf16[4,128,192]{1,2,0:T(8,128)(2,1)S(1)}, u32[]{:S(2)}, u32[]{:S(2)}) async-start(bf16[4,128,192]{1,2,0:T(8,128)(2,1)} %copy.37), calls=%async_computation.5 | async-start | bytes 393216 | tf_op jit(solution)/shard_map/all_to_all | solution.py:52
  223.5 6.4 %collective-permute-done.36.refs_2_ = bf16[96,576]{1,0:T(8,128)(2,1)S(1)} collective-permute-done((bf16[96,576]{1,0:T(8,128)(2,1)S(1)}, bf16[96,576]{1,0:T(8,128)(2,1)S(1)}, u32[]{:S(2)}, u32[]{:S(2)}) %collective-permute-start.36) | collective-permute-done | bytes 110624 | tf_op jit(solution)/shard_map/ppermute | solution.py:48
  (210 shorter events, 92.6 us)
Async XLA Ops:
  4.4 21.1 %all-to-all-start = ((bf16[4,160,192]{2,1,0:T(8,128)(2,1)}), bf16[4,160,192]{2,1,0:T(8,128)(2,1)S(1)}, u32[]{:S(2)}, u32[]{:S(2)}) async-start(bf16[4,160,192]{2,1,0:T(8,128)(2,1)} %pad_maximum_fusion), calls=%async_computation | async-start | bytes 655360 | tf_op jit(solution)/shard_map/all_to_all | solution.py:52
  12.9 18.6 %collective-permute-start.4 = (bf16[96,768]{1,0:T(8,128)(2,1)S(1)}, bf16[96,768]{1,0:T(8,128)(2,1)S(1)}, u32[]{:S(2)}, u32[]{:S(2)}) collective-permute-start(bf16[96,768]{1,0:T(8,128)(2,1)S(1)} %fusion), channel_id=1, source_target_pairs={{0,2},{1,3},{2,0},{3,1},{4,6},{5,7},{6,4},{7,5},{8,10},{9,11},{10,... | collective-permute-start | bytes 442376 | tf_op jit(solution)/shard_map/ppermute | solution.py:48
  15.9 15.6 %collective-permute-start.3 = (bf16[96,768]{1,0:T(8,128)(2,1)S(1)}, bf16[96,768]{1,0:T(8,128)(2,1)S(1)}, u32[]{:S(2)}, u32[]{:S(2)}) collective-permute-start(bf16[96,768]{1,0:T(8,128)(2,1)S(1)} %fusion), channel_id=1, source_target_pairs={{0,1},{1,0},{2,3},{3,2},{4,5},{5,4},{6,7},{7,6},{8,9},{9,8},{10,11... | collective-permute-start | bytes 442376 | tf_op jit(solution)/shard_map/ppermute | solution.py:48
  17.4 14.2 %collective-permute-start.5 = (bf16[96,768]{1,0:T(8,128)(2,1)S(1)}, bf16[96,768]{1,0:T(8,128)(2,1)S(1)}, u32[]{:S(2)}, u32[]{:S(2)}) collective-permute-start(bf16[96,768]{1,0:T(8,128)(2,1)S(1)} %fusion), channel_id=1, source_target_pairs={{0,3},{1,2},{2,1},{3,0},{4,7},{5,6},{6,5},{7,4},{8,11},{9,10},{10,... | collective-permute-start | bytes 442376 | tf_op jit(solution)/shard_map/ppermute | solution.py:48
  44.1 16.5 %all-to-all-start.1 = ((bf16[4,128,384]{2,1,0:T(8,128)(2,1)}), bf16[4,128,384]{2,1,0:T(8,128)(2,1)S(1)}, u32[]{:S(2)}, u32[]{:S(2)}) async-start(bf16[4,128,384]{2,1,0:T(8,128)(2,1)} %get-tuple-element.74), calls=%async_computation.1 | async-start | bytes 786432 | tf_op jit(solution)/shard_map/all_to_all | solution.py:52
  64.4 22.1 %all-to-all-start.2 = ((bf16[4,128,128]{2,1,0:T(8,128)(2,1)}), bf16[4,128,128]{2,1,0:T(8,128)(2,1)S(1)}, u32[]{:S(2)}, u32[]{:S(2)}) async-start(bf16[4,128,128]{2,1,0:T(8,128)(2,1)} %shard_map.247), calls=%async_computation.2 | async-start | bytes 262144 | tf_op jit(solution)/shard_map/all_to_all | solution.py:52
  67.8 19.1 %collective-permute-start.16 = (bf16[384,384]{1,0:T(8,128)(2,1)S(1)}, bf16[384,384]{1,0:T(8,128)(2,1)S(1)}, u32[]{:S(2)}, u32[]{:S(2)}) collective-permute-start(bf16[384,384]{1,0:T(8,128)(2,1)S(1)} %pad_maximum_fusion.1), channel_id=1, source_target_pairs={{0,3},{1,2},{2,1},{3,0},{4,7},{5,6},{6,5},{7,4},{8,11},{9,10},{10,... | collective-permute-start | bytes 884744 | tf_op jit(solution)/shard_map/ppermute | solution.py:48
  71.6 26.9 %collective-permute-start.15 = (bf16[384,384]{1,0:T(8,128)(2,1)S(1)}, bf16[384,384]{1,0:T(8,128)(2,1)S(1)}, u32[]{:S(2)}, u32[]{:S(2)}) collective-permute-start(bf16[384,384]{1,0:T(8,128)(2,1)S(1)} %pad_maximum_fusion.1), channel_id=1, source_target_pairs={{0,2},{1,3},{2,0},{3,1},{4,6},{5,7},{6,4},{7,5},{8,10},{9,11},{10,... | collective-permute-start | bytes 884744 | tf_op jit(solution)/shard_map/ppermute | solution.py:48
  71.6 28.4 %collective-permute-start.14 = (bf16[384,384]{1,0:T(8,128)(2,1)S(1)}, bf16[384,384]{1,0:T(8,128)(2,1)}, u32[]{:S(2)}, u32[]{:S(2)}) collective-permute-start(bf16[384,384]{1,0:T(8,128)(2,1)S(1)} %pad_maximum_fusion.1), channel_id=1, source_target_pairs={{0,1},{1,0},{2,3},{3,2},{4,5},{5,4},{6,7},{7,6},{8,9},{9,8},{10,11... | collective-permute-start | bytes 884744 | tf_op jit(solution)/shard_map/ppermute | solution.py:48
  86.9 18.6 %collective-permute-start.19 = (bf16[384,384]{1,0:T(8,128)(2,1)S(1)}, bf16[384,384]{1,0:T(8,128)(2,1)S(1)}, u32[]{:S(2)}, u32[]{:S(2)}) collective-permute-start(bf16[384,384]{1,0:T(8,128)(2,1)S(1)} %collective-permute-done.16.refs_13_), channel_id=1, source_target_pairs={{0,16},{16,0},{1,17},{17,1},{2,18},{18,2},{3,19},{19,3},{4,20},{20... | collective-permute-start | bytes 884744 | tf_op jit(solution)/shard_map/ppermute | solution.py:48
  88.5 12.1 %collective-permute-start.10 = (bf16[64,768]{1,0:T(8,128)(2,1)S(1)}, bf16[64,768]{1,0:T(8,128)(2,1)S(1)}, u32[]{:S(2)}, u32[]{:S(2)}) collective-permute-start(bf16[64,768]{1,0:T(8,128)(2,1)S(1)} %get-tuple-element.79), channel_id=1, source_target_pairs={{0,8},{4,12},{8,0},{12,4},{1,9},{5,13},{9,1},{13,5},{2,10},{6,14},... | collective-permute-start | bytes 294920 | tf_op jit(solution)/shard_map/ppermute | solution.py:48
  100.1 12.5 %collective-permute-start.17 = (bf16[384,384]{1,0:T(8,128)(2,1)}, bf16[384,384]{1,0:T(8,128)(2,1)S(1)}, u32[]{:S(2)}, u32[]{:S(2)}) collective-permute-start(bf16[384,384]{1,0:T(8,128)(2,1)} %collective-permute-done.14.refs_11_), channel_id=1, source_target_pairs={{0,16},{16,0},{1,17},{17,1},{2,18},{18,2},{3,19},{19,3},{4,20},{20... | collective-permute-start | bytes 884744 | tf_op jit(solution)/shard_map/ppermute | solution.py:48
  102.4 10.2 %collective-permute-start.12 = (bf16[64,768]{1,0:T(8,128)(2,1)S(1)}, bf16[64,768]{1,0:T(8,128)(2,1)S(1)}, u32[]{:S(2)}, u32[]{:S(2)}) collective-permute-start(bf16[64,768]{1,0:T(8,128)(2,1)S(1)} %get-tuple-element.80.refs_0_), channel_id=1, source_target_pairs={{0,4},{4,0},{8,12},{12,8},{1,5},{5,1},{9,13},{13,9},{2,6},{6,2},{1... | collective-permute-start | bytes 294920 | tf_op jit(solution)/shard_map/ppermute | solution.py:48
  133.7 10.4 %all-to-all-start.3 = ((bf16[4,128,128]{2,1,0:T(8,128)(2,1)}), bf16[4,128,128]{2,1,0:T(8,128)(2,1)}, u32[]{:S(2)}, u32[]{:S(2)}) async-start(bf16[4,128,128]{2,1,0:T(8,128)(2,1)} %get-tuple-element.90), calls=%async_computation.3 | async-start | bytes 262144 | tf_op jit(solution)/shard_map/all_to_all | solution.py:52
  140.5 38.2 %collective-permute-start.39 = (bf16[1536,384]{1,0:T(8,128)(2,1)}, bf16[1536,384]{1,0:T(8,128)(2,1)S(1)}, u32[]{:S(2)}, u32[]{:S(2)}) collective-permute-start(bf16[1536,384]{1,0:T(8,128)(2,1)} %get-tuple-element.115), channel_id=1, source_target_pairs={{0,16},{16,0},{1,17},{17,1},{2,18},{18,2},{3,19},{19,3},{4,20},{20... | collective-permute-start | bytes 3538952 | tf_op jit(solution)/shard_map/ppermute | solution.py:48
  180.5 11.1 %collective-permute-start.41 = (bf16[432,384]{1,0:T(8,128)(2,1)S(1)}, bf16[432,384]{1,0:T(8,128)(2,1)S(1)}, u32[]{:S(2)}, u32[]{:S(2)}) collective-permute-start(bf16[432,384]{1,0:T(8,128)(2,1)S(1)} %get-tuple-element.118), channel_id=1, source_target_pairs={{0,1},{1,0},{2,3},{3,2},{4,5},{5,4},{6,7},{7,6},{8,9},{9,8},{10,11... | collective-permute-start | bytes 995336 | tf_op jit(solution)/shard_map/ppermute | solution.py:48
  180.8 25.5 %collective-permute-start.42 = (bf16[432,384]{1,0:T(8,128)(2,1)S(1)}, bf16[432,384]{1,0:T(8,128)(2,1)S(1)}, u32[]{:S(2)}, u32[]{:S(2)}) collective-permute-start(bf16[432,384]{1,0:T(8,128)(2,1)S(1)} %get-tuple-element.119), channel_id=1, source_target_pairs={{0,2},{1,3},{2,0},{3,1},{4,6},{5,7},{6,4},{7,5},{8,10},{9,11},{10,... | collective-permute-start | bytes 995336 | tf_op jit(solution)/shard_map/ppermute | solution.py:48
  182.6 25.8 %collective-permute-start.43 = (bf16[432,384]{1,0:T(8,128)(2,1)S(1)}, bf16[432,384]{1,0:T(8,128)(2,1)S(1)}, u32[]{:S(2)}, u32[]{:S(2)}) collective-permute-start(bf16[432,384]{1,0:T(8,128)(2,1)S(1)} %get-tuple-element.120), channel_id=1, source_target_pairs={{0,3},{1,2},{2,1},{3,0},{4,7},{5,6},{6,5},{7,4},{8,11},{9,10},{10,... | collective-permute-start | bytes 995336 | tf_op jit(solution)/shard_map/ppermute | solution.py:48
  186.4 29.1 %collective-permute-start.34 = (bf16[384,576]{1,0:T(8,128)(2,1)}, bf16[384,576]{1,0:T(8,128)(2,1)S(1)}, u32[]{:S(2)}, u32[]{:S(2)}) collective-permute-start(bf16[384,576]{1,0:T(8,128)(2,1)} %get-tuple-element.106), channel_id=1, source_target_pairs={{0,16},{16,0},{1,17},{17,1},{2,18},{18,2},{3,19},{19,3},{4,20},{20... | collective-permute-start | bytes 1327112 | tf_op jit(solution)/shard_map/ppermute | solution.py:48
  187.0 22.6 %collective-permute-start.28 = (bf16[64,768]{1,0:T(8,128)(2,1)S(1)}, bf16[64,768]{1,0:T(8,128)(2,1)S(1)}, u32[]{:S(2)}, u32[]{:S(2)}) collective-permute-start(bf16[64,768]{1,0:T(8,128)(2,1)S(1)} %get-tuple-element.100), channel_id=1, source_target_pairs={{0,8},{4,12},{8,0},{12,4},{1,9},{5,13},{9,1},{13,5},{2,10},{6,14},... | collective-permute-start | bytes 294920 | tf_op jit(solution)/shard_map/ppermute | solution.py:48
  191.6 23.9 %collective-permute-start.33 = (f32[6,768]{1,0:T(8,128)S(1)}, f32[6,768]{1,0:T(8,128)S(1)}, u32[]{:S(2)}, u32[]{:S(2)}) collective-permute-start(f32[6,768]{1,0:T(8,128)S(1)} %slice_add_fusion), channel_id=1, source_target_pairs={{0,8},{4,12},{8,0},{12,4},{1,9},{5,13},{9,1},{13,5},{2,10},{6,14},... | collective-permute-start | bytes 55304 | tf_op jit(solution)/shard_map/ppermute | solution.py:48
  208.6 21.7 %collective-permute-start.44 = (bf16[432,384]{1,0:T(8,128)(2,1)S(1)}, bf16[432,384]{1,0:T(8,128)(2,1)S(1)}, u32[]{:S(2)}, u32[]{:S(2)}) collective-permute-start(bf16[432,384]{1,0:T(8,128)(2,1)S(1)} %shard_map.265.part), channel_id=1, source_target_pairs={{0,16},{16,0},{1,17},{17,1},{2,18},{18,2},{3,19},{19,3},{4,20},{20... | collective-permute-start | bytes 995336 | tf_op jit(solution)/shard_map/ppermute | solution.py:48
  212.1 20.7 %all-to-all-start.5 = ((bf16[4,128,192]{1,2,0:T(8,128)(2,1)}), bf16[4,128,192]{1,2,0:T(8,128)(2,1)S(1)}, u32[]{:S(2)}, u32[]{:S(2)}) async-start(bf16[4,128,192]{1,2,0:T(8,128)(2,1)} %copy.37), calls=%async_computation.5 | async-start | bytes 393216 | tf_op jit(solution)/shard_map/all_to_all | solution.py:52
  218.3 11.6 %collective-permute-start.36 = (bf16[96,576]{1,0:T(8,128)(2,1)S(1)}, bf16[96,576]{1,0:T(8,128)(2,1)S(1)}, u32[]{:S(2)}, u32[]{:S(2)}) collective-permute-start(bf16[96,576]{1,0:T(8,128)(2,1)S(1)} %get-tuple-element.109), channel_id=1, source_target_pairs={{0,2},{1,3},{2,0},{3,1},{4,6},{5,7},{6,4},{7,5},{8,10},{9,11},{10,... | collective-permute-start | bytes 331784 | tf_op jit(solution)/shard_map/ppermute | solution.py:48
  (60 other events, 588.0 us)

commit v4 on v3

--- a/solution.py
+++ b/solution.py
@@ -31,7 +31,7 @@
     return lax.dot_general(a, b, (((0,), (0,)), ((), ())), preferred_element_type=f32)
 
 
-def call(kernel, outs, scalars, args, scratch=()):
+def call(kernel, outs, scalars, args, scratch=(), limit=20):
     first = [] if scalars is None else [scalars]
     return pl.pallas_call(
         kernel,
@@ -39,7 +39,8 @@
         in_specs=[SMEM] * len(first) + [VMEM] * len(args),
         out_specs=[VMEM] * len(outs),
         scratch_shapes=[pltpu.VMEM(s, t) for s, t in scratch],
-        compiler_params=pltpu.CompilerParams(vmem_limit_bytes=20 * 1024 * 1024),
+        compiler_params=pltpu.CompilerParams(vmem_limit_bytes=limit * 1024 * 1024),
+        cost_estimate=pl.CostEstimate(flops=1, bytes_accessed=1, transcendentals=0),
     )(*first, *args)
 
 
@@ -76,6 +77,14 @@
     return pieces
 
 
+def gather_col(value):
+    pieces = {0: value}
+    for b in reversed(bits_of("col")):
+        for k in list(pieces):
+            pieces[k ^ b] = swap(pieces[k], "col", b)
+    return [pieces[k] for k in range(lax.axis_size("col"))]
+
+
 def finish_row(keep, send):
     bits = bits_of("row")
     for b in bits[:-1]:
@@ -88,12 +97,8 @@
     return call(halves_kernel, [((rows // 2, width), f32), ((rows // 2, width), bf16)], None, [keep, got])
 
 
-def three_parts(v):
-    high = lax.optimization_barrier(v.astype(bf16))
-    rest = v - high.astype(f32)
-    middle = lax.optimization_barrier(rest.astype(bf16))
-    low = (rest - middle.astype(f32)).astype(bf16)
-    return jnp.concatenate([high, middle, low], axis=0)
+def after(value, *others):
+    return lax.optimization_barrier((value, others))[0]
 
 
 def place(scal, order, col, kk, chunk, n_col, second):
@@ -208,24 +213,61 @@
     send[...] = (keep_ref[half:, :] + got_ref[half:, :].astype(f32)).astype(bf16)
 
 
-def halves_out(value, keep, send):
-    half = value.shape[0] // 2
-    keep[...] = value[:half]
-    send[...] = value[half:].astype(bf16)
+def halves_out(value, keep, send, at=0):
+    half, width = value.shape[0] // 2, value.shape[1]
+    keep[:, at : at + width] = value[:half]
+    send[:, at : at + width] = value[half:].astype(bf16)
+
+
+def message_kernel(own, x, g, *refs):
+    vectors, out = refs[:-1], refs[-1]
+    n_col = out.shape[0]
+    x_all = x[...].astype(f32).T.astype(bf16)
+    g_all = g[...].astype(f32).T.astype(bf16)
+    width = x_all.shape[1]
+    rest = jnp.concatenate([v[...] for v in vectors] + [jnp.zeros((8 - len(vectors), width), f32)], axis=0)
+    parts = []
+    for _ in range(3):
+        part = rest.astype(bf16).astype(f32)
+        parts.append(part)
+        rest = rest - part
+    parts.append(jnp.zeros((8, width), f32))
+    parts = jnp.concatenate(parts, axis=0).astype(bf16)
+    parts = beside(parts, parts.shape[0])
+    half = own // 2
+    for j in range(n_col):
+        out[j, :half, :] = beside(x_all[j * own : (j + 1) * own], own)
+        out[j, half:own, :] = beside(g_all[j * own : (j + 1) * own], own)
+        out[j, own:, :] = parts
+
+
+def prep_kernel(scal, qkv, out, half_a):
+    half, width3 = half_a.shape[0], qkv.shape[1]
+    rows = pl.ds(pl.multiple_of(scal[2] * half, 32), half)
+    half_a[:, :width3] = qkv[rows, :]
+    half_a[:, width3:] = out[rows, :]
+
+
+def prep_mlp_kernel(scal, up, down, half_m):
+    tall, half_ff = up.shape[0], half_m.shape[1]
+    lanes = pl.ds(pl.multiple_of(scal[2] * half_ff, 128), half_ff)
+    half_m[:tall, :] = up[:, lanes]
+    half_m[tall:, :] = down[:, lanes]
 
 
 def token_kernel(got, xg, vec):
     n_col, rows, width = got.shape
-    two = xg.shape[0]
+    width = width // 2
+    own = xg.shape[0] // 2
     for j in range(n_col):
         at = slice(j * width, (j + 1) * width)
-        xg[:, at] = got[j, :two, :]
-        v = got[j, two:, :].astype(f32)
+        xg[:, at] = under(got[j, :own, :], own)
+        v = under(got[j, own:, :].astype(f32), 2 * (rows - own))
         vec[:, at] = v[:8] + v[8:16] + v[16:24]
 
 
 def qkv_kernel(heads, tokens, n_row, n_col, scal, *refs):
-    xgs, (vec, shifts, own_qkv, own_out), refs = refs[:n_row], refs[n_row : n_row + 4], refs[n_row + 4 :]
+    xgs, (vec, qv_bias, own_qkv, own_out), refs = refs[:n_row], refs[n_row : n_row + 4], refs[n_row + 4 :]
     near, far, (cut, a1_out, w_all, w_out) = refs[: n_col - 1], refs[n_col - 1 : 2 * n_col - 2], refs[2 * n_col - 2 :]
     c, d = scal[1], scal[2]
     rows, width3 = own_qkv.shape
@@ -240,8 +282,9 @@
     centred, _ = norm_stats(x.astype(f32))
     a1 = (centred * vec[0:1, :] + vec[1:2, :]).astype(bf16)
     a1_out[...] = a1
-    qkv = (dot_nn(a1, w_all[...]) + shifts[...]).astype(bf16)
     width = heads * HEAD
+    shifts = jnp.concatenate([qv_bias[0:1, :], jnp.zeros((1, width), f32), qv_bias[1:2, :]], axis=1)
+    qkv = (dot_nn(a1, w_all[...]) + shifts).astype(bf16)
     for h in range(n_col):
         if h < heads:
             lo = h * HEAD
@@ -270,7 +313,7 @@
     a2s, gs, refs = refs[:n_row], refs[n_row : 2 * n_row], refs[2 * n_row :]
     up_bias, up_own, down_own = refs[:3]
     near, far = refs[3 : 2 + n_col], refs[2 + n_col : 1 + 2 * n_col]
-    act_out, d_pre_out, bias_sum, a_keep, a_send, y_keep, y_send, wu, wd = refs[1 + 2 * n_col :]
+    act_out, d_pre_out, bias_sum, keep, send, wu, wd = refs[1 + 2 * n_col :]
     c, d = scal[1], scal[2]
     rows, width = up_own.shape
     half = width // 2
@@ -300,28 +343,25 @@
     total = jnp.sum(d_pre.astype(f32), axis=0, keepdims=True)
     bias_sum[:, mine] = total[:, :half]
     bias_sum[:, other] = total[:, half:]
-    halves_out(dot_nt(d_pre, wu[...]), a_keep, a_send)
-    halves_out(dot_nt(act, wd[...]), y_keep, y_send)
-
-
-def mlp_grad_kernel(n_row, n_col, *refs):
+    halves_out(dot_nt(d_pre, wu[...]), keep, send)
+    halves_out(dot_nt(act, wd[...]), keep, send, D)
+
+
+def mlp_grad_kernel(n_row, *refs):
     a2s, gs, refs = refs[:n_row], refs[n_row : 2 * n_row], refs[2 * n_row :]
-    act, d_pre, mine, other = refs
+    act, d_pre, up_mine, up_other, down_mine, down_other = refs
     half = act.shape[1] // 2
     own = a2s[0].shape[0]
     a2, g = stacked(a2s), stacked(gs, slice(own, 2 * own))
-    rows = a2.shape[1] // n_col
-    for value, right, at in ((a2, d_pre, 0), (g, act, rows)):
-        grad = dot_tn(value, right[...]).astype(bf16)
-        for j in range(n_col):
-            to = slice(2 * j * rows + at, 2 * j * rows + at + rows)
-            mine[to, :] = grad[j * rows : (j + 1) * rows, :half]
-            other[to, :] = grad[j * rows : (j + 1) * rows, half:]
+    up_mine[...] = dot_tn(a2, d_pre[:, :half]).astype(bf16)
+    up_other[...] = dot_tn(a2, d_pre[:, half:]).astype(bf16)
+    down_mine[...] = dot_tn(g, act[:, :half]).astype(bf16)
+    down_other[...] = dot_tn(g, act[:, half:]).astype(bf16)
 
 
 def norm2_back_kernel(keep, got, xg, vec, resid_ref, gp_out, d_resid_out, sums):
     own = keep.shape[0]
-    d_a2 = keep[...] + got[...].astype(f32)
+    d_a2 = keep[:, :D] + got[:, :D].astype(f32)
     centred, inverse = norm_stats(resid_ref[...])
     g = xg[own:, :].astype(f32)
     d_resid = g + norm_back(d_a2, centred, inverse, vec[2:3, :])
@@ -354,6 +394,7 @@
 
 def d_a1_kernel(n_row, heads, scal, *refs):
     xgs, (ds, a1, w), refs = refs[:n_row], refs[n_row : n_row + 3], refs[n_row + 3 :]
+    sums2, up_sum, refs = refs[0], refs[1], refs[2:]
     keep, send, sums, mine, other, full = refs
     d = scal[2]
     tokens = a1.shape[0]
@@ -369,35 +410,46 @@
         mine[at, :] = full[pl.ds(pl.multiple_of((2 * j + d) * half, 32), half), :]
         other[at, :] = full[pl.ds(pl.multiple_of((2 * j + 1 - d) * half, 32), half), :]
     centred, _ = norm_stats(stacked(xgs, slice(0, tokens // n_row)).astype(f32))
-    sums[...] = jnp.zeros_like(sums)
-    sums[0:1, :] = jnp.sum(part * centred, axis=0, keepdims=True)
-    sums[1:2, :] = jnp.sum(part, axis=0, keepdims=True)
-    sums[2:3, : d_qkv.shape[1]] = jnp.sum(d_qkv.astype(f32), axis=0, keepdims=True)
-
-
-def final_kernel(a_keep, a_got, y_keep, y_got, xg, vec, resid, d_resid, out):
-    n_col, rows, width = out.shape
+    pad = jnp.zeros((1, D - d_qkv.shape[1]), f32)
+    total = jnp.concatenate(
+        [
+            jnp.sum(part * centred, axis=0, keepdims=True),
+            jnp.sum(part, axis=0, keepdims=True),
+            sums2[...],
+            up_sum[...],
+            jnp.concatenate([jnp.sum(d_qkv.astype(f32), axis=0, keepdims=True), pad], axis=1),
+        ],
+        axis=0,
+    )
+    sums[...] = total
+    other[n_col * half :, :] = pack_sums(total)
+
+
+def final_kernel(d_keep, d_got, a_keep, a_got, xg, vec, resid, d_resid, out):
+    n_col, width, rows = out.shape
     own = rows // 2
-    d_a1 = a_keep[...] + a_got[...].astype(f32)
+    d_a1 = d_keep[...] + d_got[...].astype(f32)
     centred, inverse = norm_stats(xg[:own, :].astype(f32))
     d_x = (d_resid[...] + norm_back(d_a1, centred, inverse, vec[0:1, :])).astype(bf16)
-    y = (resid[...] + (y_keep[...] + y_got[...].astype(f32)) + vec[5:6, :]).astype(bf16)
+    y = (resid[...] + (a_keep[:, D:] + a_got[:, D:].astype(f32)) + vec[5:6, :]).astype(bf16)
+    both = jnp.concatenate([d_x.astype(f32), y.astype(f32)], axis=0)
     for j in range(n_col):
-        out[j, :own, :] = d_x[:, j * width : (j + 1) * width]
-        out[j, own:, :] = y[:, j * width : (j + 1) * width]
-
-
-def part_kernel(n_in, scal, *refs):
-    mine, got, outs = refs[:n_in], refs[n_in : 2 * n_in], refs[2 * n_in :]
-    n_col = len(outs)
-    at = 0
-    for m, g in zip(mine, got):
-        rows = m.shape[0] // n_col
-        for k in range(n_col):
+        out[j] = both[:, j * width : (j + 1) * width].T.astype(bf16)
+
+
+def part_kernel(n_in, order, scal, *refs):
+    mine, got, (keep, send) = refs[:n_in], refs[n_in : 2 * n_in], refs[2 * n_in :]
+    n_col = len(order)
+    height = 2 * keep.shape[0] // n_col
+    for i, k in enumerate(order):
+        to, at = (keep, i) if i < n_col // 2 else (send, i - n_col // 2)
+        at = at * height
+        for m, g in zip(mine, got):
+            rows = m.shape[0] // n_col
             there = pl.ds(pl.multiple_of((scal[1] ^ k) * rows, 16), rows)
             total = m[there, :].astype(f32) + g[there, :].astype(f32)
-            outs[k][at : at + rows, :] = total.astype(outs[k].dtype)
-        at += rows
+            to[at : at + rows, :] = total.astype(to.dtype)
+            at += rows
 
 
 def add_kernel(*refs):
@@ -407,40 +459,145 @@
     refs[-1][...] = total.astype(refs[-1].dtype)
 
 
-def mlp_out_kernel(scal, part, away, up, down, out):
+def pack_sums(v):
+    parts = []
+    for _ in range(3):
+        part = v.astype(bf16).astype(f32)
+        parts.append(part)
+        v = v - part
+    cut = 3 * v.shape[1] // 4
+    rows = [p[:, :cut] for p in parts] + [jnp.concatenate([p[:, cut:] for p in parts], axis=1)]
+    return jnp.concatenate(rows, axis=0).astype(bf16)
+
+
+def unpack_sums(v):
+    v = v.astype(f32)
+    n = v.shape[0] // 4
+    third = v.shape[1] // 3
+    parts = [
+        jnp.concatenate([v[i * n : (i + 1) * n], v[3 * n :, i * third : (i + 1) * third]], axis=1) for i in range(3)
+    ]
+    return parts[0] + parts[1] + parts[2]
+
+
+def qkv_part_kernel(order, scal, mine, got, own_sums, keep, send, sums):
+    n_col = len(order)
+    rows = mine.shape[0] // n_col
+    for i, k in enumerate(order):
+        to, at = (keep, i) if i < n_col // 2 else (send, i - n_col // 2)
+        there = pl.ds(pl.multiple_of((scal[1] ^ k) * rows, 16), rows)
+        total = mine[there, :].astype(f32) + got[there, :].astype(f32)
+        to[at * rows : (at + 1) * rows, :] = total.astype(to.dtype)
+    total = own_sums[...] + unpack_sums(got[mine.shape[0] :, :])
+    sums[...] = total
+    send[keep.shape[0] :, :] = pack_sums(total)
+
+
+def qkv_half_kernel(keep_ref, got_ref, sums_ref, keep, send, sums):
+    rows = keep_ref.shape[0]
+    half = rows // 2
+    keep[...] = keep_ref[:half, :] + got_ref[:half, :].astype(f32)
+    send[:half, :] = (keep_ref[half:, :] + got_ref[half:rows, :].astype(f32)).astype(bf16)
+    total = sums_ref[...] + unpack_sums(got_ref[rows:, :])
+    sums[...] = total
+    send[half:, :] = pack_sums(total)
+
+
+def qkv_add_kernel(keep_ref, got_ref, sums_ref, out, sums):
+    rows = keep_ref.shape[0]
+    out[...] = (keep_ref[...] + got_ref[:rows, :].astype(f32)).astype(bf16)
+    sums[...] = sums_ref[...] + unpack_sums(got_ref[rows:, :])
+
+
+def flat_store(value, cut, out):
+    rows, width = value.shape
+    lines = 2 * width // 128
+    for i in range(cut.shape[0]):
+        high = min(width, (i + 1) * 128)
+        cut[i, :, : high - i * 128] = value[:, i * 128 : high]
+    both = []
+    for odd in range(2):
+        pieces = [cut[i, pl.ds(odd, rows // 2, stride=2), :] for i in range(cut.shape[0])]
+        both.append(jnp.concatenate(pieces, axis=1)[:, :width])
+    both = jnp.concatenate(both, axis=1)
+    for g in range(lines):
+        out[pl.ds(g, rows // 2, stride=lines), :] = both[:, g * 128 : (g + 1) * 128]
+
+
+def up_out_kernel(scal, part, away, up):
+    half = part.shape[1]
+    up[:, pl.ds(pl.multiple_of(scal[2] * half, 128), half)] = part[...].astype(f32)
+    up[:, pl.ds(pl.multiple_of((1 - scal[2]) * half, 128), half)] = away[...].astype(f32)
+
+
+def down_out_kernel(scal, part, away, down, out, full, cut):
     d = scal[2]
-    rows, width = up.shape
+    rows, width = down.shape
     half = width // 2
     for ref, index in ((part, d), (away, 1 - d)):
-        lanes = pl.ds(pl.multiple_of(index * half, 128), half)
-        up[:, lanes] = ref[:rows, :].astype(f32)
-        down[:, lanes] = ref[rows : 2 * rows, :].astype(f32)
-        piece = under(ref[2 * rows :, :].astype(f32), rows // 2)
-        out[pl.ds(pl.multiple_of(index * (rows // 2), 32), rows // 2), :] = piece
-
-
-def qkv_out_kernel(scal, part, away, out):
+        down[:, pl.ds(pl.multiple_of(index * half, 128), half)] = ref[:rows, :].astype(f32)
+        piece = under(ref[rows:, :].astype(f32), rows // 2)
+        full[pl.ds(pl.multiple_of(index * (rows // 2), 32), rows // 2), :] = piece
+    flat_store(full, cut, out)
+
+
+def qkv_out_kernel(scal, part, away, out, full, cut):
     half = part.shape[0]
-    out[pl.ds(pl.multiple_of(scal[2] * half, 32), half), :] = part[...].astype(f32)
-    out[pl.ds(pl.multiple_of((1 - scal[2]) * half, 32), half), :] = away[...].astype(f32)
-
-
-def sum_parts(pairs, scal):
-    n_col = lax.axis_size("col")
-    mine = [m for m, _ in pairs]
-    got = [swap(o, "dp", 1) for _, o in pairs]
-    rows = sum(m.shape[0] for m in mine) // n_col
+    full[pl.ds(pl.multiple_of(scal[2] * half, 32), half), :] = part[...].astype(f32)
+    full[pl.ds(pl.multiple_of((1 - scal[2]) * half, 32), half), :] = away[...].astype(f32)
+    flat_store(full, cut, out)
+
+
+def vector_kernel(scal, sums, feats, *outs):
+    width = outs[0].shape[1]
+    mine = feats[:, :width]
+    for j in range(1, feats.shape[1] // width):
+        mine = jnp.where(scal[1] == j, feats[:, j * width : (j + 1) * width], mine)
+    for i in range(6):
+        outs[i][...] = mine[i : i + 1, :]
+    outs[6][...] = sums[6:7, :]
+    width = outs[7].shape[1]
+    outs[7][0:1, :] = sums[7:8, :width]
+    outs[7][1:2, :] = sums[7:8, 2 * width : 3 * width]
+
+
+def last_kernel(got, first, second):
+    n_col, _, two = got.shape
+    own = two // 2
+    first[...] = jnp.concatenate([got[j, :, :own] for j in range(n_col)], axis=1)
+    second[...] = jnp.concatenate([got[j, :, own:] for j in range(n_col)], axis=1)
+
+
+def col_order():
+    order = [0]
+    for b in reversed(bits_of("col")):
+        order = order + [o ^ b for o in order]
+    return order
+
+
+def join_dp(mine, got, scal):
+    rows = sum(m.shape[0] for m in mine) // 2
     width = mine[0].shape[1]
-    parts = call(
-        functools.partial(part_kernel, len(mine)),
-        [((rows, width), f32)] + [((rows, width), bf16)] * (n_col - 1),
+    return call(
+        functools.partial(part_kernel, len(mine), col_order()),
+        [((rows, width), f32), ((rows, width), bf16)],
         scal,
         [*mine, *got],
     )
-    got = [swap(parts[k], "col", k) for k in range(1, n_col)]
-    total = call(add_kernel, [((rows, width), bf16)], None, [parts[0], *got])[0]
+
+
+def finish_col(keep, send, first=1):
+    bits = bits_of("col", first)
+    for b in bits[:-1]:
+        keep, send = add_halves(keep, swap(send, "col", b))
+    return keep, swap(send, "col", bits[-1])
+
+
+def share_dp(own, got):
+    shape = own.shape
+    total = call(add_kernel, [(shape, bf16)], None, [own, got])[0]
     for b in bits_of("dp", 2):
-        total = call(add_kernel, [((rows, width), bf16)], None, [total, swap(total, "dp", b)])[0]
+        total = call(add_kernel, [(shape, bf16)], None, [total, swap(total, "dp", b)])[0]
     return total, swap(total, "dp", 1)
 
 
@@ -476,34 +633,33 @@
     scal = jnp.stack([lax.axis_index("row").astype(jnp.int32), c, d])
     token_sum = [((tokens // 2, D), f32), ((tokens // 2, D), bf16)]
 
-    zero = jnp.zeros_like(ln1_gain)
-    vectors = three_parts(jnp.stack([ln1_gain, ln1_bias, ln2_gain, ln2_bias, out_bias, down_bias, zero, zero]))
-    message = jnp.concatenate(
+    message = call(
+        functools.partial(message_kernel, own),
+        [((n_col, own + 16, 2 * width_in), bf16)],
+        None,
         [
-            block_input.reshape(n_col, own, width_in),
-            out_grad.reshape(n_col, own, width_in),
-            jnp.broadcast_to(jnp.pad(vectors, ((0, 8), (0, 0)))[None], (n_col, 32, width_in)),
+            block_input.T,
+            out_grad.T,
+            *[v[None] for v in (ln1_gain, ln1_bias, ln2_gain, ln2_bias, out_bias, down_bias)],
         ],
-        axis=1,
-    )
-    got = turn(message.reshape(-1, width_in)).reshape(message.shape)
+    )[0]
+
+    qkv_flat, out_flat = qkv_weight, out_weight
+    own_qkv = qkv_flat.reshape(width_in, 3 * width_out)
+    own_out = out_flat.reshape(width_out, width_in)
+    half_a = call(
+        prep_kernel, [((width_in // 2, 3 * width_out + width_in), bf16)], scal, [own_qkv, own_out]
+    )[0]
+    half_m = call(prep_mlp_kernel, [((2 * width_in, half_ff), bf16)], scal, [up_weight, down_weight])[0]
+    near_a = gather_col(half_a)[1:]
+    far_a = [swap(v, "dp", 1) for v in near_a]
+    half_m = after(half_m, near_a[2])
+    near_m = gather_col(half_m)[1:]
+    far_m = [swap(v, "dp", 1) for v in near_m]
+
+    got = after(turn(message), near_a[0])
     xg_own, vec = call(token_kernel, [((2 * own, D), bf16), ((8, D), f32)], None, [got])
-
-    own_qkv = qkv_weight.reshape(width_in, 3 * width_out)
-    own_out = out_weight.reshape(width_out, width_in)
-    both = jnp.concatenate([own_qkv, own_out], axis=1)
-    half_a = lax.dynamic_slice_in_dim(both, d * (width_in // 2), width_in // 2, 0)
-    near_a = [swap(half_a, "col", k) for k in cols]
-    near_a, up_w, down_w = lax.optimization_barrier((near_a, up_weight, down_weight))
-    far_a = [swap(v, "dp", 1) for v in near_a]
-    half_m = jnp.concatenate(
-        [lax.dynamic_slice_in_dim(w, d * half_ff, half_ff, 1) for w in (up_w, down_w)], axis=0
-    )
-    near_m = [swap(half_m, "col", k) for k in cols]
-    far_m = [swap(v, "dp", 1) for v in near_m]
-
     xg = gather_row(xg_own)
-    shifts = jnp.concatenate([qv_bias[0], jnp.zeros_like(qv_bias[0]), qv_bias[1]])[None]
     qkv_cut, a1, w_qkv, w_out = call(
         functools.partial(qkv_kernel, heads, tokens, n_row, n_col),
         [
@@ -513,9 +669,9 @@
             ((n_col, width_out, width_in), bf16),
         ],
         scal,
-        [*xg, vec, shifts, own_qkv, own_out, *near_a, *far_a],
-    )
-    qkv_head = turn(qkv_cut)
+        [*xg, vec, qv_bias, own_qkv, own_out, *near_a, *far_a],
+    )
+    qkv_head = turn(after(qkv_cut, near_m[:2]))
     att_head = call(
         functools.partial(forward_kernel, order),
         [((n_col, tokens // 2, 2 * HEAD), bf16)],
@@ -527,32 +683,42 @@
         functools.partial(out_kernel, heads, own),
         [((tokens, width_out), bf16)] + token_sum,
         None,
-        [turn(att_head), w_out],
+        [after(turn(after(att_head, near_m[2])), far_m[:2]), w_out],
     )
     resid1, a2_own = call(
-        norm2_kernel, [((own, D), f32), ((own, D), bf16)], None, [*finish_row(o_keep, o_send), xg_own, vec]
+        norm2_kernel, [((own, D), f32), ((own, D), bf16)], None, [*after(finish_row(o_keep, o_send), far_m[2]), xg_own, vec]
     )
     a2 = gather_row(a2_own)
-    act, d_pre, up_sum, a_keep, a_send, y_keep, y_send = call(
+    act, d_pre, up_sum, a_keep, a_send = call(
         functools.partial(mlp_kernel, n_row, n_col),
-        [((tokens, ff), bf16), ((tokens, ff), bf16), ((1, ff), f32)] + token_sum + token_sum,
+        [
+            ((tokens, ff), bf16),
+            ((tokens, ff), bf16),
+            ((1, ff), f32),
+            ((tokens // 2, 2 * D), f32),
+            ((tokens // 2, 2 * D), bf16),
+        ],
         scal,
         [*a2, *xg, up_bias[None], up_weight, down_weight, *near_m, *far_m],
         [((D, ff), bf16), ((D, ff), bf16)],
     )
+    up_mine, up_other, down_mine, down_other = call(
+        functools.partial(mlp_grad_kernel, n_row),
+        [((D, half_ff), bf16)] * 4,
+        None,
+        [*a2, *xg, act, d_pre],
+    )
+    a_keep, a_got = finish_row(a_keep, a_send)
+    a_got = after(a_got, up_other, down_other)
+    up_got = swap(up_other, "dp", 1)
+    down_got = swap(after(down_other, up_got), "dp", 1)
     gp, d_resid1, sums2 = call(
         norm2_back_kernel,
         [((own, D), bf16), ((own, D), f32), ((4, D), f32)],
         None,
-        [*finish_row(a_keep, a_send), xg_own, vec, resid1],
+        [a_keep, a_got, xg_own, vec, resid1],
     )
     gp_all = gather_row(gp)
-    mlp_mine, mlp_other = call(
-        functools.partial(mlp_grad_kernel, n_row, n_col),
-        [((2 * D, half_ff), bf16)] * 2,
-        None,
-        [*a2, *xg, act, d_pre],
-    )
     d_att_cut, out_mine, out_other = call(
         functools.partial(d_att_kernel, n_row, heads),
         [((n_col, tokens // 2, 2 * HEAD), bf16)] + [((n_col * width_out // 4, 2 * width_in), bf16)] * 2,
@@ -560,11 +726,15 @@
         [*gp_all, attended, w_out],
         [((width_out, D), bf16)],
     )
+    out_got = swap(out_other, "dp", 1)
+    up_parts = join_dp([up_mine], [after(up_got, gp_all)], scal)
+    d_att_head = after(turn(d_att_cut), up_parts, down_got)
+    up_total, up_away = share_dp(*finish_col(*up_parts))
     d_qkv_head = call(
         functools.partial(backward_kernel, order),
         [((n_col, tokens // 2, 6 * HEAD), bf16)],
         scal,
-        [qkv_head, turn(d_att_cut)],
+        [qkv_head, d_att_head],
         [
             ((tokens * n_col, 3 * HEAD), bf16),
             ((tokens * n_col, HEAD), bf16),
@@ -573,57 +743,94 @@
             ((HEAD, tokens * n_col), f32),
         ],
     )[0]
+    down_parts = join_dp([down_mine, out_mine], [down_got, out_got], scal)
+    d_qkv_cut = after(turn(after(d_qkv_head, up_total)), down_parts)
     d_keep, d_send, sums1, qkv_mine, qkv_other = call(
         functools.partial(d_a1_kernel, n_row, heads),
-        token_sum + [((3, D), f32)] + [((D // 2, 3 * width_out), bf16)] * 2,
-        scal,
-        [*xg, turn(d_qkv_head), a1, w_qkv],
+        token_sum + [((8, D), f32), ((D // 2, 3 * width_out), bf16), ((D // 2 + 32, 3 * width_out), bf16)],
+        scal,
+        [*xg, d_qkv_cut, a1, w_qkv, sums2, up_sum],
         [((D, 3 * width_out), bf16)],
     )
-
-    d_up, d_down, d_out = call(
-        mlp_out_kernel,
-        [((width_in, ff), f32), ((width_in, ff), f32), ((width_out, width_in), f32)],
-        scal,
-        sum_parts([(mlp_mine, mlp_other), (out_mine, out_other)], scal),
-    )
-    d_qkv = call(qkv_out_kernel, [((width_in, 3 * width_out), f32)], scal, sum_parts([(qkv_mine, qkv_other)], scal))[0]
+    qkv_got = swap(qkv_other, "dp", 1)
 
     outs = call(
         final_kernel,
-        [((n_col, 2 * own, width_in), bf16)],
+        [((n_col, width_in, 2 * own), bf16)],
         None,
-        [*finish_row(d_keep, d_send), *finish_row(y_keep, y_send), xg_own, vec, resid1, d_resid1],
+        [*finish_row(d_keep, d_send), a_keep, a_got, xg_own, vec, resid1, d_resid1],
     )[0]
-    outs = turn(outs)
-    input_grad = outs[:, :own].reshape(-1, width_in)
-    block_output = outs[:, own:].reshape(-1, width_in)
-
-    sums = jnp.concatenate([sums1[:2], sums2, up_sum.reshape(-1, D), sums1[2:]])
-    for axis in ("col", "dp"):
-        for b in bits_of(axis):
-            sums = sums + swap(sums, axis, b)
-    feats = sums[:6]
+    input_grad, block_output = call(last_kernel, [((width_in, tokens), bf16)] * 2, None, [turn(outs)])
+
+    d_up = call(up_out_kernel, [((width_in, ff), f32)], scal, [up_total, up_away])[0]
+    d_down, d_out = call(
+        down_out_kernel,
+        [((width_in, ff), f32), ((width_out * width_in // 128, 128), f32)],
+        scal,
+        share_dp(*finish_col(*down_parts)),
+        [((width_out, width_in), f32), ((pl.cdiv(width_in, 128), width_out, 128), f32)],
+    )
+    rows, width = D // 2, 3 * width_out
+    keep, send, sums = call(
+        functools.partial(qkv_part_kernel, col_order()),
+        [((rows // 2, width), f32), ((rows // 2 + 32, width), bf16), ((8, D), f32)],
+        scal,
+        [qkv_mine, after(qkv_got, outs), sums1],
+    )
+    bits = bits_of("col")
+    for b in bits[:-1]:
+        rows //= 2
+        keep, send, sums = call(
+            qkv_half_kernel,
+            [((rows // 2, width), f32), ((rows // 2 + 32, width), bf16), ((8, D), f32)],
+            None,
+            [keep, swap(send, "col", b), sums],
+        )
+    total, sums = call(
+        qkv_add_kernel,
+        [((rows // 2, width), bf16), ((8, D), f32)],
+        None,
+        [keep, swap(send, "col", bits[-1]), sums],
+    )
+
+    def add(value, axis, bit, kind=f32):
+        return call(add_kernel, [(value.shape, kind)], None, [value, swap(value, axis, bit)])[0]
+
+    for b in bits_of("dp", 2):
+        total, sums = add(total, "dp", b, bf16), add(sums, "dp", b)
+    away = swap(total, "dp", 1)
+    feats = sums
     for b in bits_of("row"):
-        feats = feats + swap(feats, "row", b)
-    feats = lax.dynamic_slice_in_dim(feats, c * width_in, width_in, 1)
-    d_qv_bias = jnp.stack([sums[-1, :width_out], sums[-1, 2 * width_out : 3 * width_out]])
+        feats = add(feats, "row", b)
+    d_qkv = call(
+        qkv_out_kernel,
+        [((width * width_in // 128, 128), f32)],
+        scal,
+        [total, after(away, d_up, d_down, input_grad)],
+        [((width_in, width), f32), ((pl.cdiv(width, 128), width_in, 128), f32)],
+    )[0]
+    vecs = call(
+        vector_kernel,
+        [((1, width_in), f32)] * 6 + [((1, ff), f32), ((2, width_out), f32)],
+        scal,
+        [sums, feats],
+    )
 
     return (
-        block_output,
-        input_grad,
-        feats[0],
-        feats[1],
+        block_output.T,
+        input_grad.T,
+        vecs[0].reshape(-1),
+        vecs[1].reshape(-1),
         d_qkv.reshape(1, 1, -1),
-        d_qv_bias,
+        vecs[7],
         d_out.reshape(1, 1, -1),
-        feats[4],
-        feats[2],
-        feats[3],
+        vecs[4].reshape(-1),
+        vecs[2].reshape(-1),
+        vecs[3].reshape(-1),
         d_up,
-        sums[6:-1].reshape(ff),
+        vecs[6].reshape(-1),
         d_down,
-        feats[5],
+        vecs[5].reshape(-1),
     )
 
 

time: 238 us -> 202 us (0.85)
  waiting for transfers between devices: 104 us -> 76.8 us
  blocking collectives: 14 us -> 0 us
  Pallas kernels: 26.3 us -> 35 us
  local copies, waits for them, and re-layouts: 18.3 us -> 12.9 us
  starting transfers between devices: 69.1 us -> 72.4 us
    all_to_all x5 -> x6, waiting for transfers between devices: 34.3 us -> 15.1 us  [turn(): return lax.all_to_all(value, 'col', split, concat, tiled=True)]
    all_to_all x1 -> x0, blocking collectives: 14 us -> none  [turn(): return lax.all_to_all(value, 'col', split, concat, tiled=True)]
    pallas_call x22 -> x34, Pallas kernels: 26.3 us -> 35 us  [call(): pl.pallas_call(kernel, out_shape=[jax.ShapeDtypeStruct(s, t) for s, t in...]
    ppermute x45 -> x42, waiting for transfers between devices: 70 us -> 61.8 us  [swap(): return lax.ppermute(value, axis, [(i, i ^ bit) for i in range(n)])]
    ppermute x45 -> x42, starting transfers between devices: 45.6 us -> 47.9 us  [swap(): return lax.ppermute(value, axis, [(i, i ^ bit) for i in range(n)])]
    all_to_all x5 -> x6, starting transfers between devices: 23.5 us -> 24.5 us  [turn(): return lax.all_to_all(value, 'col', split, concat, tiled=True)]
  transfers between devices with their start and end apart: 50 -> 48, of which waited for: 25 -> 26; matrix products, arithmetic and copies ran while one was open for 3% -> 1% of each run, Pallas kernels for 6% -> 14%
where the time goes in v4:
time: 202 us; the launch traced here: 201 us
  waiting for transfers between devices  76.8 us (38%)
  starting transfers between devices  72.4 us (36%)
  Pallas kernels  35 us (17%)
  local copies, waits for them, and re-layouts  12.9 us (6%)
  other arithmetic  2.42 us (1%)
    ppermute x42, waiting for transfers between devices, swap(): return lax.ppermute(value, axis, [(i, i ^ bit) for i in range(n)])  61.8 us
    ppermute x42, starting transfers between devices, swap(): return lax.ppermute(value, axis, [(i, i ^ bit) for i in range(n)])  47.9 us
    pallas_call x34, Pallas kernels, call(): pl.pallas_call(kernel, out_shape=[jax.ShapeDtypeStruct(s, t) for s, t in...  35 us
    all_to_all x6, starting transfers between devices, turn(): return lax.all_to_all(value, 'col', split, concat, tiled=True)  24.5 us
    all_to_all x6, waiting for transfers between devices, turn(): return lax.all_to_all(value, 'col', split, concat, tiled=True)  15.1 us
    unnamed x72, local copies, waits for them, and re-layouts  12.5 us
  transfers between devices with their start and end apart: 48, of which 26 were waited for; matrix products, arithmetic and copies ran while one was open for 1% of the time, Pallas kernels for 14%

profile of v4, /device:TPU:0, one launch (start us, length us, event | category | flops | bytes accessed | tf_op | source)
XLA Modules:
  0.0 200.6 jit_solution(16211688739382242773)
XLA Ops:
  4.1 6.4 %all-to-all-start = ((bf16[4,80,384]{2,1,0:T(8,128)(2,1)}), bf16[4,80,384]{2,1,0:T(8,128)(2,1)S(1)}, u32[]{:S(2)}, u32[]{:S(2)}) async-start(bf16[4,80,384]{2,1,0:T(8,128)(2,1)} %shard_map.245), calls=%async_computation | async-start | bytes 491520 | tf_op jit(solution)/shard_map/all_to_all | solution.py:53
  13.4 3.0 %collective-permute-start.4 = (bf16[96,768]{1,0:T(8,128)(2,1)S(1)}, bf16[96,768]{1,0:T(8,128)(2,1)S(1)}, u32[]{:S(2)}, u32[]{:S(2)}) collective-permute-start(bf16[96,768]{1,0:T(8,128)(2,1)S(1)} %shard_map.246), channel_id=1, source_target_pairs={{0,2},{1,3},{2,0},{3,1},{4,6},{5,7},{6,4},{7,5},{8,10},{9,11},{10,... | collective-permute-start | bytes 442376 | tf_op jit(solution)/shard_map/ppermute | solution.py:49
  17.9 7.6 %collective-permute-done.4.refs_9_ = bf16[96,768]{1,0:T(8,128)(2,1)S(1)} collective-permute-done((bf16[96,768]{1,0:T(8,128)(2,1)S(1)}, bf16[96,768]{1,0:T(8,128)(2,1)S(1)}, u32[]{:S(2)}, u32[]{:S(2)}) %collective-permute-start.4) | collective-permute-done | bytes 147488 | tf_op jit(solution)/shard_map/ppermute | solution.py:49
  37.1 3.0 %collective-permute-done.8.refs_13_ = bf16[96,768]{1,0:T(8,128)(2,1)S(1)} collective-permute-done((bf16[96,768]{1,0:T(8,128)(2,1)S(1)}, bf16[96,768]{1,0:T(8,128)(2,1)S(1)}, u32[]{:S(2)}, u32[]{:S(2)}) %collective-permute-start.8) | collective-permute-done | bytes 147488 | tf_op jit(solution)/shard_map/ppermute | solution.py:49
  44.8 3.8 %all-to-all-start.1 = ((bf16[4,128,384]{2,1,0:T(8,128)(2,1)}), bf16[4,128,384]{2,1,0:T(8,128)(2,1)S(1)}, u32[]{:S(2)}, u32[]{:S(2)}) async-start(bf16[4,128,384]{2,1,0:T(8,128)(2,1)} %copy-done.10), calls=%async_computation.1 | async-start | bytes 786432 | tf_op jit(solution)/shard_map/all_to_all | solution.py:53
  52.7 7.0 %all-to-all-done.1.qkv_ref = bf16[4,128,384]{2,1,0:T(8,128)(2,1)S(1)} async-done(((bf16[4,128,384]{2,1,0:T(8,128)(2,1)}), bf16[4,128,384]{2,1,0:T(8,128)(2,1)S(1)}, u32[]{:S(2)}, u32[]{:S(2)}) %all-to-all-start.1) | async-done | bytes 393248 | tf_op jit(solution)/shard_map/all_to_all | solution.py:53
  59.7 3.8 %shard_map.250 = bf16[4,128,128]{2,1,0:T(8,128)(2,1)} custom-call(s32[3]{0:T(128)S(1)} %pad_add_fusion.scal, bf16[4,128,384]{2,1,0:T(8,128)(2,1)S(1)} %all-to-all-done.1.qkv_ref), custom_call_target="tpu_custom_call" | custom-call | flops 1 | bytes 1 | tf_op jit(solution)/shard_map/pallas_call | solution.py:36
  63.6 3.7 %all-to-all-start.2 = ((bf16[4,128,128]{2,1,0:T(8,128)(2,1)}), bf16[4,128,128]{2,1,0:T(8,128)(2,1)S(1)}, u32[]{:S(2)}, u32[]{:S(2)}) async-start(bf16[4,128,128]{2,1,0:T(8,128)(2,1)} %shard_map.250), calls=%async_computation.2 | async-start | bytes 262144 | tf_op jit(solution)/shard_map/all_to_all | solution.py:53
  67.3 5.9 %all-to-all-done.2.o = bf16[4,128,128]{2,1,0:T(8,128)(2,1)S(1)} async-done(((bf16[4,128,128]{2,1,0:T(8,128)(2,1)}), bf16[4,128,128]{2,1,0:T(8,128)(2,1)S(1)}, u32[]{:S(2)}, u32[]{:S(2)}) %all-to-all-start.2) | async-done | bytes 131104 | tf_op jit(solution)/shard_map/all_to_all | solution.py:53
  77.1 6.2 %collective-permute-done.16.refs_16_ = bf16[384,384]{1,0:T(8,128)(2,1)S(1)} collective-permute-done((bf16[384,384]{1,0:T(8,128)(2,1)}, bf16[384,384]{1,0:T(8,128)(2,1)S(1)}, u32[]{:S(2)}, u32[]{:S(2)}) %collective-permute-start.16) | collective-permute-done | bytes 294944 | tf_op jit(solution)/shard_map/ppermute | solution.py:49
  89.5 3.0 %shard_map.254 = (bf16[256,768]{1,0:T(8,128)(2,1)S(1)}, bf16[256,768]{1,0:T(8,128)(2,1)S(1)}, f32[1,768]{1,0:T(1,128)S(1)}, f32[128,1536]{1,0:T(8,128)S(1)}, bf16[128,1536]{1,0:T(8,128)(2,1)S(1)}) custom-call(s32[3]{0:T(128)S(1)} %pad_add_fusion.scal, bf16[64,768]{1,0:T(8,128)(2,1)S(1)} %get-tuple-element.109.refs_0_, ...), custom_call_target="tpu_custom_call" | custom-call | flops 1 | bytes 1 | tf_op jit(solution)/shard_map/pallas_call | solution.py:36
  98.0 5.1 %collective-permute-done.21.got.a_got = bf16[64,1536]{1,0:T(8,128)(2,1)S(1)} collective-permute-done((bf16[64,1536]{1,0:T(8,128)(2,1)S(1)}, bf16[64,1536]{1,0:T(8,128)(2,1)S(1)}, u32[]{:S(2)}, u32[]{:S(2)}) %collective-permute-start.21) | collective-permute-done | bytes 196640 | tf_op jit(solution)/shard_map/ppermute | solution.py:49
  105.2 5.0 %collective-permute-done.25.refs_1_ = bf16[768,384]{1,0:T(8,128)(2,1)S(1)} collective-permute-done((bf16[768,384]{1,0:T(8,128)(2,1)S(1)}, bf16[768,384]{1,0:T(8,128)(2,1)S(1)}, u32[]{:S(2)}, u32[]{:S(2)}) %collective-permute-start.25) | collective-permute-done | bytes 589856 | tf_op jit(solution)/shard_map/ppermute | solution.py:49
  118.1 3.5 %all-to-all-start.3 = ((bf16[4,128,128]{2,1,0:T(8,128)(2,1)}), bf16[4,128,128]{2,1,0:T(8,128)(2,1)S(1)}, u32[]{:S(2)}, u32[]{:S(2)}) async-start(bf16[4,128,128]{2,1,0:T(8,128)(2,1)} %copy-done.19), calls=%async_computation.3 | async-start | bytes 262144 | tf_op jit(solution)/shard_map/all_to_all | solution.py:53
  128.4 6.0 %shard_map.260 = bf16[4,128,384]{2,1,0:T(8,128)(2,1)} custom-call(s32[3]{0:T(128)S(1)} %pad_add_fusion.scal, bf16[4,128,384]{2,1,0:T(8,128)(2,1)S(1)} %all-to-all-done.1.qkv_ref, bf16[4,128,128]{2,1,0:T(8,128)(2,1)S(1)} %all-to-all-done.3.do_ref), custom_call_target="tpu_custom_call" | custom-call | flops 1 | bytes 1 | tf_op jit(solution)/shard_map/pallas_call | solution.py:36
  137.1 3.6 %all-to-all-start.4 = ((bf16[4,128,384]{2,1,0:T(8,128)(2,1)}), bf16[4,128,384]{2,1,0:T(8,128)(2,1)S(1)}, u32[]{:S(2)}, u32[]{:S(2)}) async-start(bf16[4,128,384]{2,1,0:T(8,128)(2,1)} %shard_map.260), calls=%async_computation.4 | async-start | bytes 786432 | tf_op jit(solution)/shard_map/all_to_all | solution.py:53
  141.3 4.6 %collective-permute-done.29.refs_3_ = bf16[192,384]{1,0:T(8,128)(2,1)S(1)} collective-permute-done((bf16[192,384]{1,0:T(8,128)(2,1)S(1)}, bf16[192,384]{1,0:T(8,128)(2,1)S(1)}, u32[]{:S(2)}, u32[]{:S(2)}) %collective-permute-start.29) | collective-permute-done | bytes 147488 | tf_op jit(solution)/shard_map/ppermute | solution.py:49
  158.6 3.1 %collective-permute-done.31.d_got = bf16[64,768]{1,0:T(8,128)(2,1)S(1)} collective-permute-done((bf16[64,768]{1,0:T(8,128)(2,1)S(1)}, bf16[64,768]{1,0:T(8,128)(2,1)S(1)}, u32[]{:S(2)}, u32[]{:S(2)}) %collective-permute-start.31) | collective-permute-done | bytes 98336 | tf_op jit(solution)/shard_map/ppermute | solution.py:49
  162.7 3.7 %collective-permute-done.32.got = bf16[416,576]{1,0:T(8,128)(2,1)S(1)} collective-permute-done((bf16[416,576]{1,0:T(8,128)(2,1)S(1)}, bf16[416,576]{1,0:T(8,128)(2,1)S(1)}, u32[]{:S(2)}, u32[]{:S(2)}) %collective-permute-start.32) | collective-permute-done | bytes 479264 | tf_op jit(solution)/shard_map/ppermute | solution.py:49
  167.5 2.9 %collective-permute-start.40 = (bf16[240,384]{1,0:T(8,128)(2,1)S(1)}, bf16[240,384]{1,0:T(8,128)(2,1)S(1)}, u32[]{:S(2)}, u32[]{:S(2)}) collective-permute-start(bf16[240,384]{1,0:T(8,128)(2,1)S(1)} %get-tuple-element.164), channel_id=1, source_target_pairs={{0,2},{1,3},{2,0},{3,1},{4,6},{5,7},{6,4},{7,5},{8,10},{9,11},{10,... | collective-permute-start | bytes 552968 | tf_op jit(solution)/shard_map/ppermute | solution.py:49
  170.4 3.4 %all-to-all-start.5 = ((bf16[4,192,128]{2,1,0:T(8,128)(2,1)}), bf16[4,192,128]{2,1,0:T(8,128)(2,1)S(1)}, u32[]{:S(2)}, u32[]{:S(2)}) async-start(bf16[4,192,128]{2,1,0:T(8,128)(2,1)} %shard_map.266), calls=%async_computation.5 | async-start | bytes 393216 | tf_op jit(solution)/shard_map/all_to_all | solution.py:53
  173.8 4.6 %collective-permute-done.33.got_ref = bf16[224,576]{1,0:T(8,128)(2,1)S(1)} collective-permute-done((bf16[224,576]{1,0:T(8,128)(2,1)S(1)}, bf16[224,576]{1,0:T(8,128)(2,1)S(1)}, u32[]{:S(2)}, u32[]{:S(2)}) %collective-permute-start.33) | collective-permute-done | bytes 258080 | tf_op jit(solution)/shard_map/ppermute | solution.py:49
  180.1 5.9 %collective-permute-start.41 = (bf16[240,384]{1,0:T(8,128)(2,1)S(1)}, bf16[240,384]{1,0:T(8,128)(2,1)S(1)}, u32[]{:S(2)}, u32[]{:S(2)}) collective-permute-start(bf16[240,384]{1,0:T(8,128)(2,1)S(1)} %shard_map.276.part), channel_id=1, source_target_pairs={{0,16},{16,0},{1,17},{17,1},{2,18},{18,2},{3,19},{19,3},{4,20},{20... | collective-permute-start | bytes 552968 | tf_op jit(solution)/shard_map/ppermute | solution.py:49
  186.1 3.0 %collective-permute-done.34.got_ref = bf16[128,576]{1,0:T(8,128)(2,1)S(1)} collective-permute-done((bf16[128,576]{1,0:T(8,128)(2,1)S(1)}, bf16[128,576]{1,0:T(8,128)(2,1)S(1)}, u32[]{:S(2)}, u32[]{:S(2)}) %collective-permute-start.34) | collective-permute-done | bytes 147488 | tf_op jit(solution)/shard_map/ppermute | solution.py:49
  (185 shorter events, 91.6 us)
Async XLA Ops:
  4.1 21.3 %all-to-all-start = ((bf16[4,80,384]{2,1,0:T(8,128)(2,1)}), bf16[4,80,384]{2,1,0:T(8,128)(2,1)S(1)}, u32[]{:S(2)}, u32[]{:S(2)}) async-start(bf16[4,80,384]{2,1,0:T(8,128)(2,1)} %shard_map.245), calls=%async_computation | async-start | bytes 491520 | tf_op jit(solution)/shard_map/all_to_all | solution.py:53
  13.4 12.0 %collective-permute-start.4 = (bf16[96,768]{1,0:T(8,128)(2,1)S(1)}, bf16[96,768]{1,0:T(8,128)(2,1)S(1)}, u32[]{:S(2)}, u32[]{:S(2)}) collective-permute-start(bf16[96,768]{1,0:T(8,128)(2,1)S(1)} %shard_map.246), channel_id=1, source_target_pairs={{0,2},{1,3},{2,0},{3,1},{4,6},{5,7},{6,4},{7,5},{8,10},{9,11},{10,... | collective-permute-start | bytes 442376 | tf_op jit(solution)/shard_map/ppermute | solution.py:49
  30.6 14.2 %collective-permute-start.10 = (bf16[384,384]{1,0:T(8,128)(2,1)S(1)}, bf16[384,384]{1,0:T(8,128)(2,1)}, u32[]{:S(2)}, u32[]{:S(2)}) collective-permute-start(bf16[384,384]{1,0:T(8,128)(2,1)S(1)} %shard_map.249), channel_id=1, source_target_pairs={{0,2},{1,3},{2,0},{3,1},{4,6},{5,7},{6,4},{7,5},{8,10},{9,11},{10,... | collective-permute-start | bytes 884744 | tf_op jit(solution)/shard_map/ppermute | solution.py:49
  31.9 12.9 %collective-permute-start.9 = (bf16[384,384]{1,0:T(8,128)(2,1)S(1)}, bf16[384,384]{1,0:T(8,128)(2,1)}, u32[]{:S(2)}, u32[]{:S(2)}) collective-permute-start(bf16[384,384]{1,0:T(8,128)(2,1)S(1)} %shard_map.249), channel_id=1, source_target_pairs={{0,1},{1,0},{2,3},{3,2},{4,5},{5,4},{6,7},{7,6},{8,9},{9,8},{10,11... | collective-permute-start | bytes 884744 | tf_op jit(solution)/shard_map/ppermute | solution.py:49
  44.8 14.9 %all-to-all-start.1 = ((bf16[4,128,384]{2,1,0:T(8,128)(2,1)}), bf16[4,128,384]{2,1,0:T(8,128)(2,1)S(1)}, u32[]{:S(2)}, u32[]{:S(2)}) async-start(bf16[4,128,384]{2,1,0:T(8,128)(2,1)} %copy-done.10), calls=%async_computation.1 | async-start | bytes 786432 | tf_op jit(solution)/shard_map/all_to_all | solution.py:53
  48.6 14.9 %collective-permute-start.11 = (bf16[384,384]{1,0:T(8,128)(2,1)}, bf16[384,384]{1,0:T(8,128)(2,1)}, u32[]{:S(2)}, u32[]{:S(2)}) collective-permute-start(bf16[384,384]{1,0:T(8,128)(2,1)} %collective-permute-done.10.refs_12_), channel_id=1, source_target_pairs={{0,1},{1,0},{2,3},{3,2},{4,5},{5,4},{6,7},{7,6},{8,9},{9,8},{10,11... | collective-permute-start | bytes 884744 | tf_op jit(solution)/shard_map/ppermute | solution.py:49
  50.6 16.6 %collective-permute-start.13 = (bf16[384,384]{1,0:T(8,128)(2,1)}, bf16[384,384]{1,0:T(8,128)(2,1)}, u32[]{:S(2)}, u32[]{:S(2)}) collective-permute-start(bf16[384,384]{1,0:T(8,128)(2,1)} %collective-permute-done.10.refs_12_), channel_id=1, source_target_pairs={{0,16},{16,0},{1,17},{17,1},{2,18},{18,2},{3,19},{19,3},{4,20},{20... | collective-permute-start | bytes 884744 | tf_op jit(solution)/shard_map/ppermute | solution.py:49
  52.1 15.2 %collective-permute-start.12 = (bf16[384,384]{1,0:T(8,128)(2,1)}, bf16[384,384]{1,0:T(8,128)(2,1)}, u32[]{:S(2)}, u32[]{:S(2)}) collective-permute-start(bf16[384,384]{1,0:T(8,128)(2,1)} %collective-permute-done.9.refs_11_), channel_id=1, source_target_pairs={{0,16},{16,0},{1,17},{17,1},{2,18},{18,2},{3,19},{19,3},{4,20},{20... | collective-permute-start | bytes 884744 | tf_op jit(solution)/shard_map/ppermute | solution.py:49
  63.6 9.6 %all-to-all-start.2 = ((bf16[4,128,128]{2,1,0:T(8,128)(2,1)}), bf16[4,128,128]{2,1,0:T(8,128)(2,1)S(1)}, u32[]{:S(2)}, u32[]{:S(2)}) async-start(bf16[4,128,128]{2,1,0:T(8,128)(2,1)} %shard_map.250), calls=%async_computation.2 | async-start | bytes 262144 | tf_op jit(solution)/shard_map/all_to_all | solution.py:53
  73.7 9.6 %collective-permute-start.16 = (bf16[384,384]{1,0:T(8,128)(2,1)}, bf16[384,384]{1,0:T(8,128)(2,1)S(1)}, u32[]{:S(2)}, u32[]{:S(2)}) collective-permute-start(bf16[384,384]{1,0:T(8,128)(2,1)} %collective-permute-done.11.refs_13_), channel_id=1, source_target_pairs={{0,16},{16,0},{1,17},{17,1},{2,18},{18,2},{3,19},{19,3},{4,20},{20... | collective-permute-start | bytes 884744 | tf_op jit(solution)/shard_map/ppermute | solution.py:49
  94.5 15.6 %collective-permute-start.25 = (bf16[768,384]{1,0:T(8,128)(2,1)S(1)}, bf16[768,384]{1,0:T(8,128)(2,1)S(1)}, u32[]{:S(2)}, u32[]{:S(2)}) collective-permute-start(bf16[768,384]{1,0:T(8,128)(2,1)S(1)} %get-tuple-element.116), channel_id=1, source_target_pairs={{0,16},{16,0},{1,17},{17,1},{2,18},{18,2},{3,19},{19,3},{4,20},{20... | collective-permute-start | bytes 1769480 | tf_op jit(solution)/shard_map/ppermute | solution.py:49
  110.1 18.2 %collective-permute-start.26 = (bf16[768,384]{1,0:T(8,128)(2,1)}, bf16[768,384]{1,0:T(8,128)(2,1)}, u32[]{:S(2)}, u32[]{:S(2)}) collective-permute-start(bf16[768,384]{1,0:T(8,128)(2,1)} %get-tuple-element.127), channel_id=1, source_target_pairs={{0,16},{16,0},{1,17},{17,1},{2,18},{18,2},{3,19},{19,3},{4,20},{20... | collective-permute-start | bytes 1769480 | tf_op jit(solution)/shard_map/ppermute | solution.py:49
  114.4 9.6 %collective-permute-start.27 = (bf16[384,384]{1,0:T(8,128)(2,1)}, bf16[384,384]{1,0:T(8,128)(2,1)}, u32[]{:S(2)}, u32[]{:S(2)}) collective-permute-start(bf16[384,384]{1,0:T(8,128)(2,1)} %get-tuple-element.126), channel_id=1, source_target_pairs={{0,1},{1,0},{2,3},{3,2},{4,5},{5,4},{6,7},{7,6},{8,9},{9,8},{10,11... | collective-permute-start | bytes 884744 | tf_op jit(solution)/shard_map/ppermute | solution.py:49
  118.1 10.2 %all-to-all-start.3 = ((bf16[4,128,128]{2,1,0:T(8,128)(2,1)}), bf16[4,128,128]{2,1,0:T(8,128)(2,1)S(1)}, u32[]{:S(2)}, u32[]{:S(2)}) async-start(bf16[4,128,128]{2,1,0:T(8,128)(2,1)} %copy-done.19), calls=%async_computation.3 | async-start | bytes 262144 | tf_op jit(solution)/shard_map/all_to_all | solution.py:53
  127.4 9.6 %collective-permute-start.28 = (bf16[192,384]{1,0:T(8,128)(2,1)}, bf16[192,384]{1,0:T(8,128)(2,1)S(1)}, u32[]{:S(2)}, u32[]{:S(2)}) collective-permute-start(bf16[192,384]{1,0:T(8,128)(2,1)} %get-tuple-element.130), channel_id=1, source_target_pairs={{0,2},{1,3},{2,0},{3,1},{4,6},{5,7},{6,4},{7,5},{8,10},{9,11},{10,... | collective-permute-start | bytes 442376 | tf_op jit(solution)/shard_map/ppermute | solution.py:49
  137.1 15.0 %all-to-all-start.4 = ((bf16[4,128,384]{2,1,0:T(8,128)(2,1)}), bf16[4,128,384]{2,1,0:T(8,128)(2,1)S(1)}, u32[]{:S(2)}, u32[]{:S(2)}) async-start(bf16[4,128,384]{2,1,0:T(8,128)(2,1)} %shard_map.260), calls=%async_computation.4 | async-start | bytes 786432 | tf_op jit(solution)/shard_map/all_to_all | solution.py:53
  154.6 11.8 %collective-permute-start.32 = (bf16[416,576]{1,0:T(8,128)(2,1)S(1)}, bf16[416,576]{1,0:T(8,128)(2,1)S(1)}, u32[]{:S(2)}, u32[]{:S(2)}) collective-permute-start(bf16[416,576]{1,0:T(8,128)(2,1)S(1)} %get-tuple-element.150), channel_id=1, source_target_pairs={{0,16},{16,0},{1,17},{17,1},{2,18},{18,2},{3,19},{19,3},{4,20},{20... | collective-permute-start | bytes 1437704 | tf_op jit(solution)/shard_map/ppermute | solution.py:49
  155.2 12.2 %collective-permute-start.39 = (bf16[480,384]{1,0:T(8,128)(2,1)S(1)}, bf16[480,384]{1,0:T(8,128)(2,1)S(1)}, u32[]{:S(2)}, u32[]{:S(2)}) collective-permute-start(bf16[480,384]{1,0:T(8,128)(2,1)S(1)} %copy-done.30), channel_id=1, source_target_pairs={{0,1},{1,0},{2,3},{3,2},{4,5},{5,4},{6,7},{7,6},{8,9},{9,8},{10,11... | collective-permute-start | bytes 1105928 | tf_op jit(solution)/shard_map/ppermute | solution.py:49
  167.2 11.2 %collective-permute-start.33 = (bf16[224,576]{1,0:T(8,128)(2,1)S(1)}, bf16[224,576]{1,0:T(8,128)(2,1)S(1)}, u32[]{:S(2)}, u32[]{:S(2)}) collective-permute-start(bf16[224,576]{1,0:T(8,128)(2,1)S(1)} %get-tuple-element.154), channel_id=1, source_target_pairs={{0,1},{1,0},{2,3},{3,2},{4,5},{5,4},{6,7},{7,6},{8,9},{9,8},{10,11... | collective-permute-start | bytes 774152 | tf_op jit(solution)/shard_map/ppermute | solution.py:49
  167.5 12.5 %collective-permute-start.40 = (bf16[240,384]{1,0:T(8,128)(2,1)S(1)}, bf16[240,384]{1,0:T(8,128)(2,1)S(1)}, u32[]{:S(2)}, u32[]{:S(2)}) collective-permute-start(bf16[240,384]{1,0:T(8,128)(2,1)S(1)} %get-tuple-element.164), channel_id=1, source_target_pairs={{0,2},{1,3},{2,0},{3,1},{4,6},{5,7},{6,4},{7,5},{8,10},{9,11},{10,... | collective-permute-start | bytes 552968 | tf_op jit(solution)/shard_map/ppermute | solution.py:49
  170.4 25.8 %all-to-all-start.5 = ((bf16[4,192,128]{2,1,0:T(8,128)(2,1)}), bf16[4,192,128]{2,1,0:T(8,128)(2,1)S(1)}, u32[]{:S(2)}, u32[]{:S(2)}) async-start(bf16[4,192,128]{2,1,0:T(8,128)(2,1)} %shard_map.266), calls=%async_computation.5 | async-start | bytes 393216 | tf_op jit(solution)/shard_map/all_to_all | solution.py:53
  178.5 10.6 %collective-permute-start.34 = (bf16[128,576]{1,0:T(8,128)(2,1)S(1)}, bf16[128,576]{1,0:T(8,128)(2,1)S(1)}, u32[]{:S(2)}, u32[]{:S(2)}) collective-permute-start(bf16[128,576]{1,0:T(8,128)(2,1)S(1)} %get-tuple-element.157), channel_id=1, source_target_pairs={{0,2},{1,3},{2,0},{3,1},{4,6},{5,7},{6,4},{7,5},{8,10},{9,11},{10,... | collective-permute-start | bytes 442376 | tf_op jit(solution)/shard_map/ppermute | solution.py:49
  180.1 14.6 %collective-permute-start.41 = (bf16[240,384]{1,0:T(8,128)(2,1)S(1)}, bf16[240,384]{1,0:T(8,128)(2,1)S(1)}, u32[]{:S(2)}, u32[]{:S(2)}) collective-permute-start(bf16[240,384]{1,0:T(8,128)(2,1)S(1)} %shard_map.276.part), channel_id=1, source_target_pairs={{0,16},{16,0},{1,17},{17,1},{2,18},{18,2},{3,19},{19,3},{4,20},{20... | collective-permute-start | bytes 552968 | tf_op jit(solution)/shard_map/ppermute | solution.py:49
  189.2 9.9 %collective-permute-start.37 = (bf16[96,576]{1,0:T(8,128)(2,1)S(1)}, bf16[96,576]{1,0:T(8,128)(2,1)S(1)}, u32[]{:S(2)}, u32[]{:S(2)}) collective-permute-start(bf16[96,576]{1,0:T(8,128)(2,1)S(1)} %get-tuple-element.162.part), channel_id=1, source_target_pairs={{0,16},{16,0},{1,17},{17,1},{2,18},{18,2},{3,19},{19,3},{4,20},{20... | collective-permute-start | bytes 331784 | tf_op jit(solution)/shard_map/ppermute | solution.py:49
  (60 other events, 241.2 us)

commit v5 on v4

--- a/solution.py
+++ b/solution.py
@@ -31,7 +31,7 @@
     return lax.dot_general(a, b, (((0,), (0,)), ((), ())), preferred_element_type=f32)
 
 
-def call(kernel, outs, scalars, args, scratch=(), limit=20):
+def call(kernel, outs, scalars, args, scratch=(), limit=20, cost=0):
     first = [] if scalars is None else [scalars]
     return pl.pallas_call(
         kernel,
@@ -40,7 +40,7 @@
         out_specs=[VMEM] * len(outs),
         scratch_shapes=[pltpu.VMEM(s, t) for s, t in scratch],
         compiler_params=pltpu.CompilerParams(vmem_limit_bytes=limit * 1024 * 1024),
-        cost_estimate=pl.CostEstimate(flops=1, bytes_accessed=1, transcendentals=0),
+        cost_estimate=pl.CostEstimate(flops=1, bytes_accessed=1 + 3_000_000 * cost, transcendentals=0),
     )(*first, *args)
 
 
@@ -101,32 +101,6 @@
     return lax.optimization_barrier((value, others))[0]
 
 
-def place(scal, order, col, kk, chunk, n_col, second):
-    half = chunk // 2
-    at = ((scal[0] ^ order[kk]) * n_col + col) * chunk + second * half
-    return pl.ds(pl.multiple_of(at, half), half)
-
-
-def load_natural(scal, order, src, dst):
-    n_col, rows, width = src.shape
-    half = rows // len(order)
-    for col in range(n_col):
-        for kk in range(len(order)):
-            both = src[col, kk * half : (kk + 1) * half, :]
-            for second in range(2):
-                at = place(scal, order, col, kk, 2 * half, n_col, second)
-                dst[at, :] = both[:, second * (width // 2) : (second + 1) * (width // 2)]
-
-
-def store_natural(scal, order, src, dst):
-    n_col, rows, _ = dst.shape
-    half = rows // len(order)
-    for col in range(n_col):
-        for kk in range(len(order)):
-            both = [src[place(scal, order, col, kk, 2 * half, n_col, second), :] for second in range(2)]
-            dst[col, kk * half : (kk + 1) * half, :] = jnp.concatenate(both, axis=1)
-
-
 def beside(value, chunk):
     half = chunk // 2
     starts = range(0, value.shape[0], chunk)
@@ -144,49 +118,99 @@
     return jnp.concatenate(parts, axis=0)
 
 
-def block_probs(q, k, block, i):
-    scores = dot_nt(q, k) * SCALE
-    rows = lax.broadcasted_iota(jnp.int32, scores.shape, 0) + i * block
-    cols = lax.broadcasted_iota(jnp.int32, scores.shape, 1)
-    scores = jnp.where(cols <= rows, scores, -1e30)
+def place(scal, order, k, kk, chunk, n_col):
+    at = ((scal[0] ^ order[kk]) * n_col + (scal[1] ^ k)) * chunk
+    return pl.ds(pl.multiple_of(at, chunk), chunk)
+
+
+def load_natural(scal, order, pieces, dst):
+    chunk = pieces[0].shape[0] // len(order)
+    for k, piece in enumerate(pieces):
+        for kk in range(len(order)):
+            dst[place(scal, order, k, kk, chunk, len(pieces)), :] = piece[kk * chunk : (kk + 1) * chunk, :]
+
+
+def chunk_of(scal, order, quarter, chunk):
+    want = quarter ^ scal[0]
+    index = jnp.int32(0)
+    for i, o in enumerate(order):
+        index = jnp.where(want == o, i, index)
+    return pl.ds(pl.multiple_of(index * chunk, chunk), chunk)
+
+
+def row_exps(q, k, low, first):
+    scores = dot_nt(q, k)
+    tail = scores[:, low:]
+    rows = lax.broadcasted_iota(jnp.int32, tail.shape, 0) + first
+    cols = lax.broadcasted_iota(jnp.int32, tail.shape, 1)
+    tail = jnp.where(cols <= rows, tail, -1e30)
+    scores = tail if low == 0 else jnp.concatenate([scores[:, :low], tail], axis=1)
     top = jnp.max(scores, axis=-1, keepdims=True)
-    e = jnp.exp(scores - top)
-    return e / jnp.sum(e, axis=-1, keepdims=True)
-
-
-def forward_kernel(order, scal, qkv_ref, out_ref, nat, res):
-    load_natural(scal, order, qkv_ref, nat)
-    block = nat.shape[0] // len(order)
-    k = nat[:, HEAD : 2 * HEAD]
-    v = nat[:, 2 * HEAD :]
-    for i in range(len(order)):
-        upto = (i + 1) * block
-        p = block_probs(nat[i * block : upto, :HEAD], k[:upto], block, i)
-        res[i * block : upto, :] = dot_nn(p.astype(bf16), v[:upto]).astype(bf16)
-    store_natural(scal, order, res, out_ref)
-
-
-def backward_kernel(order, scal, qkv_ref, do_ref, out_ref, nat, dnat, res, dkt, dvt):
-    load_natural(scal, order, qkv_ref, nat)
-    load_natural(scal, order, do_ref, dnat)
-    block = nat.shape[0] // len(order)
-    k = nat[:, HEAD : 2 * HEAD]
-    v = nat[:, 2 * HEAD :]
-    dkt[...] = jnp.zeros_like(dkt)
-    dvt[...] = jnp.zeros_like(dvt)
-    for i in range(len(order)):
-        upto = (i + 1) * block
-        q = nat[i * block : upto, :HEAD]
-        do = dnat[i * block : upto, :]
-        p = block_probs(q, k[:upto], block, i)
-        dvt[:, :upto] += dot_tn(do, p.astype(bf16))
-        dp = dot_nt(do, v[:upto])
-        ds = (p * (dp - jnp.sum(dp * p, axis=-1, keepdims=True))).astype(bf16)
-        res[i * block : upto, :HEAD] = (dot_nn(ds, k[:upto]) * SCALE).astype(bf16)
-        dkt[:, :upto] += dot_tn(q, ds)
-    res[:, HEAD : 2 * HEAD] = (dkt[...].T * SCALE).astype(bf16)
-    res[:, 2 * HEAD :] = dvt[...].T.astype(bf16)
-    store_natural(scal, order, res, out_ref)
+    e = jnp.exp2((scores - top) * (SCALE * math.log2(math.e)))
+    return e, jnp.sum(e, axis=-1, keepdims=True)
+
+
+def attention_kernel(order, n_col, heads, scal, q_ref, *refs):
+    pieces, (w, att_out, keep, send, nat) = refs[:n_col], refs[n_col:]
+    load_natural(scal, order, pieces, nat)
+    n_row = len(order)
+    chunk = q_ref.shape[0] // n_row
+    block = chunk * n_col
+    width = heads * HEAD
+    first = scal[1] * chunk
+    parts = [[] for _ in range(n_row)]
+    for h in range(heads):
+        k = nat[:, h * HEAD : (h + 1) * HEAD]
+        v = nat[:, width + h * HEAD : width + (h + 1) * HEAD]
+        for i in range(n_row):
+            upto = (i + 1) * block
+            q = q_ref[chunk_of(scal, order, i, chunk), :][:, h * HEAD : (h + 1) * HEAD]
+            e, total = row_exps(q, k[:upto], i * block, first)
+            parts[i].append((dot_nn(e.astype(bf16), v[:upto]) / total).astype(bf16))
+    for i in range(n_row):
+        att_out[chunk_of(scal, order, i, chunk), :] = jnp.concatenate(parts[i], axis=1)
+    w_all = jnp.concatenate([w[j] for j in range(n_col)], axis=1)
+    halves_out(dot_nn(att_out[...], w_all), keep, send)
+
+
+def attention_back_kernel(order, col_order, heads, scal, q_ref, *refs):
+    n_col = len(col_order)
+    pieces, (do_ref, dq, keep, send, nat, grads_t, grads) = refs[:n_col], refs[n_col:]
+    load_natural(scal, order, pieces, nat)
+    n_row = len(order)
+    chunk = q_ref.shape[0] // n_row
+    block = chunk * n_col
+    width = heads * HEAD
+    first = scal[1] * chunk
+    grads_t[...] = jnp.zeros_like(grads_t)
+    parts = [[] for _ in range(n_row)]
+    for h in range(heads):
+        here = slice(h * HEAD, (h + 1) * HEAD)
+        there = slice(width + h * HEAD, width + (h + 1) * HEAD)
+        k = nat[:, here]
+        v = nat[:, there]
+        for i in range(n_row):
+            upto = (i + 1) * block
+            at = chunk_of(scal, order, i, chunk)
+            q = q_ref[at, :][:, here]
+            do = do_ref[at, :][:, here]
+            e, total = row_exps(q, k[:upto], i * block, first)
+            p = e * (1.0 / total)
+            grads_t[there, :upto] += dot_tn(do, p.astype(bf16))
+            dp = dot_nt(do, v[:upto])
+            ds = (p * (dp - jnp.sum(dp * p, axis=-1, keepdims=True))).astype(bf16)
+            parts[i].append((dot_nn(ds, k[:upto]) * SCALE).astype(bf16))
+            grads_t[here, :upto] += dot_tn(q, ds)
+    for i in range(n_row):
+        dq[chunk_of(scal, order, i, chunk), :] = jnp.concatenate(parts[i], axis=1)
+    grads[:, :width] = grads_t[:width, :].T * SCALE
+    grads[:, width:] = grads_t[width:, :].T
+    rows = n_row * chunk
+    for i, k in enumerate(col_order):
+        to, base = (keep, i) if i < n_col // 2 else (send, i - n_col // 2)
+        for kk in range(n_row):
+            at = base * rows + kk * chunk
+            to[at : at + chunk, :] = grads[place(scal, order, k, kk, chunk, n_col), :].astype(to.dtype)
 
 
 def norm_stats(v):
@@ -219,9 +243,8 @@
     send[:, at : at + width] = value[half:].astype(bf16)
 
 
-def message_kernel(own, x, g, *refs):
-    vectors, out = refs[:-1], refs[-1]
-    n_col = out.shape[0]
+def message_kernel(own, n_col, scal, x, g, *refs):
+    vectors, outs, cut = refs[: -n_col - 1], refs[-n_col - 1 : -1], refs[-1]
     x_all = x[...].astype(f32).T.astype(bf16)
     g_all = g[...].astype(f32).T.astype(bf16)
     width = x_all.shape[1]
@@ -236,9 +259,11 @@
     parts = beside(parts, parts.shape[0])
     half = own // 2
     for j in range(n_col):
-        out[j, :half, :] = beside(x_all[j * own : (j + 1) * own], own)
-        out[j, half:own, :] = beside(g_all[j * own : (j + 1) * own], own)
-        out[j, own:, :] = parts
+        cut[j, :half, :] = beside(x_all[j * own : (j + 1) * own], own)
+        cut[j, half:own, :] = beside(g_all[j * own : (j + 1) * own], own)
+    for k in range(n_col):
+        outs[k][:own, :] = cut[scal[1] ^ k]
+        outs[k][own:, :] = parts
 
 
 def prep_kernel(scal, qkv, out, half_a):
@@ -255,9 +280,12 @@
     half_m[tall:, :] = down[:, lanes]
 
 
-def token_kernel(got, xg, vec):
+def token_kernel(scal, *refs):
+    pieces, (xg, vec, got) = refs[:-3], refs[-3:]
     n_col, rows, width = got.shape
     width = width // 2
+    for k in range(n_col):
+        got[scal[1] ^ k] = pieces[k][...]
     own = xg.shape[0] // 2
     for j in range(n_col):
         at = slice(j * width, (j + 1) * width)
@@ -268,7 +296,7 @@
 
 def qkv_kernel(heads, tokens, n_row, n_col, scal, *refs):
     xgs, (vec, qv_bias, own_qkv, own_out), refs = refs[:n_row], refs[n_row : n_row + 4], refs[n_row + 4 :]
-    near, far, (cut, a1_out, w_all, w_out) = refs[: n_col - 1], refs[n_col - 1 : 2 * n_col - 2], refs[2 * n_col - 2 :]
+    near, far, (q_out, kv_out, a1_out, w_all, w_out) = refs[: n_col - 1], refs[n_col - 1 : 2 * n_col - 2], refs[2 * n_col - 2 :]
     c, d = scal[1], scal[2]
     rows, width3 = own_qkv.shape
     half = rows // 2
@@ -285,20 +313,8 @@
     width = heads * HEAD
     shifts = jnp.concatenate([qv_bias[0:1, :], jnp.zeros((1, width), f32), qv_bias[1:2, :]], axis=1)
     qkv = (dot_nn(a1, w_all[...]) + shifts).astype(bf16)
-    for h in range(n_col):
-        if h < heads:
-            lo = h * HEAD
-            piece = jnp.concatenate([qkv[:, j * width + lo : j * width + lo + HEAD] for j in range(3)], axis=1)
-            cut[h] = beside(piece, tokens // n_row)
-        else:
-            cut[h] = jnp.zeros((tokens // 2, 6 * HEAD), bf16)
-
-
-def out_kernel(heads, chunk, o, w, att_out, keep, send):
-    att = jnp.concatenate([under(o[h], chunk) for h in range(heads)], axis=1)
-    att_out[...] = att
-    w_all = jnp.concatenate([w[j] for j in range(w.shape[0])], axis=1)
-    halves_out(dot_nn(att, w_all), keep, send)
+    q_out[...] = qkv[:, :width]
+    kv_out[...] = qkv[:, width:]
 
 
 def norm2_kernel(keep, got, xg, vec, resid_out, a2_out):
@@ -373,17 +389,13 @@
 
 
 def d_att_kernel(n_row, heads, scal, *refs):
-    gps, (att, w, cut, mine, other, full) = refs[:n_row], refs[n_row:]
+    gps, (att, w, d_att_out, mine, other, full) = refs[:n_row], refs[n_row:]
     d = scal[2]
     gp = stacked(gps)
     n_col, rows, width = w.shape
     w_all = jnp.concatenate([w[j] for j in range(n_col)], axis=1)
     d_att = dot_nt(gp, w_all).astype(bf16)
-    for h in range(n_col):
-        if h < heads:
-            cut[h] = beside(d_att[:, h * HEAD : (h + 1) * HEAD], gps[0].shape[0])
-        else:
-            cut[h] = jnp.zeros((gp.shape[0] // 2, 2 * HEAD), bf16)
+    d_att_out[...] = d_att
     full[...] = dot_tn(att[...], gp).astype(bf16)
     half = rows // 2
     for to, part in ((mine, d), (other, 1 - d)):
@@ -392,18 +404,19 @@
             to[j * (half // 2) : (j + 1) * (half // 2), :] = beside(piece[:, j * width : (j + 1) * width], half)
 
 
-def d_a1_kernel(n_row, heads, scal, *refs):
-    xgs, (ds, a1, w), refs = refs[:n_row], refs[n_row : n_row + 3], refs[n_row + 3 :]
+def d_a1_kernel(n_row, n_col, scal, *refs):
+    xgs, (dq, dkv_keep, dkv_got, a1, w), refs = refs[:n_row], refs[n_row : n_row + 5], refs[n_row + 5 :]
     sums2, up_sum, refs = refs[0], refs[1], refs[2:]
     keep, send, sums, mine, other, full = refs
     d = scal[2]
     tokens = a1.shape[0]
-    pieces = [under(ds[h], tokens // n_row) for h in range(heads)]
-    d_qkv = jnp.concatenate([p[:, j * HEAD : (j + 1) * HEAD] for j in range(3) for p in pieces], axis=1)
+    d_kv = (dkv_keep[...] + dkv_got[...].astype(f32)).astype(bf16)
+    d_qkv = jnp.concatenate([dq[...], d_kv], axis=1)
     part = dot_nt(d_qkv, w[...])
-    halves_out(part, keep, send)
+    half = tokens // 2
+    keep[...] = part[:half]
+    send[:half, :] = part[half:].astype(bf16)
     full[...] = dot_tn(a1[...], d_qkv).astype(bf16)
-    n_col = ds.shape[0]
     half = full.shape[0] // (2 * n_col)
     for j in range(n_col):
         at = slice(j * half, (j + 1) * half)
@@ -422,13 +435,14 @@
         axis=0,
     )
     sums[...] = total
-    other[n_col * half :, :] = pack_sums(total)
-
-
-def final_kernel(d_keep, d_got, a_keep, a_got, xg, vec, resid, d_resid, out):
+    send[tokens // 2 :, :] = pack_wide(total)
+
+
+def final_kernel(d_keep, d_got, sums_ref, a_keep, a_got, xg, vec, resid, d_resid, out, sums):
     n_col, width, rows = out.shape
     own = rows // 2
-    d_a1 = d_keep[...] + d_got[...].astype(f32)
+    d_a1 = d_keep[...] + d_got[:own, :].astype(f32)
+    sums[...] = add_row_sums(sums_ref[...], unpack_wide(d_got[own:, :]))
     centred, inverse = norm_stats(xg[:own, :].astype(f32))
     d_x = (d_resid[...] + norm_back(d_a1, centred, inverse, vec[0:1, :])).astype(bf16)
     y = (resid[...] + (a_keep[:, D:] + a_got[:, D:].astype(f32)) + vec[5:6, :]).astype(bf16)
@@ -459,12 +473,27 @@
     refs[-1][...] = total.astype(refs[-1].dtype)
 
 
-def pack_sums(v):
+def three_parts(v):
     parts = []
     for _ in range(3):
         part = v.astype(bf16).astype(f32)
         parts.append(part)
         v = v - part
+    return parts
+
+
+def pack_wide(v):
+    return jnp.concatenate(three_parts(v) + [jnp.zeros_like(v)], axis=0).astype(bf16)
+
+
+def unpack_wide(v):
+    v = v.astype(f32)
+    n = v.shape[0] // 4
+    return v[:n] + v[n : 2 * n] + v[2 * n : 3 * n]
+
+
+def pack_sums(v):
+    parts = three_parts(v)
     cut = 3 * v.shape[1] // 4
     rows = [p[:, :cut] for p in parts] + [jnp.concatenate([p[:, cut:] for p in parts], axis=1)]
     return jnp.concatenate(rows, axis=0).astype(bf16)
@@ -480,7 +509,21 @@
     return parts[0] + parts[1] + parts[2]
 
 
-def qkv_part_kernel(order, scal, mine, got, own_sums, keep, send, sums):
+def add_row_sums(own, got):
+    return jnp.concatenate([own[:6] + got[:6], own[6:]], axis=0)
+
+
+def d_half_kernel(keep_ref, got_ref, sums_ref, keep, send, sums):
+    rows = keep_ref.shape[0]
+    half = rows // 2
+    keep[...] = keep_ref[:half, :] + got_ref[:half, :].astype(f32)
+    send[:half, :] = (keep_ref[half:, :] + got_ref[half:rows, :].astype(f32)).astype(bf16)
+    total = add_row_sums(sums_ref[...], unpack_wide(got_ref[rows:, :]))
+    sums[...] = total
+    send[half:, :] = pack_wide(total)
+
+
+def qkv_part_kernel(order, scal, mine, got, own_sums, keep, send):
     n_col = len(order)
     rows = mine.shape[0] // n_col
     for i, k in enumerate(order):
@@ -488,9 +531,7 @@
         there = pl.ds(pl.multiple_of((scal[1] ^ k) * rows, 16), rows)
         total = mine[there, :].astype(f32) + got[there, :].astype(f32)
         to[at * rows : (at + 1) * rows, :] = total.astype(to.dtype)
-    total = own_sums[...] + unpack_sums(got[mine.shape[0] :, :])
-    sums[...] = total
-    send[keep.shape[0] :, :] = pack_sums(total)
+    send[keep.shape[0] :, :] = pack_sums(own_sums[...])
 
 
 def qkv_half_kernel(keep_ref, got_ref, sums_ref, keep, send, sums):
@@ -504,9 +545,11 @@
 
 
 def qkv_add_kernel(keep_ref, got_ref, sums_ref, out, sums):
-    rows = keep_ref.shape[0]
-    out[...] = (keep_ref[...] + got_ref[:rows, :].astype(f32)).astype(bf16)
-    sums[...] = sums_ref[...] + unpack_sums(got_ref[rows:, :])
+    rows = out.shape[0] - 32
+    out[:rows, :] = (keep_ref[:rows, :].astype(f32) + got_ref[:rows, :].astype(f32)).astype(bf16)
+    total = sums_ref[...] + unpack_sums(got_ref[rows:, :])
+    sums[...] = total
+    out[rows:, :] = pack_sums(total)
 
 
 def flat_store(value, cut, out):
@@ -541,18 +584,17 @@
     flat_store(full, cut, out)
 
 
-def qkv_out_kernel(scal, part, away, out, full, cut):
-    half = part.shape[0]
-    full[pl.ds(pl.multiple_of(scal[2] * half, 32), half), :] = part[...].astype(f32)
-    full[pl.ds(pl.multiple_of((1 - scal[2]) * half, 32), half), :] = away[...].astype(f32)
+def qkv_out_kernel(scal, part, away, sums_ref, out, *refs):
+    outs, (full, cut) = refs[:-2], refs[-2:]
+    half = part.shape[0] - 32
+    full[pl.ds(pl.multiple_of(scal[2] * half, 32), half), :] = part[:half, :].astype(f32)
+    full[pl.ds(pl.multiple_of((1 - scal[2]) * half, 32), half), :] = away[:half, :].astype(f32)
     flat_store(full, cut, out)
-
-
-def vector_kernel(scal, sums, feats, *outs):
+    sums = sums_ref[...] + unpack_sums(away[half:, :])
     width = outs[0].shape[1]
-    mine = feats[:, :width]
-    for j in range(1, feats.shape[1] // width):
-        mine = jnp.where(scal[1] == j, feats[:, j * width : (j + 1) * width], mine)
+    mine = sums[:, :width]
+    for j in range(1, sums.shape[1] // width):
+        mine = jnp.where(scal[1] == j, sums[:, j * width : (j + 1) * width], mine)
     for i in range(6):
         outs[i][...] = mine[i : i + 1, :]
     outs[6][...] = sums[6:7, :]
@@ -633,16 +675,19 @@
     scal = jnp.stack([lax.axis_index("row").astype(jnp.int32), c, d])
     token_sum = [((tokens // 2, D), f32), ((tokens // 2, D), bf16)]
 
+    shape = (own + 16, 2 * width_in)
     message = call(
-        functools.partial(message_kernel, own),
-        [((n_col, own + 16, 2 * width_in), bf16)],
-        None,
+        functools.partial(message_kernel, own, n_col),
+        [(shape, bf16)] * n_col,
+        scal,
         [
             block_input.T,
             out_grad.T,
             *[v[None] for v in (ln1_gain, ln1_bias, ln2_gain, ln2_bias, out_bias, down_bias)],
         ],
-    )[0]
+        [((n_col, own, 2 * width_in), bf16)],
+    )
+    got = [message[0]] + [swap(message[k], "col", k) for k in range(1, n_col)]
 
     qkv_flat, out_flat = qkv_weight, out_weight
     own_qkv = qkv_flat.reshape(width_in, 3 * width_out)
@@ -653,17 +698,19 @@
     half_m = call(prep_mlp_kernel, [((2 * width_in, half_ff), bf16)], scal, [up_weight, down_weight])[0]
     near_a = gather_col(half_a)[1:]
     far_a = [swap(v, "dp", 1) for v in near_a]
-    half_m = after(half_m, near_a[2])
+    half_m = after(half_m, near_a[2], far_a[:2])
     near_m = gather_col(half_m)[1:]
-    far_m = [swap(v, "dp", 1) for v in near_m]
-
-    got = after(turn(message), near_a[0])
-    xg_own, vec = call(token_kernel, [((2 * own, D), bf16), ((8, D), f32)], None, [got])
+    far_m = [swap(v, "dp", 1) for v in near_m[:2]]
+
+    xg_own, vec = call(
+        token_kernel, [((2 * own, D), bf16), ((8, D), f32)], scal, got, [((n_col, *shape), bf16)]
+    )
     xg = gather_row(xg_own)
-    qkv_cut, a1, w_qkv, w_out = call(
+    q, kv, a1, w_qkv, w_out = call(
         functools.partial(qkv_kernel, heads, tokens, n_row, n_col),
         [
-            ((n_col, tokens // 2, 6 * HEAD), bf16),
+            ((tokens, width_out), bf16),
+            ((tokens, 2 * width_out), bf16),
             ((tokens, D), bf16),
             ((D, 3 * width_out), bf16),
             ((n_col, width_out, width_in), bf16),
@@ -671,22 +718,18 @@
         scal,
         [*xg, vec, qv_bias, own_qkv, own_out, *near_a, *far_a],
     )
-    qkv_head = turn(after(qkv_cut, near_m[:2]))
-    att_head = call(
-        functools.partial(forward_kernel, order),
-        [((n_col, tokens // 2, 2 * HEAD), bf16)],
-        scal,
-        [qkv_head],
-        [((tokens * n_col, 3 * HEAD), bf16), ((tokens * n_col, HEAD), bf16)],
-    )[0]
+    kv_all = gather_col(after(kv, near_m[:2]))
     attended, o_keep, o_send = call(
-        functools.partial(out_kernel, heads, own),
+        functools.partial(attention_kernel, order, n_col, heads),
         [((tokens, width_out), bf16)] + token_sum,
-        None,
-        [after(turn(after(att_head, near_m[2])), far_m[:2]), w_out],
-    )
+        scal,
+        [q, *after(kv_all, near_m[2], far_m), w_out],
+        [((tokens * n_col, 2 * width_out), bf16)],
+        cost=5,
+    )
+    far_m.append(swap(near_m[2], "dp", 1))
     resid1, a2_own = call(
-        norm2_kernel, [((own, D), f32), ((own, D), bf16)], None, [*after(finish_row(o_keep, o_send), far_m[2]), xg_own, vec]
+        norm2_kernel, [((own, D), f32), ((own, D), bf16)], None, [*after(finish_row(o_keep, o_send), far_m), xg_own, vec]
     )
     a2 = gather_row(a2_own)
     act, d_pre, up_sum, a_keep, a_send = call(
@@ -702,16 +745,19 @@
         [*a2, *xg, up_bias[None], up_weight, down_weight, *near_m, *far_m],
         [((D, ff), bf16), ((D, ff), bf16)],
     )
+    bits = bits_of("row")
+    for b in bits[:-1]:
+        a_keep, a_send = add_halves(a_keep, swap(a_send, "row", b))
+    a_got = swap(a_send, "row", bits[-1])
+    act, d_pre = after((act, d_pre), a_send)
     up_mine, up_other, down_mine, down_other = call(
         functools.partial(mlp_grad_kernel, n_row),
         [((D, half_ff), bf16)] * 4,
         None,
         [*a2, *xg, act, d_pre],
     )
-    a_keep, a_got = finish_row(a_keep, a_send)
     a_got = after(a_got, up_other, down_other)
     up_got = swap(up_other, "dp", 1)
-    down_got = swap(after(down_other, up_got), "dp", 1)
     gp, d_resid1, sums2 = call(
         norm2_back_kernel,
         [((own, D), bf16), ((own, D), f32), ((4, D), f32)],
@@ -719,63 +765,76 @@
         [a_keep, a_got, xg_own, vec, resid1],
     )
     gp_all = gather_row(gp)
-    d_att_cut, out_mine, out_other = call(
+    d_att, out_mine, out_other = call(
         functools.partial(d_att_kernel, n_row, heads),
-        [((n_col, tokens // 2, 2 * HEAD), bf16)] + [((n_col * width_out // 4, 2 * width_in), bf16)] * 2,
+        [((tokens, width_out), bf16)] + [((n_col * width_out // 4, 2 * width_in), bf16)] * 2,
         scal,
         [*gp_all, attended, w_out],
         [((width_out, D), bf16)],
     )
     out_got = swap(out_other, "dp", 1)
     up_parts = join_dp([up_mine], [after(up_got, gp_all)], scal)
-    d_att_head = after(turn(d_att_cut), up_parts, down_got)
-    up_total, up_away = share_dp(*finish_col(*up_parts))
-    d_qkv_head = call(
-        functools.partial(backward_kernel, order),
-        [((n_col, tokens // 2, 6 * HEAD), bf16)],
-        scal,
-        [qkv_head, d_att_head],
+    down_got = swap(after(down_other, up_parts), "dp", 1)
+    up_got = swap(up_parts[1], "col", 1)
+    dq, dkv_keep, dkv_send = call(
+        functools.partial(attention_back_kernel, order, col_order(), heads),
         [
-            ((tokens * n_col, 3 * HEAD), bf16),
-            ((tokens * n_col, HEAD), bf16),
-            ((tokens * n_col, 3 * HEAD), bf16),
-            ((HEAD, tokens * n_col), f32),
-            ((HEAD, tokens * n_col), f32),
+            ((tokens, width_out), bf16),
+            ((n_col // 2 * tokens, 2 * width_out), f32),
+            ((n_col // 2 * tokens, 2 * width_out), bf16),
         ],
-    )[0]
-    down_parts = join_dp([down_mine, out_mine], [down_got, out_got], scal)
-    d_qkv_cut = after(turn(after(d_qkv_head, up_total)), down_parts)
+        scal,
+        [q, *kv_all, after(d_att, up_parts)],
+        [
+            ((tokens * n_col, 2 * width_out), bf16),
+            ((2 * width_out, tokens * n_col), f32),
+            ((tokens * n_col, 2 * width_out), f32),
+        ],
+        cost=10,
+    )
+    dkv_got = swap(after(dkv_send, up_got), "col", 1)
+    up_pair = finish_col(*add_halves(up_parts[0], after(up_got, dkv_send)), 2)
+    dkv_keep, dkv_send = add_halves(dkv_keep, after(dkv_got, down_got, up_pair))
+    dkv_keep, dkv_got = finish_col(dkv_keep, dkv_send, 2)
+    down_parts = join_dp([down_mine, out_mine], after((down_got, out_got), dkv_send), scal)
+    down_got = swap(down_parts[1], "col", 1)
+    dkv_got = after(dkv_got, down_got)
     d_keep, d_send, sums1, qkv_mine, qkv_other = call(
-        functools.partial(d_a1_kernel, n_row, heads),
-        token_sum + [((8, D), f32), ((D // 2, 3 * width_out), bf16), ((D // 2 + 32, 3 * width_out), bf16)],
-        scal,
-        [*xg, d_qkv_cut, a1, w_qkv, sums2, up_sum],
+        functools.partial(d_a1_kernel, n_row, n_col),
+        [((tokens // 2, D), f32), ((tokens // 2 + 32, D), bf16), ((8, D), f32)]
+        + [((D // 2, 3 * width_out), bf16)] * 2,
+        scal,
+        [*xg, dq, dkv_keep, dkv_got, a1, w_qkv, sums2, up_sum],
         [((D, 3 * width_out), bf16)],
     )
     qkv_got = swap(qkv_other, "dp", 1)
 
-    outs = call(
+    down_half = add_halves(down_parts[0], after(down_got, d_send))
+    up_total, up_away = share_dp(*after(up_pair, d_send))
+    bits = bits_of("row")
+    for b in bits[:-1]:
+        half = d_keep.shape[0] // 2
+        d_keep, d_send, sums1 = call(
+            d_half_kernel,
+            [((half, D), f32), ((half + 32, D), bf16), ((8, D), f32)],
+            None,
+            [d_keep, swap(d_send, "row", b), sums1],
+        )
+    outs, sums = call(
         final_kernel,
-        [((n_col, width_in, 2 * own), bf16)],
+        [((n_col, width_in, 2 * own), bf16), ((8, D), f32)],
         None,
-        [*finish_row(d_keep, d_send), a_keep, a_got, xg_own, vec, resid1, d_resid1],
-    )[0]
+        [d_keep, swap(d_send, "row", bits[-1]), sums1, a_keep, a_got, xg_own, vec, resid1, d_resid1],
+    )
+    down_pair = finish_col(*down_half, 2)
     input_grad, block_output = call(last_kernel, [((width_in, tokens), bf16)] * 2, None, [turn(outs)])
 
-    d_up = call(up_out_kernel, [((width_in, ff), f32)], scal, [up_total, up_away])[0]
-    d_down, d_out = call(
-        down_out_kernel,
-        [((width_in, ff), f32), ((width_out * width_in // 128, 128), f32)],
-        scal,
-        share_dp(*finish_col(*down_parts)),
-        [((width_out, width_in), f32), ((pl.cdiv(width_in, 128), width_out, 128), f32)],
-    )
     rows, width = D // 2, 3 * width_out
-    keep, send, sums = call(
+    keep, send = call(
         functools.partial(qkv_part_kernel, col_order()),
-        [((rows // 2, width), f32), ((rows // 2 + 32, width), bf16), ((8, D), f32)],
-        scal,
-        [qkv_mine, after(qkv_got, outs), sums1],
+        [((rows // 2, width), f32), ((rows // 2 + 32, width), bf16)],
+        scal,
+        [qkv_mine, after(qkv_got, outs, down_pair), sums],
     )
     bits = bits_of("col")
     for b in bits[:-1]:
@@ -786,34 +845,27 @@
             None,
             [keep, swap(send, "col", b), sums],
         )
-    total, sums = call(
-        qkv_add_kernel,
-        [((rows // 2, width), bf16), ((8, D), f32)],
-        None,
-        [keep, swap(send, "col", bits[-1]), sums],
-    )
-
-    def add(value, axis, bit, kind=f32):
-        return call(add_kernel, [(value.shape, kind)], None, [value, swap(value, axis, bit)])[0]
-
+    d_up = call(up_out_kernel, [((width_in, ff), f32)], scal, [up_total, up_away])[0]
+    last = [((rows // 2 + 32, width), bf16), ((8, D), f32)]
+    got = after(swap(send, "col", bits[-1]), input_grad, d_up)
+    total, sums = call(qkv_add_kernel, last, None, [keep, got, sums])
     for b in bits_of("dp", 2):
-        total, sums = add(total, "dp", b, bf16), add(sums, "dp", b)
-    away = swap(total, "dp", 1)
-    feats = sums
-    for b in bits_of("row"):
-        feats = add(feats, "row", b)
-    d_qkv = call(
+        total, sums = call(qkv_add_kernel, last, None, [total, swap(total, "dp", b), sums])
+    d_down, d_out = call(
+        down_out_kernel,
+        [((width_in, ff), f32), ((width_out * width_in // 128, 128), f32)],
+        scal,
+        share_dp(*after(down_pair, send)),
+        [((width_out, width_in), f32), ((pl.cdiv(width_in, 128), width_out, 128), f32)],
+    )
+    d_qkv, *vecs = call(
         qkv_out_kernel,
-        [((width * width_in // 128, 128), f32)],
-        scal,
-        [total, after(away, d_up, d_down, input_grad)],
+        [((width * width_in // 128, 128), f32)]
+        + [((1, width_in), f32)] * 6
+        + [((1, ff), f32), ((2, width_out), f32)],
+        scal,
+        [total, after(swap(total, "dp", 1), d_down), sums],
         [((width_in, width), f32), ((pl.cdiv(width, 128), width_in, 128), f32)],
-    )[0]
-    vecs = call(
-        vector_kernel,
-        [((1, width_in), f32)] * 6 + [((1, ff), f32), ((2, width_out), f32)],
-        scal,
-        [sums, feats],
     )
 
     return (

time: 202 us -> 187 us (0.926)
  starting transfers between devices: 72.4 us -> 49.9 us
  waiting for transfers between devices: 76.8 us -> 97.3 us
  local copies, waits for them, and re-layouts: 12.9 us -> 0.4 us
    ppermute x42 -> x48, waiting for transfers between devices: 61.8 us -> 97.3 us  [swap(): return lax.ppermute(value, axis, [(i, i ^ bit) for i in range(n)])]
    all_to_all x6 -> x1, starting transfers between devices: 24.5 us -> 3.92 us  [turn(): return lax.all_to_all(value, 'col', split, concat, tiled=True)]
    all_to_all x6 -> x1, waiting for transfers between devices: 15.1 us -> 0.01 us  [turn(): return lax.all_to_all(value, 'col', split, concat, tiled=True)]
    unnamed x72 -> x24, local copies, waits for them, and re-layouts: 12.5 us -> 0.07 us
    ppermute x42 -> x48, starting transfers between devices: 47.9 us -> 46 us  [swap(): return lax.ppermute(value, axis, [(i, i ^ bit) for i in range(n)])]
    pallas_call x34 -> x31, Pallas kernels: 35 us -> 34.1 us  [call(): pl.pallas_call(kernel, out_shape=[jax.ShapeDtypeStruct(s, t) for s, t in...]
  transfers between devices with their start and end apart: 48 -> 49, of which waited for: 26 -> 27; matrix products, arithmetic and copies ran while one was open for 1% -> 0% of each run, Pallas kernels for 14% -> 11%
where the time goes in v5:
time: 187 us
  waiting for transfers between devices  97.3 us (52%)
  starting transfers between devices  49.9 us (27%)
  Pallas kernels  34.1 us (18%)
  other arithmetic  4.24 us (2%)
    ppermute x48, waiting for transfers between devices, swap(): return lax.ppermute(value, axis, [(i, i ^ bit) for i in range(n)])  97.3 us
    ppermute x48, starting transfers between devices, swap(): return lax.ppermute(value, axis, [(i, i ^ bit) for i in range(n)])  46 us
    pallas_call x31, Pallas kernels, call(): pl.pallas_call(kernel, out_shape=[jax.ShapeDtypeStruct(s, t) for s, t in...  34.1 us
    all_to_all x1, starting transfers between devices, turn(): return lax.all_to_all(value, 'col', split, concat, tiled=True)  3.92 us
  transfers between devices with their start and end apart: 49, of which 27 were waited for; matrix products, arithmetic and copies ran while one was open for 0% of the time, Pallas kernels for 11%

profile of v5, /device:TPU:0, one launch (start us, length us, event | category | flops | bytes accessed | tf_op | source)
XLA Modules:
  0.0 187.1 jit_solution(10093892070637345061)
XLA Ops:
  5.4 4.1 %collective-permute-start.7 = (bf16[96,768]{1,0:T(8,128)(2,1)S(1)}, bf16[96,768]{1,0:T(8,128)(2,1)S(1)}, u32[]{:S(2)}, u32[]{:S(2)}) collective-permute-start(bf16[96,768]{1,0:T(8,128)(2,1)S(1)} %shard_map.247), channel_id=1, source_target_pairs={{0,2},{1,3},{2,0},{3,1},{4,6},{5,7},{6,4},{7,5},{8,10},{9,11},{10,... | collective-permute-start | bytes 442376 | tf_op jit(solution)/shard_map/ppermute | solution.py:49
  12.5 3.9 %collective-permute-start.2 = (bf16[80,384]{1,0:T(8,128)(2,1)S(1)}, bf16[80,384]{1,0:T(8,128)(2,1)S(1)}, u32[]{:S(2)}, u32[]{:S(2)}) collective-permute-start(bf16[80,384]{1,0:T(8,128)(2,1)S(1)} %get-tuple-element.123), channel_id=1, source_target_pairs={{0,3},{1,2},{2,1},{3,0},{4,7},{5,6},{6,5},{7,4},{8,11},{9,10},{10,... | collective-permute-start | bytes 184328 | tf_op jit(solution)/shard_map/ppermute | solution.py:49
  31.6 4.3 %collective-permute-done.11.refs_13_ = bf16[96,768]{1,0:T(8,128)(2,1)S(1)} collective-permute-done((bf16[96,768]{1,0:T(8,128)(2,1)S(1)}, bf16[96,768]{1,0:T(8,128)(2,1)S(1)}, u32[]{:S(2)}, u32[]{:S(2)}) %collective-permute-start.11) | collective-permute-done | bytes 147488 | tf_op jit(solution)/shard_map/ppermute | solution.py:49
  37.2 3.6 %collective-permute-done.13.refs_12_ = bf16[384,384]{1,0:T(8,128)(2,1)S(1)} collective-permute-done((bf16[384,384]{1,0:T(8,128)(2,1)S(1)}, bf16[384,384]{1,0:T(8,128)(2,1)S(1)}, u32[]{:S(2)}, u32[]{:S(2)}) %collective-permute-start.13) | collective-permute-done | bytes 294944 | tf_op jit(solution)/shard_map/ppermute | solution.py:49
  43.6 2.6 %collective-permute-start.17 = (bf16[384,384]{1,0:T(8,128)(2,1)S(1)}, bf16[384,384]{1,0:T(8,128)(2,1)S(1)}, u32[]{:S(2)}, u32[]{:S(2)}) collective-permute-start(bf16[384,384]{1,0:T(8,128)(2,1)S(1)} %collective-permute-done.13.refs_12_), channel_id=1, source_target_pairs={{0,1},{1,0},{2,3},{3,2},{4,5},{5,4},{6,7},{7,6},{8,9},{9,8},{10,11... | collective-permute-start | bytes 884744 | tf_op jit(solution)/shard_map/ppermute | solution.py:49
  46.7 5.2 %collective-permute-done.15.refs_2_ = bf16[256,384]{1,0:T(8,128)(2,1)S(1)} collective-permute-done((bf16[256,384]{1,0:T(8,128)(2,1)S(1)}, bf16[256,384]{1,0:T(8,128)(2,1)S(1)}, u32[]{:S(2)}, u32[]{:S(2)}) %collective-permute-start.15) | collective-permute-done | bytes 196640 | tf_op jit(solution)/shard_map/ppermute | solution.py:49
  51.9 9.0 %collective-permute-done.14.refs_1_ = bf16[256,384]{1,0:T(8,128)(2,1)S(1)} collective-permute-done((bf16[256,384]{1,0:T(8,128)(2,1)S(1)}, bf16[256,384]{1,0:T(8,128)(2,1)S(1)}, u32[]{:S(2)}, u32[]{:S(2)}) %collective-permute-start.14) | collective-permute-done | bytes 196640 | tf_op jit(solution)/shard_map/ppermute | solution.py:49
  60.9 2.8 %collective-permute-done.16.refs_3_ = bf16[256,384]{1,0:T(8,128)(2,1)S(1)} collective-permute-done((bf16[256,384]{1,0:T(8,128)(2,1)S(1)}, bf16[256,384]{1,0:T(8,128)(2,1)S(1)}, u32[]{:S(2)}, u32[]{:S(2)}) %collective-permute-start.16) | collective-permute-done | bytes 196640 | tf_op jit(solution)/shard_map/ppermute | solution.py:49
  63.7 4.5 %shard_map.250 = (bf16[256,192]{1,0:T(8,128)(2,1)S(1)}, f32[128,768]{1,0:T(8,128)S(1)}, bf16[128,768]{1,0:T(8,128)(2,1)S(1)}) custom-call(s32[3]{0:T(128)S(1)} %pad_add_fusion.scal, bf16[256,192]{1,0:T(8,128)(2,1)S(1)} %get-tuple-element.126.q_ref, bf16[256,384]{1,0:T(8,128)(2,1)S(1)} %get-tuple-element.130.refs_0_, ...), custom_call_target="tpu_custom_call" | custom-call | flops 1 | bytes 15000001 | tf_op jit(solution)/shard_map/pallas_call | solution.py:36
  70.0 7.7 %collective-permute-done.22.refs_16_ = bf16[384,384]{1,0:T(8,128)(2,1)S(1)} collective-permute-done((bf16[384,384]{1,0:T(8,128)(2,1)S(1)}, bf16[384,384]{1,0:T(8,128)(2,1)S(1)}, u32[]{:S(2)}, u32[]{:S(2)}) %collective-permute-start.22) | collective-permute-done | bytes 294944 | tf_op jit(solution)/shard_map/ppermute | solution.py:49
  78.1 4.5 %collective-permute-done.23.refs_1_ = bf16[64,768]{1,0:T(8,128)(2,1)S(1)} collective-permute-done((bf16[64,768]{1,0:T(8,128)(2,1)S(1)}, bf16[64,768]{1,0:T(8,128)(2,1)S(1)}, u32[]{:S(2)}, u32[]{:S(2)}) %collective-permute-start.23) | collective-permute-done | bytes 98336 | tf_op jit(solution)/shard_map/ppermute | solution.py:49
  83.9 2.3 %shard_map.253 = (bf16[256,768]{1,0:T(8,128)(2,1)S(1)}, bf16[256,768]{1,0:T(8,128)(2,1)S(1)}, f32[1,768]{1,0:T(1,128)S(1)}, f32[128,1536]{1,0:T(8,128)S(1)}, bf16[128,1536]{1,0:T(8,128)(2,1)S(1)}) custom-call(s32[3]{0:T(128)S(1)} %pad_add_fusion.scal, bf16[64,768]{1,0:T(8,128)(2,1)S(1)} %get-tuple-element.141.refs_0_, ...), custom_call_target="tpu_custom_call" | custom-call | flops 1 | bytes 1 | tf_op jit(solution)/shard_map/pallas_call | solution.py:36
  89.9 6.5 %collective-permute-done.27.got.a_got = bf16[64,1536]{1,0:T(8,128)(2,1)S(1)} collective-permute-done((bf16[64,1536]{1,0:T(8,128)(2,1)S(1)}, bf16[64,1536]{1,0:T(8,128)(2,1)S(1)}, u32[]{:S(2)}, u32[]{:S(2)}) %collective-permute-start.27) | collective-permute-done | bytes 196640 | tf_op jit(solution)/shard_map/ppermute | solution.py:49
  96.9 4.3 %collective-permute-done.28.refs_1_ = bf16[64,768]{1,0:T(8,128)(2,1)S(1)} collective-permute-done((bf16[64,768]{1,0:T(8,128)(2,1)S(1)}, bf16[64,768]{1,0:T(8,128)(2,1)S(1)}, u32[]{:S(2)}, u32[]{:S(2)}) %collective-permute-start.28) | collective-permute-done | bytes 98336 | tf_op jit(solution)/shard_map/ppermute | solution.py:49
  106.9 9.9 %shard_map.259 = (bf16[256,192]{1,0:T(8,128)(2,1)S(1)}, f32[512,384]{1,0:T(8,128)S(1)}, bf16[512,384]{1,0:T(8,128)(2,1)S(1)}) custom-call(s32[3]{0:T(128)S(1)} %pad_add_fusion.scal, bf16[256,192]{1,0:T(8,128)(2,1)S(1)} %get-tuple-element.126.q_ref, bf16[256,384]{1,0:T(8,128)(2,1)S(1)} %get-tuple-element.130.refs_0_, ...), custom_call_target="tpu_custom_call" | custom-call | flops 1 | bytes 30000000 | tf_op jit(solution)/shard_map/pallas_call | solution.py:36
  122.2 7.2 %collective-permute-done.35.refs_1_ = bf16[192,384]{1,0:T(8,128)(2,1)S(1)} collective-permute-done((bf16[192,384]{1,0:T(8,128)(2,1)S(1)}, bf16[192,384]{1,0:T(8,128)(2,1)S(1)}, u32[]{:S(2)}, u32[]{:S(2)}) %collective-permute-start.35) | collective-permute-done | bytes 147488 | tf_op jit(solution)/shard_map/ppermute | solution.py:49
  131.0 3.4 %collective-permute-start.38 = (bf16[480,384]{1,0:T(8,128)(2,1)S(1)}, bf16[480,384]{1,0:T(8,128)(2,1)S(1)}, u32[]{:S(2)}, u32[]{:S(2)}) collective-permute-start(bf16[480,384]{1,0:T(8,128)(2,1)S(1)} %get-tuple-element.178), channel_id=1, source_target_pairs={{0,1},{1,0},{2,3},{3,2},{4,5},{5,4},{6,7},{7,6},{8,9},{9,8},{10,11... | collective-permute-start | bytes 1105928 | tf_op jit(solution)/shard_map/ppermute | solution.py:49
  134.8 9.4 %collective-permute-done.36.refs_6_ = bf16[256,384]{1,0:T(8,128)(2,1)S(1)} collective-permute-done((bf16[256,384]{1,0:T(8,128)(2,1)S(1)}, bf16[256,384]{1,0:T(8,128)(2,1)S(1)}, u32[]{:S(2)}, u32[]{:S(2)}) %collective-permute-start.36) | collective-permute-done | bytes 196640 | tf_op jit(solution)/shard_map/ppermute | solution.py:49
  148.0 2.7 %collective-permute-start.42 = (bf16[240,384]{1,0:T(8,128)(2,1)S(1)}, bf16[240,384]{1,0:T(8,128)(2,1)S(1)}, u32[]{:S(2)}, u32[]{:S(2)}) collective-permute-start(bf16[240,384]{1,0:T(8,128)(2,1)S(1)} %get-tuple-element.199), channel_id=1, source_target_pairs={{0,2},{1,3},{2,0},{3,1},{4,6},{5,7},{6,4},{7,5},{8,10},{9,11},{10,... | collective-permute-start | bytes 552968 | tf_op jit(solution)/shard_map/ppermute | solution.py:49
  151.3 5.6 %collective-permute-done.40.d_got = bf16[96,768]{1,0:T(8,128)(2,1)S(1)} collective-permute-done((bf16[96,768]{1,0:T(8,128)(2,1)S(1)}, bf16[96,768]{1,0:T(8,128)(2,1)S(1)}, u32[]{:S(2)}, u32[]{:S(2)}) %collective-permute-start.40) | collective-permute-done | bytes 147488 | tf_op jit(solution)/shard_map/ppermute | solution.py:49
  160.8 3.9 %all-to-all-start = ((bf16[4,192,128]{2,1,0:T(8,128)(2,1)}), bf16[4,192,128]{2,1,0:T(8,128)(2,1)S(1)}, u32[]{:S(2)}, u32[]{:S(2)}) async-start(bf16[4,192,128]{2,1,0:T(8,128)(2,1)} %get-tuple-element.191), calls=%async_computation | async-start | bytes 393216 | tf_op jit(solution)/shard_map/all_to_all | solution.py:53
  165.4 6.7 %collective-permute-done.43.got_ref = bf16[224,576]{1,0:T(8,128)(2,1)S(1)} collective-permute-done((bf16[224,576]{1,0:T(8,128)(2,1)S(1)}, bf16[224,576]{1,0:T(8,128)(2,1)S(1)}, u32[]{:S(2)}, u32[]{:S(2)}) %collective-permute-start.43) | collective-permute-done | bytes 258080 | tf_op jit(solution)/shard_map/ppermute | solution.py:49
  175.1 4.2 %collective-permute-done.44.got_ref = bf16[128,576]{1,0:T(8,128)(2,1)S(1)} collective-permute-done((bf16[128,576]{1,0:T(8,128)(2,1)S(1)}, bf16[128,576]{1,0:T(8,128)(2,1)S(1)}, u32[]{:S(2)}, u32[]{:S(2)}) %collective-permute-start.44) | collective-permute-done | bytes 147488 | tf_op jit(solution)/shard_map/ppermute | solution.py:49
  181.6 3.2 %collective-permute-done.46.away = bf16[128,576]{1,0:T(8,128)(2,1)S(1)} collective-permute-done((bf16[128,576]{1,0:T(8,128)(2,1)S(1)}, bf16[128,576]{1,0:T(8,128)(2,1)S(1)}, u32[]{:S(2)}, u32[]{:S(2)}) %collective-permute-start.46) | collective-permute-done | bytes 147488 | tf_op jit(solution)/shard_map/ppermute | solution.py:49
  (136 shorter events, 64.7 us)
Async XLA Ops:
  5.4 12.0 %collective-permute-start.7 = (bf16[96,768]{1,0:T(8,128)(2,1)S(1)}, bf16[96,768]{1,0:T(8,128)(2,1)S(1)}, u32[]{:S(2)}, u32[]{:S(2)}) collective-permute-start(bf16[96,768]{1,0:T(8,128)(2,1)S(1)} %shard_map.247), channel_id=1, source_target_pairs={{0,2},{1,3},{2,0},{3,1},{4,6},{5,7},{6,4},{7,5},{8,10},{9,11},{10,... | collective-permute-start | bytes 442376 | tf_op jit(solution)/shard_map/ppermute | solution.py:49
  9.5 11.3 %collective-permute-start.6 = (bf16[96,768]{1,0:T(8,128)(2,1)S(1)}, bf16[96,768]{1,0:T(8,128)(2,1)S(1)}, u32[]{:S(2)}, u32[]{:S(2)}) collective-permute-start(bf16[96,768]{1,0:T(8,128)(2,1)S(1)} %shard_map.247), channel_id=1, source_target_pairs={{0,1},{1,0},{2,3},{3,2},{4,5},{5,4},{6,7},{7,6},{8,9},{9,8},{10,11... | collective-permute-start | bytes 442376 | tf_op jit(solution)/shard_map/ppermute | solution.py:49
  12.4 9.8 %collective-permute-start.1 = (bf16[80,384]{1,0:T(8,128)(2,1)S(1)}, bf16[80,384]{1,0:T(8,128)(2,1)S(1)}, u32[]{:S(2)}, u32[]{:S(2)}) collective-permute-start(bf16[80,384]{1,0:T(8,128)(2,1)S(1)} %get-tuple-element.122), channel_id=1, source_target_pairs={{0,2},{1,3},{2,0},{3,1},{4,6},{5,7},{6,4},{7,5},{8,10},{9,11},{10,... | collective-permute-start | bytes 184328 | tf_op jit(solution)/shard_map/ppermute | solution.py:49
  12.5 9.7 %collective-permute-start.2 = (bf16[80,384]{1,0:T(8,128)(2,1)S(1)}, bf16[80,384]{1,0:T(8,128)(2,1)S(1)}, u32[]{:S(2)}, u32[]{:S(2)}) collective-permute-start(bf16[80,384]{1,0:T(8,128)(2,1)S(1)} %get-tuple-element.123), channel_id=1, source_target_pairs={{0,3},{1,2},{2,1},{3,0},{4,7},{5,6},{6,5},{7,4},{8,11},{9,10},{10,... | collective-permute-start | bytes 184328 | tf_op jit(solution)/shard_map/ppermute | solution.py:49
  25.9 14.9 %collective-permute-start.13 = (bf16[384,384]{1,0:T(8,128)(2,1)S(1)}, bf16[384,384]{1,0:T(8,128)(2,1)S(1)}, u32[]{:S(2)}, u32[]{:S(2)}) collective-permute-start(bf16[384,384]{1,0:T(8,128)(2,1)S(1)} %shard_map.249), channel_id=1, source_target_pairs={{0,2},{1,3},{2,0},{3,1},{4,6},{5,7},{6,4},{7,5},{8,10},{9,11},{10,... | collective-permute-start | bytes 884744 | tf_op jit(solution)/shard_map/ppermute | solution.py:49
  27.5 13.8 %collective-permute-start.12 = (bf16[384,384]{1,0:T(8,128)(2,1)S(1)}, bf16[384,384]{1,0:T(8,128)(2,1)S(1)}, u32[]{:S(2)}, u32[]{:S(2)}) collective-permute-start(bf16[384,384]{1,0:T(8,128)(2,1)S(1)} %shard_map.249), channel_id=1, source_target_pairs={{0,1},{1,0},{2,3},{3,2},{4,5},{5,4},{6,7},{7,6},{8,9},{9,8},{10,11... | collective-permute-start | bytes 884744 | tf_op jit(solution)/shard_map/ppermute | solution.py:49
  41.2 10.7 %collective-permute-start.15 = (bf16[256,384]{1,0:T(8,128)(2,1)S(1)}, bf16[256,384]{1,0:T(8,128)(2,1)S(1)}, u32[]{:S(2)}, u32[]{:S(2)}) collective-permute-start(bf16[256,384]{1,0:T(8,128)(2,1)S(1)} %get-tuple-element.130.refs_0_), channel_id=1, source_target_pairs={{0,2},{1,3},{2,0},{3,1},{4,6},{5,7},{6,4},{7,5},{8,10},{9,11},{10,... | collective-permute-start | bytes 589832 | tf_op jit(solution)/shard_map/ppermute | solution.py:49
  42.1 18.8 %collective-permute-start.19 = (bf16[384,384]{1,0:T(8,128)(2,1)S(1)}, bf16[384,384]{1,0:T(8,128)(2,1)S(1)}, u32[]{:S(2)}, u32[]{:S(2)}) collective-permute-start(bf16[384,384]{1,0:T(8,128)(2,1)S(1)} %collective-permute-done.13.refs_12_), channel_id=1, source_target_pairs={{0,16},{16,0},{1,17},{17,1},{2,18},{18,2},{3,19},{19,3},{4,20},{20... | collective-permute-start | bytes 884744 | tf_op jit(solution)/shard_map/ppermute | solution.py:49
  43.6 17.3 %collective-permute-start.17 = (bf16[384,384]{1,0:T(8,128)(2,1)S(1)}, bf16[384,384]{1,0:T(8,128)(2,1)S(1)}, u32[]{:S(2)}, u32[]{:S(2)}) collective-permute-start(bf16[384,384]{1,0:T(8,128)(2,1)S(1)} %collective-permute-done.13.refs_12_), channel_id=1, source_target_pairs={{0,1},{1,0},{2,3},{3,2},{4,5},{5,4},{6,7},{7,6},{8,9},{9,8},{10,11... | collective-permute-start | bytes 884744 | tf_op jit(solution)/shard_map/ppermute | solution.py:49
  46.2 14.7 %collective-permute-start.18 = (bf16[384,384]{1,0:T(8,128)(2,1)S(1)}, bf16[384,384]{1,0:T(8,128)(2,1)S(1)}, u32[]{:S(2)}, u32[]{:S(2)}) collective-permute-start(bf16[384,384]{1,0:T(8,128)(2,1)S(1)} %collective-permute-done.12.refs_11_), channel_id=1, source_target_pairs={{0,16},{16,0},{1,17},{17,1},{2,18},{18,2},{3,19},{19,3},{4,20},{20... | collective-permute-start | bytes 884744 | tf_op jit(solution)/shard_map/ppermute | solution.py:49
  46.7 14.2 %collective-permute-start.14 = (bf16[256,384]{1,0:T(8,128)(2,1)S(1)}, bf16[256,384]{1,0:T(8,128)(2,1)S(1)}, u32[]{:S(2)}, u32[]{:S(2)}) collective-permute-start(bf16[256,384]{1,0:T(8,128)(2,1)S(1)} %get-tuple-element.130.refs_0_), channel_id=1, source_target_pairs={{0,1},{1,0},{2,3},{3,2},{4,5},{5,4},{6,7},{7,6},{8,9},{9,8},{10,11... | collective-permute-start | bytes 589832 | tf_op jit(solution)/shard_map/ppermute | solution.py:49
  51.9 11.8 %collective-permute-start.16 = (bf16[256,384]{1,0:T(8,128)(2,1)S(1)}, bf16[256,384]{1,0:T(8,128)(2,1)S(1)}, u32[]{:S(2)}, u32[]{:S(2)}) collective-permute-start(bf16[256,384]{1,0:T(8,128)(2,1)S(1)} %collective-permute-done.15.refs_2_), channel_id=1, source_target_pairs={{0,1},{1,0},{2,3},{3,2},{4,5},{5,4},{6,7},{7,6},{8,9},{9,8},{10,11... | collective-permute-start | bytes 589832 | tf_op jit(solution)/shard_map/ppermute | solution.py:49
  89.0 15.4 %collective-permute-start.31 = (bf16[768,384]{1,0:T(8,128)(2,1)S(1)}, bf16[768,384]{1,0:T(8,128)(2,1)S(1)}, u32[]{:S(2)}, u32[]{:S(2)}) collective-permute-start(bf16[768,384]{1,0:T(8,128)(2,1)S(1)} %get-tuple-element.150), channel_id=1, source_target_pairs={{0,16},{16,0},{1,17},{17,1},{2,18},{18,2},{3,19},{19,3},{4,20},{20... | collective-permute-start | bytes 1769480 | tf_op jit(solution)/shard_map/ppermute | solution.py:49
  105.2 11.7 %collective-permute-start.32 = (bf16[384,384]{1,0:T(8,128)(2,1)S(1)}, bf16[384,384]{1,0:T(8,128)(2,1)S(1)}, u32[]{:S(2)}, u32[]{:S(2)}) collective-permute-start(bf16[384,384]{1,0:T(8,128)(2,1)S(1)} %get-tuple-element.160), channel_id=1, source_target_pairs={{0,1},{1,0},{2,3},{3,2},{4,5},{5,4},{6,7},{7,6},{8,9},{9,8},{10,11... | collective-permute-start | bytes 884744 | tf_op jit(solution)/shard_map/ppermute | solution.py:49
  105.3 24.1 %collective-permute-start.34 = (bf16[768,384]{1,0:T(8,128)(2,1)S(1)}, bf16[768,384]{1,0:T(8,128)(2,1)S(1)}, u32[]{:S(2)}, u32[]{:S(2)}) collective-permute-start(bf16[768,384]{1,0:T(8,128)(2,1)S(1)} %get-tuple-element.166), channel_id=1, source_target_pairs={{0,16},{16,0},{1,17},{17,1},{2,18},{18,2},{3,19},{19,3},{4,20},{20... | collective-permute-start | bytes 1769480 | tf_op jit(solution)/shard_map/ppermute | solution.py:49
  116.9 13.3 %collective-permute-start.33 = (bf16[512,384]{1,0:T(8,128)(2,1)S(1)}, bf16[512,384]{1,0:T(8,128)(2,1)S(1)}, u32[]{:S(2)}, u32[]{:S(2)}) collective-permute-start(bf16[512,384]{1,0:T(8,128)(2,1)S(1)} %get-tuple-element.165), channel_id=1, source_target_pairs={{0,1},{1,0},{2,3},{3,2},{4,5},{5,4},{6,7},{7,6},{8,9},{9,8},{10,11... | collective-permute-start | bytes 1179656 | tf_op jit(solution)/shard_map/ppermute | solution.py:49
  119.0 10.4 %collective-permute-start.35 = (bf16[192,384]{1,0:T(8,128)(2,1)S(1)}, bf16[192,384]{1,0:T(8,128)(2,1)S(1)}, u32[]{:S(2)}, u32[]{:S(2)}) collective-permute-start(bf16[192,384]{1,0:T(8,128)(2,1)S(1)} %get-tuple-element.169), channel_id=1, source_target_pairs={{0,2},{1,3},{2,0},{3,1},{4,6},{5,7},{6,4},{7,5},{8,10},{9,11},{10,... | collective-permute-start | bytes 442376 | tf_op jit(solution)/shard_map/ppermute | solution.py:49
  120.7 9.5 %collective-permute-start.37 = (bf16[192,384]{1,0:T(8,128)(2,1)S(1)}, bf16[192,384]{1,0:T(8,128)(2,1)S(1)}, u32[]{:S(2)}, u32[]{:S(2)}) collective-permute-start(bf16[192,384]{1,0:T(8,128)(2,1)S(1)} %get-tuple-element.175), channel_id=1, source_target_pairs={{0,16},{16,0},{1,17},{17,1},{2,18},{18,2},{3,19},{19,3},{4,20},{20... | collective-permute-start | bytes 442376 | tf_op jit(solution)/shard_map/ppermute | solution.py:49
  131.0 13.9 %collective-permute-start.38 = (bf16[480,384]{1,0:T(8,128)(2,1)S(1)}, bf16[480,384]{1,0:T(8,128)(2,1)S(1)}, u32[]{:S(2)}, u32[]{:S(2)}) collective-permute-start(bf16[480,384]{1,0:T(8,128)(2,1)S(1)} %get-tuple-element.178), channel_id=1, source_target_pairs={{0,1},{1,0},{2,3},{3,2},{4,5},{5,4},{6,7},{7,6},{8,9},{9,8},{10,11... | collective-permute-start | bytes 1105928 | tf_op jit(solution)/shard_map/ppermute | solution.py:49
  134.4 9.8 %collective-permute-start.36 = (bf16[256,384]{1,0:T(8,128)(2,1)S(1)}, bf16[256,384]{1,0:T(8,128)(2,1)S(1)}, u32[]{:S(2)}, u32[]{:S(2)}) collective-permute-start(bf16[256,384]{1,0:T(8,128)(2,1)S(1)} %get-tuple-element.172), channel_id=1, source_target_pairs={{0,2},{1,3},{2,0},{3,1},{4,6},{5,7},{6,4},{7,5},{8,10},{9,11},{10,... | collective-permute-start | bytes 589832 | tf_op jit(solution)/shard_map/ppermute | solution.py:49
  146.4 13.6 %collective-permute-start.41 = (bf16[384,576]{1,0:T(8,128)(2,1)S(1)}, bf16[384,576]{1,0:T(8,128)(2,1)S(1)}, u32[]{:S(2)}, u32[]{:S(2)}) collective-permute-start(bf16[384,576]{1,0:T(8,128)(2,1)S(1)} %get-tuple-element.195), channel_id=1, source_target_pairs={{0,16},{16,0},{1,17},{17,1},{2,18},{18,2},{3,19},{19,3},{4,20},{20... | collective-permute-start | bytes 1327112 | tf_op jit(solution)/shard_map/ppermute | solution.py:49
  148.0 12.0 %collective-permute-start.42 = (bf16[240,384]{1,0:T(8,128)(2,1)S(1)}, bf16[240,384]{1,0:T(8,128)(2,1)S(1)}, u32[]{:S(2)}, u32[]{:S(2)}) collective-permute-start(bf16[240,384]{1,0:T(8,128)(2,1)S(1)} %get-tuple-element.199), channel_id=1, source_target_pairs={{0,2},{1,3},{2,0},{3,1},{4,6},{5,7},{6,4},{7,5},{8,10},{9,11},{10,... | collective-permute-start | bytes 552968 | tf_op jit(solution)/shard_map/ppermute | solution.py:49
  160.7 11.4 %collective-permute-start.43 = (bf16[224,576]{1,0:T(8,128)(2,1)S(1)}, bf16[224,576]{1,0:T(8,128)(2,1)S(1)}, u32[]{:S(2)}, u32[]{:S(2)}) collective-permute-start(bf16[224,576]{1,0:T(8,128)(2,1)S(1)} %get-tuple-element.203), channel_id=1, source_target_pairs={{0,1},{1,0},{2,3},{3,2},{4,5},{5,4},{6,7},{7,6},{8,9},{9,8},{10,11... | collective-permute-start | bytes 774152 | tf_op jit(solution)/shard_map/ppermute | solution.py:49
  160.8 13.6 %all-to-all-start = ((bf16[4,192,128]{2,1,0:T(8,128)(2,1)}), bf16[4,192,128]{2,1,0:T(8,128)(2,1)S(1)}, u32[]{:S(2)}, u32[]{:S(2)}) async-start(bf16[4,192,128]{2,1,0:T(8,128)(2,1)} %get-tuple-element.191), calls=%async_computation | async-start | bytes 393216 | tf_op jit(solution)/shard_map/all_to_all | solution.py:53
  (37 other events, 238.7 us)

commit v6 on v5

--- a/solution.py
+++ b/solution.py
@@ -77,11 +77,12 @@
     return pieces
 
 
-def gather_col(value):
+def gather_col(value, *others):
     pieces = {0: value}
     for b in reversed(bits_of("col")):
         for k in list(pieces):
-            pieces[k ^ b] = swap(pieces[k], "col", b)
+            piece = after(pieces[k], *others) if k and others else pieces[k]
+            pieces[k ^ b] = swap(piece, "col", b)
     return [pieces[k] for k in range(lax.axis_size("col"))]
 
 
@@ -158,15 +159,14 @@
     block = chunk * n_col
     width = heads * HEAD
     first = scal[1] * chunk
-    parts = [[] for _ in range(n_row)]
-    for h in range(heads):
-        k = nat[:, h * HEAD : (h + 1) * HEAD]
-        v = nat[:, width + h * HEAD : width + (h + 1) * HEAD]
-        for i in range(n_row):
-            upto = (i + 1) * block
-            q = q_ref[chunk_of(scal, order, i, chunk), :][:, h * HEAD : (h + 1) * HEAD]
-            e, total = row_exps(q, k[:upto], i * block, first)
-            parts[i].append((dot_nn(e.astype(bf16), v[:upto]) / total).astype(bf16))
+    ks = [nat[:, h * HEAD : (h + 1) * HEAD] for h in range(heads)]
+    vs = [nat[:, width + h * HEAD : width + (h + 1) * HEAD] for h in range(heads)]
+    parts = []
+    for i in range(n_row):
+        upto = (i + 1) * block
+        q = q_ref[chunk_of(scal, order, i, chunk), :]
+        es = [row_exps(q[:, h * HEAD : (h + 1) * HEAD], ks[h][:upto], i * block, first) for h in range(heads)]
+        parts.append([(dot_nn(e.astype(bf16), v[:upto]) / total).astype(bf16) for (e, total), v in zip(es, vs)])
     for i in range(n_row):
         att_out[chunk_of(scal, order, i, chunk), :] = jnp.concatenate(parts[i], axis=1)
     w_all = jnp.concatenate([w[j] for j in range(n_col)], axis=1)
@@ -183,24 +183,28 @@
     width = heads * HEAD
     first = scal[1] * chunk
     grads_t[...] = jnp.zeros_like(grads_t)
-    parts = [[] for _ in range(n_row)]
-    for h in range(heads):
-        here = slice(h * HEAD, (h + 1) * HEAD)
-        there = slice(width + h * HEAD, width + (h + 1) * HEAD)
-        k = nat[:, here]
-        v = nat[:, there]
-        for i in range(n_row):
-            upto = (i + 1) * block
-            at = chunk_of(scal, order, i, chunk)
-            q = q_ref[at, :][:, here]
-            do = do_ref[at, :][:, here]
-            e, total = row_exps(q, k[:upto], i * block, first)
-            p = e * (1.0 / total)
-            grads_t[there, :upto] += dot_tn(do, p.astype(bf16))
-            dp = dot_nt(do, v[:upto])
-            ds = (p * (dp - jnp.sum(dp * p, axis=-1, keepdims=True))).astype(bf16)
-            parts[i].append((dot_nn(ds, k[:upto]) * SCALE).astype(bf16))
-            grads_t[here, :upto] += dot_tn(q, ds)
+    here = [slice(h * HEAD, (h + 1) * HEAD) for h in range(heads)]
+    there = [slice(width + h * HEAD, width + (h + 1) * HEAD) for h in range(heads)]
+    ks = [nat[:, at] for at in here]
+    vs = [nat[:, at] for at in there]
+    parts = []
+    for i in range(n_row):
+        upto = (i + 1) * block
+        at = chunk_of(scal, order, i, chunk)
+        q_all, do_all = q_ref[at, :], do_ref[at, :]
+        qs, dos = [q_all[:, x] for x in here], [do_all[:, x] for x in here]
+        es = [row_exps(q, k[:upto], i * block, first) for q, k in zip(qs, ks)]
+        dps = [dot_nt(do, v[:upto]) for do, v in zip(dos, vs)]
+        ps = [e * (1.0 / total) for e, total in es]
+        dss = [
+            (p * (dp - jnp.sum(dp * p, axis=-1, keepdims=True))).astype(bf16) for p, dp in zip(ps, dps)
+        ]
+        parts.append([(dot_nn(ds, k[:upto]) * SCALE).astype(bf16) for ds, k in zip(dss, ks)])
+        d_vs = [dot_tn(do, p.astype(bf16)) for do, p in zip(dos, ps)]
+        d_ks = [dot_tn(q, ds) for q, ds in zip(qs, dss)]
+        for h in range(heads):
+            grads_t[there[h], :upto] += d_vs[h]
+            grads_t[here[h], :upto] += d_ks[h]
     for i in range(n_row):
         dq[chunk_of(scal, order, i, chunk), :] = jnp.concatenate(parts[i], axis=1)
     grads[:, :width] = grads_t[:width, :].T * SCALE
@@ -404,6 +408,16 @@
             to[j * (half // 2) : (j + 1) * (half // 2), :] = beside(piece[:, j * width : (j + 1) * width], half)
 
 
+def narrow(value):
+    wide = 2 * value.shape[1] // 3
+    return jnp.concatenate([value[:, :wide], beside(value[:, wide:], value.shape[0])], axis=0)
+
+
+def widen(value):
+    rows = 2 * value.shape[0] // 3
+    return jnp.concatenate([value[:rows], under(value[rows:], rows)], axis=1)
+
+
 def d_a1_kernel(n_row, n_col, scal, *refs):
     xgs, (dq, dkv_keep, dkv_got, a1, w), refs = refs[:n_row], refs[n_row : n_row + 5], refs[n_row + 5 :]
     sums2, up_sum, refs = refs[0], refs[1], refs[2:]
@@ -419,9 +433,9 @@
     full[...] = dot_tn(a1[...], d_qkv).astype(bf16)
     half = full.shape[0] // (2 * n_col)
     for j in range(n_col):
-        at = slice(j * half, (j + 1) * half)
-        mine[at, :] = full[pl.ds(pl.multiple_of((2 * j + d) * half, 32), half), :]
-        other[at, :] = full[pl.ds(pl.multiple_of((2 * j + 1 - d) * half, 32), half), :]
+        at = slice(j * 3 * half // 2, (j + 1) * 3 * half // 2)
+        mine[at, :] = narrow(full[pl.ds(pl.multiple_of((2 * j + d) * half, 32), half), :])
+        other[at, :] = narrow(full[pl.ds(pl.multiple_of((2 * j + 1 - d) * half, 32), half), :])
     centred, _ = norm_stats(stacked(xgs, slice(0, tokens // n_row)).astype(f32))
     pad = jnp.zeros((1, D - d_qkv.shape[1]), f32)
     total = jnp.concatenate(
@@ -493,19 +507,15 @@
 
 
 def pack_sums(v):
-    parts = three_parts(v)
-    cut = 3 * v.shape[1] // 4
-    rows = [p[:, :cut] for p in parts] + [jnp.concatenate([p[:, cut:] for p in parts], axis=1)]
+    half = v.shape[1] // 2
+    rows = [p[:, at : at + half] for p in three_parts(v) for at in (0, half)]
     return jnp.concatenate(rows, axis=0).astype(bf16)
 
 
 def unpack_sums(v):
     v = v.astype(f32)
-    n = v.shape[0] // 4
-    third = v.shape[1] // 3
-    parts = [
-        jnp.concatenate([v[i * n : (i + 1) * n], v[3 * n :, i * third : (i + 1) * third]], axis=1) for i in range(3)
-    ]
+    n = v.shape[0] // 6
+    parts = [jnp.concatenate([v[i * n : (i + 1) * n], v[(i + 1) * n : (i + 2) * n]], axis=1) for i in (0, 2, 4)]
     return parts[0] + parts[1] + parts[2]
 
 
@@ -545,7 +555,7 @@
 
 
 def qkv_add_kernel(keep_ref, got_ref, sums_ref, out, sums):
-    rows = out.shape[0] - 32
+    rows = out.shape[0] - 48
     out[:rows, :] = (keep_ref[:rows, :].astype(f32) + got_ref[:rows, :].astype(f32)).astype(bf16)
     total = sums_ref[...] + unpack_sums(got_ref[rows:, :])
     sums[...] = total
@@ -586,11 +596,12 @@
 
 def qkv_out_kernel(scal, part, away, sums_ref, out, *refs):
     outs, (full, cut) = refs[:-2], refs[-2:]
-    half = part.shape[0] - 32
-    full[pl.ds(pl.multiple_of(scal[2] * half, 32), half), :] = part[:half, :].astype(f32)
-    full[pl.ds(pl.multiple_of((1 - scal[2]) * half, 32), half), :] = away[:half, :].astype(f32)
+    rows = part.shape[0] - 48
+    half = 2 * rows // 3
+    full[pl.ds(pl.multiple_of(scal[2] * half, 32), half), :] = widen(part[:rows, :].astype(f32))
+    full[pl.ds(pl.multiple_of((1 - scal[2]) * half, 32), half), :] = widen(away[:rows, :].astype(f32))
     flat_store(full, cut, out)
-    sums = sums_ref[...] + unpack_sums(away[half:, :])
+    sums = sums_ref[...] + unpack_sums(away[rows:, :])
     width = outs[0].shape[1]
     mine = sums[:, :width]
     for j in range(1, sums.shape[1] // width):
@@ -696,11 +707,11 @@
         prep_kernel, [((width_in // 2, 3 * width_out + width_in), bf16)], scal, [own_qkv, own_out]
     )[0]
     half_m = call(prep_mlp_kernel, [((2 * width_in, half_ff), bf16)], scal, [up_weight, down_weight])[0]
-    near_a = gather_col(half_a)[1:]
+    near_a = gather_col(half_a, got)[1:]
     far_a = [swap(v, "dp", 1) for v in near_a]
     half_m = after(half_m, near_a[2], far_a[:2])
-    near_m = gather_col(half_m)[1:]
-    far_m = [swap(v, "dp", 1) for v in near_m[:2]]
+    near_m = [swap(half_m, "col", b) for b in bits_of("col")]
+    far_m = [swap(v, "dp", 1) for v in near_m]
 
     xg_own, vec = call(
         token_kernel, [((2 * own, D), bf16), ((8, D), f32)], scal, got, [((n_col, *shape), bf16)]
@@ -718,12 +729,13 @@
         scal,
         [*xg, vec, qv_bias, own_qkv, own_out, *near_a, *far_a],
     )
-    kv_all = gather_col(after(kv, near_m[:2]))
+    kv_all = gather_col(after(kv, near_m), far_m[0])
+    near_m.append(swap(after(near_m[1], kv_all), "col", 1))
     attended, o_keep, o_send = call(
         functools.partial(attention_kernel, order, n_col, heads),
         [((tokens, width_out), bf16)] + token_sum,
         scal,
-        [q, *after(kv_all, near_m[2], far_m), w_out],
+        [q, *after(kv_all, far_m[1]), w_out],
         [((tokens * n_col, 2 * width_out), bf16)],
         cost=5,
     )
@@ -798,11 +810,10 @@
     dkv_keep, dkv_got = finish_col(dkv_keep, dkv_send, 2)
     down_parts = join_dp([down_mine, out_mine], after((down_got, out_got), dkv_send), scal)
     down_got = swap(down_parts[1], "col", 1)
-    dkv_got = after(dkv_got, down_got)
     d_keep, d_send, sums1, qkv_mine, qkv_other = call(
         functools.partial(d_a1_kernel, n_row, n_col),
         [((tokens // 2, D), f32), ((tokens // 2 + 32, D), bf16), ((8, D), f32)]
-        + [((D // 2, 3 * width_out), bf16)] * 2,
+        + [((3 * D // 4, 2 * width_out), bf16)] * 2,
         scal,
         [*xg, dq, dkv_keep, dkv_got, a1, w_qkv, sums2, up_sum],
         [((D, 3 * width_out), bf16)],
@@ -829,10 +840,10 @@
     down_pair = finish_col(*down_half, 2)
     input_grad, block_output = call(last_kernel, [((width_in, tokens), bf16)] * 2, None, [turn(outs)])
 
-    rows, width = D // 2, 3 * width_out
+    rows, width = 3 * D // 4, 2 * width_out
     keep, send = call(
         functools.partial(qkv_part_kernel, col_order()),
-        [((rows // 2, width), f32), ((rows // 2 + 32, width), bf16)],
+        [((rows // 2, width), f32), ((rows // 2 + 48, width), bf16)],
         scal,
         [qkv_mine, after(qkv_got, outs, down_pair), sums],
     )
@@ -841,12 +852,12 @@
         rows //= 2
         keep, send, sums = call(
             qkv_half_kernel,
-            [((rows // 2, width), f32), ((rows // 2 + 32, width), bf16), ((8, D), f32)],
+            [((rows // 2, width), f32), ((rows // 2 + 48, width), bf16), ((8, D), f32)],
             None,
             [keep, swap(send, "col", b), sums],
         )
     d_up = call(up_out_kernel, [((width_in, ff), f32)], scal, [up_total, up_away])[0]
-    last = [((rows // 2 + 32, width), bf16), ((8, D), f32)]
+    last = [((rows // 2 + 48, width), bf16), ((8, D), f32)]
     got = after(swap(send, "col", bits[-1]), input_grad, d_up)
     total, sums = call(qkv_add_kernel, last, None, [keep, got, sums])
     for b in bits_of("dp", 2):
@@ -860,12 +871,12 @@
     )
     d_qkv, *vecs = call(
         qkv_out_kernel,
-        [((width * width_in // 128, 128), f32)]
+        [((3 * width_out * width_in // 128, 128), f32)]
         + [((1, width_in), f32)] * 6
         + [((1, ff), f32), ((2, width_out), f32)],
         scal,
         [total, after(swap(total, "dp", 1), d_down), sums],
-        [((width_in, width), f32), ((pl.cdiv(width, 128), width_in, 128), f32)],
+        [((width_in, 3 * width_out), f32), ((pl.cdiv(3 * width_out, 128), width_in, 128), f32)],
     )
 
     return (

time: 187 us -> 177 us (0.947)
  waiting for transfers between devices: 97.3 us -> 86.7 us
  starting transfers between devices: 49.9 us -> 57.3 us
  Pallas kernels: 34.1 us -> 27.2 us
    ppermute x48, waiting for transfers between devices: 97.3 us -> 86.7 us  [swap(): return lax.ppermute(value, axis, [(i, i ^ bit) for i in range(n)])]
    pallas_call x31, Pallas kernels: 34.1 us -> 27.2 us  [call(): pl.pallas_call(kernel, out_shape=[jax.ShapeDtypeStruct(s, t) for s, t in...]
    ppermute x48, starting transfers between devices: 46 us -> 52.9 us  [swap(): return lax.ppermute(value, axis, [(i, i ^ bit) for i in range(n)])]
  transfers between devices with their start and end apart: 49 -> 49, of which waited for: 27 -> 28; matrix products, arithmetic and copies ran while one was open for 0% -> 0% of each run, Pallas kernels for 11% -> 11%
where the time goes in v6:
time: 177 us
  waiting for transfers between devices  86.7 us (49%)
  starting transfers between devices  57.3 us (32%)
  Pallas kernels  27.2 us (15%)
  other arithmetic  4.24 us (2%)
    ppermute x48, waiting for transfers between devices, swap(): return lax.ppermute(value, axis, [(i, i ^ bit) for i in range(n)])  86.7 us
    ppermute x48, starting transfers between devices, swap(): return lax.ppermute(value, axis, [(i, i ^ bit) for i in range(n)])  52.9 us
    pallas_call x31, Pallas kernels, call(): pl.pallas_call(kernel, out_shape=[jax.ShapeDtypeStruct(s, t) for s, t in...  27.2 us
    all_to_all x1, starting transfers between devices, turn(): return lax.all_to_all(value, 'col', split, concat, tiled=True)  4.43 us
    unnamed x2, other arithmetic  3.55 us
  transfers between devices with their start and end apart: 49, of which 28 were waited for; matrix products, arithmetic and copies ran while one was open for 0% of the time, Pallas kernels for 11%

profile of v6, /device:TPU:0, one launch (start us, length us, event | category | flops | bytes accessed | tf_op | source)
XLA Modules:
  0.0 176.9 jit_solution(8705413034127399702)
XLA Ops:
  2.1 2.2 %reduce = bf16[110592]{0:T(1024)(128)(2,1)S(1)} reduce(bf16[1,1,110592]{2,1,0:T(2,128)(2,1)} %param.17, bf16[]{:T(256)} %constant.17), dimensions={0,1}, to_apply=%param.17.reduce_sub_computation | reduce | bytes 442370 | tf_op args[3]
  5.4 4.1 %collective-permute-start.7 = (bf16[96,768]{1,0:T(8,128)(2,1)S(1)}, bf16[96,768]{1,0:T(8,128)(2,1)S(1)}, u32[]{:S(2)}, u32[]{:S(2)}) collective-permute-start(bf16[96,768]{1,0:T(8,128)(2,1)S(1)} %shard_map.247), channel_id=1, source_target_pairs={{0,2},{1,3},{2,0},{3,1},{4,6},{5,7},{6,4},{7,5},{8,10},{9,11},{10,... | collective-permute-start | bytes 442376 | tf_op jit(solution)/shard_map/ppermute | solution.py:49
  12.5 3.9 %collective-permute-start.2 = (bf16[80,384]{1,0:T(8,128)(2,1)S(1)}, bf16[80,384]{1,0:T(8,128)(2,1)S(1)}, u32[]{:S(2)}, u32[]{:S(2)}) collective-permute-start(bf16[80,384]{1,0:T(8,128)(2,1)S(1)} %get-tuple-element.125), channel_id=1, source_target_pairs={{0,3},{1,2},{2,1},{3,0},{4,7},{5,6},{6,5},{7,4},{8,11},{9,10},{10,... | collective-permute-start | bytes 184328 | tf_op jit(solution)/shard_map/ppermute | solution.py:49
  16.4 3.4 %collective-permute-done.refs_1_ = bf16[80,384]{1,0:T(8,128)(2,1)S(1)} collective-permute-done((bf16[80,384]{1,0:T(8,128)(2,1)S(1)}, bf16[80,384]{1,0:T(8,128)(2,1)S(1)}, u32[]{:S(2)}, u32[]{:S(2)}) %collective-permute-start) | collective-permute-done | bytes 61472 | tf_op jit(solution)/shard_map/ppermute | solution.py:49
  29.3 2.2 %collective-permute-start.12 = (bf16[384,384]{1,0:T(8,128)(2,1)S(1)}, bf16[384,384]{1,0:T(8,128)(2,1)S(1)}, u32[]{:S(2)}, u32[]{:S(2)}) collective-permute-start(bf16[384,384]{1,0:T(8,128)(2,1)S(1)} %shard_map.249), channel_id=1, source_target_pairs={{0,1},{1,0},{2,3},{3,2},{4,5},{5,4},{6,7},{7,6},{8,9},{9,8},{10,11... | collective-permute-start | bytes 884744 | tf_op jit(solution)/shard_map/ppermute | solution.py:49
  35.4 8.7 %collective-permute-done.12.refs_11_ = bf16[384,384]{1,0:T(8,128)(2,1)S(1)} collective-permute-done((bf16[384,384]{1,0:T(8,128)(2,1)S(1)}, bf16[384,384]{1,0:T(8,128)(2,1)S(1)}, u32[]{:S(2)}, u32[]{:S(2)}) %collective-permute-start.12) | collective-permute-done | bytes 294944 | tf_op jit(solution)/shard_map/ppermute | solution.py:49
  47.1 3.4 %collective-permute-start.14 = (bf16[256,384]{1,0:T(8,128)(2,1)S(1)}, bf16[256,384]{1,0:T(8,128)(2,1)S(1)}, u32[]{:S(2)}, u32[]{:S(2)}) collective-permute-start(bf16[256,384]{1,0:T(8,128)(2,1)S(1)} %get-tuple-element.134.refs_0_), channel_id=1, source_target_pairs={{0,1},{1,0},{2,3},{3,2},{4,5},{5,4},{6,7},{7,6},{8,9},{9,8},{10,11... | collective-permute-start | bytes 589832 | tf_op jit(solution)/shard_map/ppermute | solution.py:49
  50.5 6.9 %collective-permute-done.15.refs_2_ = bf16[256,384]{1,0:T(8,128)(2,1)S(1)} collective-permute-done((bf16[256,384]{1,0:T(8,128)(2,1)S(1)}, bf16[256,384]{1,0:T(8,128)(2,1)S(1)}, u32[]{:S(2)}, u32[]{:S(2)}) %collective-permute-start.15) | collective-permute-done | bytes 196640 | tf_op jit(solution)/shard_map/ppermute | solution.py:49
  58.2 5.3 %collective-permute-done.17.refs_3_ = bf16[256,384]{1,0:T(8,128)(2,1)S(1)} collective-permute-done((bf16[256,384]{1,0:T(8,128)(2,1)S(1)}, bf16[256,384]{1,0:T(8,128)(2,1)S(1)}, u32[]{:S(2)}, u32[]{:S(2)}) %collective-permute-start.17) | collective-permute-done | bytes 196640 | tf_op jit(solution)/shard_map/ppermute | solution.py:49
  65.6 2.8 %shard_map.250 = (bf16[256,192]{1,0:T(8,128)(2,1)S(1)}, f32[128,768]{1,0:T(8,128)S(1)}, bf16[128,768]{1,0:T(8,128)(2,1)S(1)}) custom-call(s32[3]{0:T(128)S(1)} %pad_add_fusion.scal, bf16[256,192]{1,0:T(8,128)(2,1)S(1)} %get-tuple-element.129.q_ref, bf16[256,384]{1,0:T(8,128)(2,1)S(1)} %get-tuple-element.134.refs_0_, ...), custom_call_target="tpu_custom_call" | custom-call | flops 1 | bytes 15000001 | tf_op jit(solution)/shard_map/pallas_call | solution.py:36
  68.5 2.4 %collective-permute-done.21.refs_13_ = bf16[384,384]{1,0:T(8,128)(2,1)S(1)} collective-permute-done((bf16[384,384]{1,0:T(8,128)(2,1)S(1)}, bf16[384,384]{1,0:T(8,128)(2,1)S(1)}, u32[]{:S(2)}, u32[]{:S(2)}) %collective-permute-start.21) | collective-permute-done | bytes 294944 | tf_op jit(solution)/shard_map/ppermute | solution.py:49
  72.7 3.1 %collective-permute-done.20.got = bf16[64,768]{1,0:T(8,128)(2,1)S(1)} collective-permute-done((bf16[64,768]{1,0:T(8,128)(2,1)S(1)}, bf16[64,768]{1,0:T(8,128)(2,1)S(1)}, u32[]{:S(2)}, u32[]{:S(2)}) %collective-permute-start.20) | collective-permute-done | bytes 98336 | tf_op jit(solution)/shard_map/ppermute | solution.py:49
  79.7 3.1 %collective-permute-done.23.refs_1_ = bf16[64,768]{1,0:T(8,128)(2,1)S(1)} collective-permute-done((bf16[64,768]{1,0:T(8,128)(2,1)S(1)}, bf16[64,768]{1,0:T(8,128)(2,1)S(1)}, u32[]{:S(2)}, u32[]{:S(2)}) %collective-permute-start.23) | collective-permute-done | bytes 98336 | tf_op jit(solution)/shard_map/ppermute | solution.py:49
  84.1 2.3 %shard_map.253 = (bf16[256,768]{1,0:T(8,128)(2,1)S(1)}, bf16[256,768]{1,0:T(8,128)(2,1)S(1)}, f32[1,768]{1,0:T(1,128)S(1)}, f32[128,1536]{1,0:T(8,128)S(1)}, bf16[128,1536]{1,0:T(8,128)(2,1)S(1)}) custom-call(s32[3]{0:T(128)S(1)} %pad_add_fusion.scal, bf16[64,768]{1,0:T(8,128)(2,1)S(1)} %get-tuple-element.146.refs_0_, ...), custom_call_target="tpu_custom_call" | custom-call | flops 1 | bytes 1 | tf_op jit(solution)/shard_map/pallas_call | solution.py:36
  91.1 5.2 %collective-permute-done.27.got.a_got = bf16[64,1536]{1,0:T(8,128)(2,1)S(1)} collective-permute-done((bf16[64,1536]{1,0:T(8,128)(2,1)S(1)}, bf16[64,1536]{1,0:T(8,128)(2,1)S(1)}, u32[]{:S(2)}, u32[]{:S(2)}) %collective-permute-start.27) | collective-permute-done | bytes 196640 | tf_op jit(solution)/shard_map/ppermute | solution.py:49
  98.2 3.1 %collective-permute-done.28.refs_1_ = bf16[64,768]{1,0:T(8,128)(2,1)S(1)} collective-permute-done((bf16[64,768]{1,0:T(8,128)(2,1)S(1)}, bf16[64,768]{1,0:T(8,128)(2,1)S(1)}, u32[]{:S(2)}, u32[]{:S(2)}) %collective-permute-start.28) | collective-permute-done | bytes 98336 | tf_op jit(solution)/shard_map/ppermute | solution.py:49
  108.5 4.9 %shard_map.259 = (bf16[256,192]{1,0:T(8,128)(2,1)S(1)}, f32[512,384]{1,0:T(8,128)S(1)}, bf16[512,384]{1,0:T(8,128)(2,1)S(1)}) custom-call(s32[3]{0:T(128)S(1)} %pad_add_fusion.scal, bf16[256,192]{1,0:T(8,128)(2,1)S(1)} %get-tuple-element.129.q_ref, bf16[256,384]{1,0:T(8,128)(2,1)S(1)} %get-tuple-element.134.refs_0_, ...), custom_call_target="tpu_custom_call" | custom-call | flops 1 | bytes 30000000 | tf_op jit(solution)/shard_map/pallas_call | solution.py:36
  116.5 9.0 %collective-permute-done.35.refs_1_ = bf16[192,384]{1,0:T(8,128)(2,1)S(1)} collective-permute-done((bf16[192,384]{1,0:T(8,128)(2,1)S(1)}, bf16[192,384]{1,0:T(8,128)(2,1)S(1)}, u32[]{:S(2)}, u32[]{:S(2)}) %collective-permute-start.35) | collective-permute-done | bytes 147488 | tf_op jit(solution)/shard_map/ppermute | solution.py:49
  126.7 2.4 %collective-permute-start.36 = (bf16[256,384]{1,0:T(8,128)(2,1)S(1)}, bf16[256,384]{1,0:T(8,128)(2,1)S(1)}, u32[]{:S(2)}, u32[]{:S(2)}) collective-permute-start(bf16[256,384]{1,0:T(8,128)(2,1)S(1)} %get-tuple-element.177), channel_id=1, source_target_pairs={{0,2},{1,3},{2,0},{3,1},{4,6},{5,7},{6,4},{7,5},{8,10},{9,11},{10,... | collective-permute-start | bytes 589832 | tf_op jit(solution)/shard_map/ppermute | solution.py:49
  129.9 6.7 %collective-permute-done.36.refs_6_ = bf16[256,384]{1,0:T(8,128)(2,1)S(1)} collective-permute-done((bf16[256,384]{1,0:T(8,128)(2,1)S(1)}, bf16[256,384]{1,0:T(8,128)(2,1)S(1)}, u32[]{:S(2)}, u32[]{:S(2)}) %collective-permute-start.36) | collective-permute-done | bytes 196640 | tf_op jit(solution)/shard_map/ppermute | solution.py:49
  143.2 4.2 %collective-permute-done.38.d_got = bf16[96,768]{1,0:T(8,128)(2,1)S(1)} collective-permute-done((bf16[96,768]{1,0:T(8,128)(2,1)S(1)}, bf16[96,768]{1,0:T(8,128)(2,1)S(1)}, u32[]{:S(2)}, u32[]{:S(2)}) %collective-permute-start.38) | collective-permute-done | bytes 147488 | tf_op jit(solution)/shard_map/ppermute | solution.py:49
  151.1 4.4 %all-to-all-start = ((bf16[4,192,128]{2,1,0:T(8,128)(2,1)}), bf16[4,192,128]{2,1,0:T(8,128)(2,1)S(1)}, u32[]{:S(2)}, u32[]{:S(2)}) async-start(bf16[4,192,128]{2,1,0:T(8,128)(2,1)} %get-tuple-element.189), calls=%async_computation | async-start | bytes 393216 | tf_op jit(solution)/shard_map/all_to_all | solution.py:53
  159.1 3.0 %collective-permute-start.44 = (bf16[192,384]{1,0:T(8,128)(2,1)S(1)}, bf16[192,384]{1,0:T(8,128)(2,1)S(1)}, u32[]{:S(2)}, u32[]{:S(2)}) collective-permute-start(bf16[192,384]{1,0:T(8,128)(2,1)S(1)} %get-tuple-element.209), channel_id=1, source_target_pairs={{0,2},{1,3},{2,0},{3,1},{4,6},{5,7},{6,4},{7,5},{8,10},{9,11},{10,... | collective-permute-start | bytes 442376 | tf_op jit(solution)/shard_map/ppermute | solution.py:49
  166.3 3.0 %collective-permute-done.44.got_ref = bf16[192,384]{1,0:T(8,128)(2,1)S(1)} collective-permute-done((bf16[192,384]{1,0:T(8,128)(2,1)S(1)}, bf16[192,384]{1,0:T(8,128)(2,1)S(1)}, u32[]{:S(2)}, u32[]{:S(2)}) %collective-permute-start.44) | collective-permute-done | bytes 147488 | tf_op jit(solution)/shard_map/ppermute | solution.py:49
  (136 shorter events, 76.3 us)
Async XLA Ops:
  5.4 16.3 %collective-permute-start.7 = (bf16[96,768]{1,0:T(8,128)(2,1)S(1)}, bf16[96,768]{1,0:T(8,128)(2,1)S(1)}, u32[]{:S(2)}, u32[]{:S(2)}) collective-permute-start(bf16[96,768]{1,0:T(8,128)(2,1)S(1)} %shard_map.247), channel_id=1, source_target_pairs={{0,2},{1,3},{2,0},{3,1},{4,6},{5,7},{6,4},{7,5},{8,10},{9,11},{10,... | collective-permute-start | bytes 442376 | tf_op jit(solution)/shard_map/ppermute | solution.py:49
  9.5 13.7 %collective-permute-start.6 = (bf16[96,768]{1,0:T(8,128)(2,1)S(1)}, bf16[96,768]{1,0:T(8,128)(2,1)S(1)}, u32[]{:S(2)}, u32[]{:S(2)}) collective-permute-start(bf16[96,768]{1,0:T(8,128)(2,1)S(1)} %shard_map.247), channel_id=1, source_target_pairs={{0,1},{1,0},{2,3},{3,2},{4,5},{5,4},{6,7},{7,6},{8,9},{9,8},{10,11... | collective-permute-start | bytes 442376 | tf_op jit(solution)/shard_map/ppermute | solution.py:49
  12.5 9.1 %collective-permute-start.2 = (bf16[80,384]{1,0:T(8,128)(2,1)S(1)}, bf16[80,384]{1,0:T(8,128)(2,1)S(1)}, u32[]{:S(2)}, u32[]{:S(2)}) collective-permute-start(bf16[80,384]{1,0:T(8,128)(2,1)S(1)} %get-tuple-element.125), channel_id=1, source_target_pairs={{0,3},{1,2},{2,1},{3,0},{4,7},{5,6},{6,5},{7,4},{8,11},{9,10},{10,... | collective-permute-start | bytes 184328 | tf_op jit(solution)/shard_map/ppermute | solution.py:49
  29.3 14.8 %collective-permute-start.12 = (bf16[384,384]{1,0:T(8,128)(2,1)S(1)}, bf16[384,384]{1,0:T(8,128)(2,1)S(1)}, u32[]{:S(2)}, u32[]{:S(2)}) collective-permute-start(bf16[384,384]{1,0:T(8,128)(2,1)S(1)} %shard_map.249), channel_id=1, source_target_pairs={{0,1},{1,0},{2,3},{3,2},{4,5},{5,4},{6,7},{7,6},{8,9},{9,8},{10,11... | collective-permute-start | bytes 884744 | tf_op jit(solution)/shard_map/ppermute | solution.py:49
  31.5 15.5 %collective-permute-start.13 = (bf16[384,384]{1,0:T(8,128)(2,1)S(1)}, bf16[384,384]{1,0:T(8,128)(2,1)S(1)}, u32[]{:S(2)}, u32[]{:S(2)}) collective-permute-start(bf16[384,384]{1,0:T(8,128)(2,1)S(1)} %shard_map.249), channel_id=1, source_target_pairs={{0,2},{1,3},{2,0},{3,1},{4,6},{5,7},{6,4},{7,5},{8,10},{9,11},{10,... | collective-permute-start | bytes 884744 | tf_op jit(solution)/shard_map/ppermute | solution.py:49
  33.4 12.2 %collective-permute-start.4 = (bf16[128,768]{1,0:T(8,128)(2,1)S(1)}, bf16[128,768]{1,0:T(8,128)(2,1)S(1)}, u32[]{:S(2)}, u32[]{:S(2)}) collective-permute-start(bf16[128,768]{1,0:T(8,128)(2,1)S(1)} %get-tuple-element.126.refs_0_.xg.refs_4_), channel_id=1, source_target_pairs={{0,4},{4,0},{8,12},{12,8},{1,5},{5,1},{9,13},{13,9},{2,6},{6,2},{1... | collective-permute-start | bytes 589832 | tf_op jit(solution)/shard_map/ppermute | solution.py:49
  33.4 12.2 %collective-permute-start.5 = (bf16[128,768]{1,0:T(8,128)(2,1)S(1)}, bf16[128,768]{1,0:T(8,128)(2,1)S(1)}, u32[]{:S(2)}, u32[]{:S(2)}) collective-permute-start(bf16[128,768]{1,0:T(8,128)(2,1)S(1)} %collective-permute-done.3.refs_1_.refs_5_), channel_id=1, source_target_pairs={{0,4},{4,0},{8,12},{12,8},{1,5},{5,1},{9,13},{13,9},{2,6},{6,2},{1... | collective-permute-start | bytes 589832 | tf_op jit(solution)/shard_map/ppermute | solution.py:49
  33.9 11.7 %collective-permute-start.11 = (bf16[96,768]{1,0:T(8,128)(2,1)S(1)}, bf16[96,768]{1,0:T(8,128)(2,1)S(1)}, u32[]{:S(2)}, u32[]{:S(2)}) collective-permute-start(bf16[96,768]{1,0:T(8,128)(2,1)S(1)} %collective-permute-done.8.refs_10_), channel_id=1, source_target_pairs={{0,16},{16,0},{1,17},{17,1},{2,18},{18,2},{3,19},{19,3},{4,20},{20... | collective-permute-start | bytes 442376 | tf_op jit(solution)/shard_map/ppermute | solution.py:49
  44.1 13.2 %collective-permute-start.16 = (bf16[384,384]{1,0:T(8,128)(2,1)S(1)}, bf16[384,384]{1,0:T(8,128)(2,1)S(1)}, u32[]{:S(2)}, u32[]{:S(2)}) collective-permute-start(bf16[384,384]{1,0:T(8,128)(2,1)S(1)} %collective-permute-done.12.refs_11_), channel_id=1, source_target_pairs={{0,16},{16,0},{1,17},{17,1},{2,18},{18,2},{3,19},{19,3},{4,20},{20... | collective-permute-start | bytes 884744 | tf_op jit(solution)/shard_map/ppermute | solution.py:49
  47.0 10.3 %collective-permute-start.15 = (bf16[256,384]{1,0:T(8,128)(2,1)S(1)}, bf16[256,384]{1,0:T(8,128)(2,1)S(1)}, u32[]{:S(2)}, u32[]{:S(2)}) collective-permute-start(bf16[256,384]{1,0:T(8,128)(2,1)S(1)} %get-tuple-element.134.refs_0_), channel_id=1, source_target_pairs={{0,2},{1,3},{2,0},{3,1},{4,6},{5,7},{6,4},{7,5},{8,10},{9,11},{10,... | collective-permute-start | bytes 589832 | tf_op jit(solution)/shard_map/ppermute | solution.py:49
  47.1 11.1 %collective-permute-start.14 = (bf16[256,384]{1,0:T(8,128)(2,1)S(1)}, bf16[256,384]{1,0:T(8,128)(2,1)S(1)}, u32[]{:S(2)}, u32[]{:S(2)}) collective-permute-start(bf16[256,384]{1,0:T(8,128)(2,1)S(1)} %get-tuple-element.134.refs_0_), channel_id=1, source_target_pairs={{0,1},{1,0},{2,3},{3,2},{4,5},{5,4},{6,7},{7,6},{8,9},{9,8},{10,11... | collective-permute-start | bytes 589832 | tf_op jit(solution)/shard_map/ppermute | solution.py:49
  89.2 15.4 %collective-permute-start.31 = (bf16[768,384]{1,0:T(8,128)(2,1)S(1)}, bf16[768,384]{1,0:T(8,128)(2,1)S(1)}, u32[]{:S(2)}, u32[]{:S(2)}) collective-permute-start(bf16[768,384]{1,0:T(8,128)(2,1)S(1)} %get-tuple-element.155), channel_id=1, source_target_pairs={{0,16},{16,0},{1,17},{17,1},{2,18},{18,2},{3,19},{19,3},{4,20},{20... | collective-permute-start | bytes 1769480 | tf_op jit(solution)/shard_map/ppermute | solution.py:49
  107.2 18.3 %collective-permute-start.34 = (bf16[768,384]{1,0:T(8,128)(2,1)S(1)}, bf16[768,384]{1,0:T(8,128)(2,1)S(1)}, u32[]{:S(2)}, u32[]{:S(2)}) collective-permute-start(bf16[768,384]{1,0:T(8,128)(2,1)S(1)} %get-tuple-element.171), channel_id=1, source_target_pairs={{0,16},{16,0},{1,17},{17,1},{2,18},{18,2},{3,19},{19,3},{4,20},{20... | collective-permute-start | bytes 1769480 | tf_op jit(solution)/shard_map/ppermute | solution.py:49
  113.7 12.9 %collective-permute-start.33 = (bf16[512,384]{1,0:T(8,128)(2,1)S(1)}, bf16[512,384]{1,0:T(8,128)(2,1)S(1)}, u32[]{:S(2)}, u32[]{:S(2)}) collective-permute-start(bf16[512,384]{1,0:T(8,128)(2,1)S(1)} %get-tuple-element.170), channel_id=1, source_target_pairs={{0,1},{1,0},{2,3},{3,2},{4,5},{5,4},{6,7},{7,6},{8,9},{9,8},{10,11... | collective-permute-start | bytes 1179656 | tf_op jit(solution)/shard_map/ppermute | solution.py:49
  115.5 10.0 %collective-permute-start.35 = (bf16[192,384]{1,0:T(8,128)(2,1)S(1)}, bf16[192,384]{1,0:T(8,128)(2,1)S(1)}, u32[]{:S(2)}, u32[]{:S(2)}) collective-permute-start(bf16[192,384]{1,0:T(8,128)(2,1)S(1)} %get-tuple-element.174), channel_id=1, source_target_pairs={{0,2},{1,3},{2,0},{3,1},{4,6},{5,7},{6,4},{7,5},{8,10},{9,11},{10,... | collective-permute-start | bytes 442376 | tf_op jit(solution)/shard_map/ppermute | solution.py:49
  115.9 13.2 %collective-permute-start.40 = (bf16[192,384]{1,0:T(8,128)(2,1)S(1)}, bf16[192,384]{1,0:T(8,128)(2,1)S(1)}, u32[]{:S(2)}, u32[]{:S(2)}) collective-permute-start(bf16[192,384]{1,0:T(8,128)(2,1)S(1)} %get-tuple-element.196), channel_id=1, source_target_pairs={{0,16},{16,0},{1,17},{17,1},{2,18},{18,2},{3,19},{19,3},{4,20},{20... | collective-permute-start | bytes 442376 | tf_op jit(solution)/shard_map/ppermute | solution.py:49
  126.7 9.8 %collective-permute-start.36 = (bf16[256,384]{1,0:T(8,128)(2,1)S(1)}, bf16[256,384]{1,0:T(8,128)(2,1)S(1)}, u32[]{:S(2)}, u32[]{:S(2)}) collective-permute-start(bf16[256,384]{1,0:T(8,128)(2,1)S(1)} %get-tuple-element.177), channel_id=1, source_target_pairs={{0,2},{1,3},{2,0},{3,1},{4,6},{5,7},{6,4},{7,5},{8,10},{9,11},{10,... | collective-permute-start | bytes 589832 | tf_op jit(solution)/shard_map/ppermute | solution.py:49
  129.8 11.6 %collective-permute-start.41 = (bf16[480,384]{1,0:T(8,128)(2,1)S(1)}, bf16[480,384]{1,0:T(8,128)(2,1)S(1)}, u32[]{:S(2)}, u32[]{:S(2)}) collective-permute-start(bf16[480,384]{1,0:T(8,128)(2,1)S(1)} %get-tuple-element.200), channel_id=1, source_target_pairs={{0,1},{1,0},{2,3},{3,2},{4,5},{5,4},{6,7},{7,6},{8,9},{9,8},{10,11... | collective-permute-start | bytes 1105928 | tf_op jit(solution)/shard_map/ppermute | solution.py:49
  138.1 12.2 %collective-permute-start.39 = (bf16[576,384]{1,0:T(8,128)(2,1)S(1)}, bf16[576,384]{1,0:T(8,128)(2,1)S(1)}, u32[]{:S(2)}, u32[]{:S(2)}) collective-permute-start(bf16[576,384]{1,0:T(8,128)(2,1)S(1)} %get-tuple-element.193), channel_id=1, source_target_pairs={{0,16},{16,0},{1,17},{17,1},{2,18},{18,2},{3,19},{19,3},{4,20},{20... | collective-permute-start | bytes 1327112 | tf_op jit(solution)/shard_map/ppermute | solution.py:49
  141.4 8.9 %collective-permute-start.42 = (bf16[240,384]{1,0:T(8,128)(2,1)S(1)}, bf16[240,384]{1,0:T(8,128)(2,1)S(1)}, u32[]{:S(2)}, u32[]{:S(2)}) collective-permute-start(bf16[240,384]{1,0:T(8,128)(2,1)S(1)} %get-tuple-element.203), channel_id=1, source_target_pairs={{0,2},{1,3},{2,0},{3,1},{4,6},{5,7},{6,4},{7,5},{8,10},{9,11},{10,... | collective-permute-start | bytes 552968 | tf_op jit(solution)/shard_map/ppermute | solution.py:49
  151.1 14.5 %all-to-all-start = ((bf16[4,192,128]{2,1,0:T(8,128)(2,1)}), bf16[4,192,128]{2,1,0:T(8,128)(2,1)S(1)}, u32[]{:S(2)}, u32[]{:S(2)}) async-start(bf16[4,192,128]{2,1,0:T(8,128)(2,1)} %get-tuple-element.189), calls=%async_computation | async-start | bytes 393216 | tf_op jit(solution)/shard_map/all_to_all | solution.py:53
  155.5 8.6 %collective-permute-start.45 = (bf16[192,384]{1,0:T(8,128)(2,1)S(1)}, bf16[192,384]{1,0:T(8,128)(2,1)S(1)}, u32[]{:S(2)}, u32[]{:S(2)}) collective-permute-start(bf16[192,384]{1,0:T(8,128)(2,1)S(1)} %shard_map.270.part), channel_id=1, source_target_pairs={{0,16},{16,0},{1,17},{17,1},{2,18},{18,2},{3,19},{19,3},{4,20},{20... | collective-permute-start | bytes 442376 | tf_op jit(solution)/shard_map/ppermute | solution.py:49
  159.1 10.2 %collective-permute-start.44 = (bf16[192,384]{1,0:T(8,128)(2,1)S(1)}, bf16[192,384]{1,0:T(8,128)(2,1)S(1)}, u32[]{:S(2)}, u32[]{:S(2)}) collective-permute-start(bf16[192,384]{1,0:T(8,128)(2,1)S(1)} %get-tuple-element.209), channel_id=1, source_target_pairs={{0,2},{1,3},{2,0},{3,1},{4,6},{5,7},{6,4},{7,5},{8,10},{9,11},{10,... | collective-permute-start | bytes 442376 | tf_op jit(solution)/shard_map/ppermute | solution.py:49
  162.1 8.9 %collective-permute-start.47 = (bf16[240,384]{1,0:T(8,128)(2,1)S(1)}, bf16[240,384]{1,0:T(8,128)(2,1)S(1)}, u32[]{:S(2)}, u32[]{:S(2)}) collective-permute-start(bf16[240,384]{1,0:T(8,128)(2,1)S(1)} %shard_map.273.part), channel_id=1, source_target_pairs={{0,16},{16,0},{1,17},{17,1},{2,18},{18,2},{3,19},{19,3},{4,20},{20... | collective-permute-start | bytes 552968 | tf_op jit(solution)/shard_map/ppermute | solution.py:49
  (37 other events, 251.4 us)

commit v7 on v6

--- a/solution.py
+++ b/solution.py
@@ -562,19 +562,20 @@
     out[rows:, :] = pack_sums(total)
 
 
-def flat_store(value, cut, out):
+def flat_store(value, cut, flat, out):
     rows, width = value.shape
     lines = 2 * width // 128
     for i in range(cut.shape[0]):
         high = min(width, (i + 1) * 128)
-        cut[i, :, : high - i * 128] = value[:, i * 128 : high]
+        cut[i, :rows, : high - i * 128] = value[:, i * 128 : high]
     both = []
     for odd in range(2):
         pieces = [cut[i, pl.ds(odd, rows // 2, stride=2), :] for i in range(cut.shape[0])]
         both.append(jnp.concatenate(pieces, axis=1)[:, :width])
     both = jnp.concatenate(both, axis=1)
     for g in range(lines):
-        out[pl.ds(g, rows // 2, stride=lines), :] = both[:, g * 128 : (g + 1) * 128]
+        flat[pl.ds(g, rows // 2, stride=lines), :] = both[:, g * 128 : (g + 1) * 128]
+    out[...] = flat[: out.shape[0], :]
 
 
 def up_out_kernel(scal, part, away, up):
@@ -583,7 +584,7 @@
     up[:, pl.ds(pl.multiple_of((1 - scal[2]) * half, 128), half)] = away[...].astype(f32)
 
 
-def down_out_kernel(scal, part, away, down, out, full, cut):
+def down_out_kernel(scal, part, away, down, out, full, cut, flat):
     d = scal[2]
     rows, width = down.shape
     half = width // 2
@@ -591,16 +592,16 @@
         down[:, pl.ds(pl.multiple_of(index * half, 128), half)] = ref[:rows, :].astype(f32)
         piece = under(ref[rows:, :].astype(f32), rows // 2)
         full[pl.ds(pl.multiple_of(index * (rows // 2), 32), rows // 2), :] = piece
-    flat_store(full, cut, out)
+    flat_store(full, cut, flat, out)
 
 
 def qkv_out_kernel(scal, part, away, sums_ref, out, *refs):
-    outs, (full, cut) = refs[:-2], refs[-2:]
+    outs, (full, cut, flat) = refs[:-3], refs[-3:]
     rows = part.shape[0] - 48
     half = 2 * rows // 3
     full[pl.ds(pl.multiple_of(scal[2] * half, 32), half), :] = widen(part[:rows, :].astype(f32))
     full[pl.ds(pl.multiple_of((1 - scal[2]) * half, 32), half), :] = widen(away[:rows, :].astype(f32))
-    flat_store(full, cut, out)
+    flat_store(full, cut, flat, out)
     sums = sums_ref[...] + unpack_sums(away[rows:, :])
     width = outs[0].shape[1]
     mine = sums[:, :width]
@@ -867,7 +868,7 @@
         [((width_in, ff), f32), ((width_out * width_in // 128, 128), f32)],
         scal,
         share_dp(*after(down_pair, send)),
-        [((width_out, width_in), f32), ((pl.cdiv(width_in, 128), width_out, 128), f32)],
+        [((width_out, width_in), f32), ((pl.cdiv(width_in, 128), width_out + 8, 128), f32), ((width_out * width_in // 128 + 8, 128), f32)],
     )
     d_qkv, *vecs = call(
         qkv_out_kernel,
@@ -876,7 +877,7 @@
         + [((1, ff), f32), ((2, width_out), f32)],
         scal,
         [total, after(swap(total, "dp", 1), d_down), sums],
-        [((width_in, 3 * width_out), f32), ((pl.cdiv(3 * width_out, 128), width_in, 128), f32)],
+        [((width_in, 3 * width_out), f32), ((pl.cdiv(3 * width_out, 128), width_in + 8, 128), f32), ((3 * width_out * width_in // 128 + 16, 128), f32)],
     )
 
     return (

time: 177 us -> 177 us (level)
  no operation moved by 1% of the time
where the time goes in v7:
time: 177 us
  waiting for transfers between devices  86.7 us (49%)
  starting transfers between devices  57.3 us (32%)
  Pallas kernels  27.2 us (15%)
  other arithmetic  4.24 us (2%)
    ppermute x48, waiting for transfers between devices, swap(): return lax.ppermute(value, axis, [(i, i ^ bit) for i in range(n)])  86.7 us
    ppermute x48, starting transfers between devices, swap(): return lax.ppermute(value, axis, [(i, i ^ bit) for i in range(n)])  52.9 us
    pallas_call x31, Pallas kernels, call(): pl.pallas_call(kernel, out_shape=[jax.ShapeDtypeStruct(s, t) for s, t in...  27.2 us
    all_to_all x1, starting transfers between devices, turn(): return lax.all_to_all(value, 'col', split, concat, tiled=True)  4.43 us
    unnamed x2, other arithmetic  3.55 us
  transfers between devices with their start and end apart: 49, of which 28 were waited for; matrix products, arithmetic and copies ran while one was open for 0% of the time, Pallas kernels for 11%

profile of v7, /device:TPU:0, one launch (start us, length us, event | category | flops | bytes accessed | tf_op | source)
XLA Modules:
  0.0 176.9 jit_solution(14381121035075969118)
XLA Ops:
  2.1 2.2 %reduce = bf16[110592]{0:T(1024)(128)(2,1)S(1)} reduce(bf16[1,1,110592]{2,1,0:T(2,128)(2,1)} %param.17, bf16[]{:T(256)} %constant.17), dimensions={0,1}, to_apply=%param.17.reduce_sub_computation | reduce | bytes 442370 | tf_op args[3]
  5.4 4.1 %collective-permute-start.7 = (bf16[96,768]{1,0:T(8,128)(2,1)S(1)}, bf16[96,768]{1,0:T(8,128)(2,1)S(1)}, u32[]{:S(2)}, u32[]{:S(2)}) collective-permute-start(bf16[96,768]{1,0:T(8,128)(2,1)S(1)} %shard_map.247), channel_id=1, source_target_pairs={{0,2},{1,3},{2,0},{3,1},{4,6},{5,7},{6,4},{7,5},{8,10},{9,11},{10,... | collective-permute-start | bytes 442376 | tf_op jit(solution)/shard_map/ppermute | solution.py:49
  12.5 3.9 %collective-permute-start.2 = (bf16[80,384]{1,0:T(8,128)(2,1)S(1)}, bf16[80,384]{1,0:T(8,128)(2,1)S(1)}, u32[]{:S(2)}, u32[]{:S(2)}) collective-permute-start(bf16[80,384]{1,0:T(8,128)(2,1)S(1)} %get-tuple-element.125), channel_id=1, source_target_pairs={{0,3},{1,2},{2,1},{3,0},{4,7},{5,6},{6,5},{7,4},{8,11},{9,10},{10,... | collective-permute-start | bytes 184328 | tf_op jit(solution)/shard_map/ppermute | solution.py:49
  16.4 3.4 %collective-permute-done.refs_1_ = bf16[80,384]{1,0:T(8,128)(2,1)S(1)} collective-permute-done((bf16[80,384]{1,0:T(8,128)(2,1)S(1)}, bf16[80,384]{1,0:T(8,128)(2,1)S(1)}, u32[]{:S(2)}, u32[]{:S(2)}) %collective-permute-start) | collective-permute-done | bytes 61472 | tf_op jit(solution)/shard_map/ppermute | solution.py:49
  29.3 2.2 %collective-permute-start.12 = (bf16[384,384]{1,0:T(8,128)(2,1)S(1)}, bf16[384,384]{1,0:T(8,128)(2,1)S(1)}, u32[]{:S(2)}, u32[]{:S(2)}) collective-permute-start(bf16[384,384]{1,0:T(8,128)(2,1)S(1)} %shard_map.249), channel_id=1, source_target_pairs={{0,1},{1,0},{2,3},{3,2},{4,5},{5,4},{6,7},{7,6},{8,9},{9,8},{10,11... | collective-permute-start | bytes 884744 | tf_op jit(solution)/shard_map/ppermute | solution.py:49
  35.4 8.7 %collective-permute-done.12.refs_11_ = bf16[384,384]{1,0:T(8,128)(2,1)S(1)} collective-permute-done((bf16[384,384]{1,0:T(8,128)(2,1)S(1)}, bf16[384,384]{1,0:T(8,128)(2,1)S(1)}, u32[]{:S(2)}, u32[]{:S(2)}) %collective-permute-start.12) | collective-permute-done | bytes 294944 | tf_op jit(solution)/shard_map/ppermute | solution.py:49
  47.1 3.4 %collective-permute-start.14 = (bf16[256,384]{1,0:T(8,128)(2,1)S(1)}, bf16[256,384]{1,0:T(8,128)(2,1)S(1)}, u32[]{:S(2)}, u32[]{:S(2)}) collective-permute-start(bf16[256,384]{1,0:T(8,128)(2,1)S(1)} %get-tuple-element.134.refs_0_), channel_id=1, source_target_pairs={{0,1},{1,0},{2,3},{3,2},{4,5},{5,4},{6,7},{7,6},{8,9},{9,8},{10,11... | collective-permute-start | bytes 589832 | tf_op jit(solution)/shard_map/ppermute | solution.py:49
  50.5 6.9 %collective-permute-done.15.refs_2_ = bf16[256,384]{1,0:T(8,128)(2,1)S(1)} collective-permute-done((bf16[256,384]{1,0:T(8,128)(2,1)S(1)}, bf16[256,384]{1,0:T(8,128)(2,1)S(1)}, u32[]{:S(2)}, u32[]{:S(2)}) %collective-permute-start.15) | collective-permute-done | bytes 196640 | tf_op jit(solution)/shard_map/ppermute | solution.py:49
  58.2 5.3 %collective-permute-done.17.refs_3_ = bf16[256,384]{1,0:T(8,128)(2,1)S(1)} collective-permute-done((bf16[256,384]{1,0:T(8,128)(2,1)S(1)}, bf16[256,384]{1,0:T(8,128)(2,1)S(1)}, u32[]{:S(2)}, u32[]{:S(2)}) %collective-permute-start.17) | collective-permute-done | bytes 196640 | tf_op jit(solution)/shard_map/ppermute | solution.py:49
  65.6 2.8 %shard_map.250 = (bf16[256,192]{1,0:T(8,128)(2,1)S(1)}, f32[128,768]{1,0:T(8,128)S(1)}, bf16[128,768]{1,0:T(8,128)(2,1)S(1)}) custom-call(s32[3]{0:T(128)S(1)} %pad_add_fusion.scal, bf16[256,192]{1,0:T(8,128)(2,1)S(1)} %get-tuple-element.129.q_ref, bf16[256,384]{1,0:T(8,128)(2,1)S(1)} %get-tuple-element.134.refs_0_, ...), custom_call_target="tpu_custom_call" | custom-call | flops 1 | bytes 15000001 | tf_op jit(solution)/shard_map/pallas_call | solution.py:36
  68.5 2.4 %collective-permute-done.21.refs_13_ = bf16[384,384]{1,0:T(8,128)(2,1)S(1)} collective-permute-done((bf16[384,384]{1,0:T(8,128)(2,1)S(1)}, bf16[384,384]{1,0:T(8,128)(2,1)S(1)}, u32[]{:S(2)}, u32[]{:S(2)}) %collective-permute-start.21) | collective-permute-done | bytes 294944 | tf_op jit(solution)/shard_map/ppermute | solution.py:49
  72.7 3.1 %collective-permute-done.20.got = bf16[64,768]{1,0:T(8,128)(2,1)S(1)} collective-permute-done((bf16[64,768]{1,0:T(8,128)(2,1)S(1)}, bf16[64,768]{1,0:T(8,128)(2,1)S(1)}, u32[]{:S(2)}, u32[]{:S(2)}) %collective-permute-start.20) | collective-permute-done | bytes 98336 | tf_op jit(solution)/shard_map/ppermute | solution.py:49
  79.7 3.1 %collective-permute-done.23.refs_1_ = bf16[64,768]{1,0:T(8,128)(2,1)S(1)} collective-permute-done((bf16[64,768]{1,0:T(8,128)(2,1)S(1)}, bf16[64,768]{1,0:T(8,128)(2,1)S(1)}, u32[]{:S(2)}, u32[]{:S(2)}) %collective-permute-start.23) | collective-permute-done | bytes 98336 | tf_op jit(solution)/shard_map/ppermute | solution.py:49
  84.1 2.3 %shard_map.253 = (bf16[256,768]{1,0:T(8,128)(2,1)S(1)}, bf16[256,768]{1,0:T(8,128)(2,1)S(1)}, f32[1,768]{1,0:T(1,128)S(1)}, f32[128,1536]{1,0:T(8,128)S(1)}, bf16[128,1536]{1,0:T(8,128)(2,1)S(1)}) custom-call(s32[3]{0:T(128)S(1)} %pad_add_fusion.scal, bf16[64,768]{1,0:T(8,128)(2,1)S(1)} %get-tuple-element.146.refs_0_, ...), custom_call_target="tpu_custom_call" | custom-call | flops 1 | bytes 1 | tf_op jit(solution)/shard_map/pallas_call | solution.py:36
  91.1 5.2 %collective-permute-done.27.got.a_got = bf16[64,1536]{1,0:T(8,128)(2,1)S(1)} collective-permute-done((bf16[64,1536]{1,0:T(8,128)(2,1)S(1)}, bf16[64,1536]{1,0:T(8,128)(2,1)S(1)}, u32[]{:S(2)}, u32[]{:S(2)}) %collective-permute-start.27) | collective-permute-done | bytes 196640 | tf_op jit(solution)/shard_map/ppermute | solution.py:49
  98.2 3.1 %collective-permute-done.28.refs_1_ = bf16[64,768]{1,0:T(8,128)(2,1)S(1)} collective-permute-done((bf16[64,768]{1,0:T(8,128)(2,1)S(1)}, bf16[64,768]{1,0:T(8,128)(2,1)S(1)}, u32[]{:S(2)}, u32[]{:S(2)}) %collective-permute-start.28) | collective-permute-done | bytes 98336 | tf_op jit(solution)/shard_map/ppermute | solution.py:49
  108.5 4.9 %shard_map.259 = (bf16[256,192]{1,0:T(8,128)(2,1)S(1)}, f32[512,384]{1,0:T(8,128)S(1)}, bf16[512,384]{1,0:T(8,128)(2,1)S(1)}) custom-call(s32[3]{0:T(128)S(1)} %pad_add_fusion.scal, bf16[256,192]{1,0:T(8,128)(2,1)S(1)} %get-tuple-element.129.q_ref, bf16[256,384]{1,0:T(8,128)(2,1)S(1)} %get-tuple-element.134.refs_0_, ...), custom_call_target="tpu_custom_call" | custom-call | flops 1 | bytes 30000000 | tf_op jit(solution)/shard_map/pallas_call | solution.py:36
  116.5 9.0 %collective-permute-done.35.refs_1_ = bf16[192,384]{1,0:T(8,128)(2,1)S(1)} collective-permute-done((bf16[192,384]{1,0:T(8,128)(2,1)S(1)}, bf16[192,384]{1,0:T(8,128)(2,1)S(1)}, u32[]{:S(2)}, u32[]{:S(2)}) %collective-permute-start.35) | collective-permute-done | bytes 147488 | tf_op jit(solution)/shard_map/ppermute | solution.py:49
  126.7 2.4 %collective-permute-start.36 = (bf16[256,384]{1,0:T(8,128)(2,1)S(1)}, bf16[256,384]{1,0:T(8,128)(2,1)S(1)}, u32[]{:S(2)}, u32[]{:S(2)}) collective-permute-start(bf16[256,384]{1,0:T(8,128)(2,1)S(1)} %get-tuple-element.177), channel_id=1, source_target_pairs={{0,2},{1,3},{2,0},{3,1},{4,6},{5,7},{6,4},{7,5},{8,10},{9,11},{10,... | collective-permute-start | bytes 589832 | tf_op jit(solution)/shard_map/ppermute | solution.py:49
  129.9 6.7 %collective-permute-done.36.refs_6_ = bf16[256,384]{1,0:T(8,128)(2,1)S(1)} collective-permute-done((bf16[256,384]{1,0:T(8,128)(2,1)S(1)}, bf16[256,384]{1,0:T(8,128)(2,1)S(1)}, u32[]{:S(2)}, u32[]{:S(2)}) %collective-permute-start.36) | collective-permute-done | bytes 196640 | tf_op jit(solution)/shard_map/ppermute | solution.py:49
  143.2 4.2 %collective-permute-done.38.d_got = bf16[96,768]{1,0:T(8,128)(2,1)S(1)} collective-permute-done((bf16[96,768]{1,0:T(8,128)(2,1)S(1)}, bf16[96,768]{1,0:T(8,128)(2,1)S(1)}, u32[]{:S(2)}, u32[]{:S(2)}) %collective-permute-start.38) | collective-permute-done | bytes 147488 | tf_op jit(solution)/shard_map/ppermute | solution.py:49
  151.1 4.4 %all-to-all-start = ((bf16[4,192,128]{2,1,0:T(8,128)(2,1)}), bf16[4,192,128]{2,1,0:T(8,128)(2,1)S(1)}, u32[]{:S(2)}, u32[]{:S(2)}) async-start(bf16[4,192,128]{2,1,0:T(8,128)(2,1)} %get-tuple-element.189), calls=%async_computation | async-start | bytes 393216 | tf_op jit(solution)/shard_map/all_to_all | solution.py:53
  159.1 3.0 %collective-permute-start.44 = (bf16[192,384]{1,0:T(8,128)(2,1)S(1)}, bf16[192,384]{1,0:T(8,128)(2,1)S(1)}, u32[]{:S(2)}, u32[]{:S(2)}) collective-permute-start(bf16[192,384]{1,0:T(8,128)(2,1)S(1)} %get-tuple-element.209), channel_id=1, source_target_pairs={{0,2},{1,3},{2,0},{3,1},{4,6},{5,7},{6,4},{7,5},{8,10},{9,11},{10,... | collective-permute-start | bytes 442376 | tf_op jit(solution)/shard_map/ppermute | solution.py:49
  166.3 3.0 %collective-permute-done.44.got_ref = bf16[192,384]{1,0:T(8,128)(2,1)S(1)} collective-permute-done((bf16[192,384]{1,0:T(8,128)(2,1)S(1)}, bf16[192,384]{1,0:T(8,128)(2,1)S(1)}, u32[]{:S(2)}, u32[]{:S(2)}) %collective-permute-start.44) | collective-permute-done | bytes 147488 | tf_op jit(solution)/shard_map/ppermute | solution.py:49
  (136 shorter events, 76.3 us)
Async XLA Ops:
  5.4 16.3 %collective-permute-start.7 = (bf16[96,768]{1,0:T(8,128)(2,1)S(1)}, bf16[96,768]{1,0:T(8,128)(2,1)S(1)}, u32[]{:S(2)}, u32[]{:S(2)}) collective-permute-start(bf16[96,768]{1,0:T(8,128)(2,1)S(1)} %shard_map.247), channel_id=1, source_target_pairs={{0,2},{1,3},{2,0},{3,1},{4,6},{5,7},{6,4},{7,5},{8,10},{9,11},{10,... | collective-permute-start | bytes 442376 | tf_op jit(solution)/shard_map/ppermute | solution.py:49
  9.5 13.7 %collective-permute-start.6 = (bf16[96,768]{1,0:T(8,128)(2,1)S(1)}, bf16[96,768]{1,0:T(8,128)(2,1)S(1)}, u32[]{:S(2)}, u32[]{:S(2)}) collective-permute-start(bf16[96,768]{1,0:T(8,128)(2,1)S(1)} %shard_map.247), channel_id=1, source_target_pairs={{0,1},{1,0},{2,3},{3,2},{4,5},{5,4},{6,7},{7,6},{8,9},{9,8},{10,11... | collective-permute-start | bytes 442376 | tf_op jit(solution)/shard_map/ppermute | solution.py:49
  12.5 9.1 %collective-permute-start.2 = (bf16[80,384]{1,0:T(8,128)(2,1)S(1)}, bf16[80,384]{1,0:T(8,128)(2,1)S(1)}, u32[]{:S(2)}, u32[]{:S(2)}) collective-permute-start(bf16[80,384]{1,0:T(8,128)(2,1)S(1)} %get-tuple-element.125), channel_id=1, source_target_pairs={{0,3},{1,2},{2,1},{3,0},{4,7},{5,6},{6,5},{7,4},{8,11},{9,10},{10,... | collective-permute-start | bytes 184328 | tf_op jit(solution)/shard_map/ppermute | solution.py:49
  29.3 14.8 %collective-permute-start.12 = (bf16[384,384]{1,0:T(8,128)(2,1)S(1)}, bf16[384,384]{1,0:T(8,128)(2,1)S(1)}, u32[]{:S(2)}, u32[]{:S(2)}) collective-permute-start(bf16[384,384]{1,0:T(8,128)(2,1)S(1)} %shard_map.249), channel_id=1, source_target_pairs={{0,1},{1,0},{2,3},{3,2},{4,5},{5,4},{6,7},{7,6},{8,9},{9,8},{10,11... | collective-permute-start | bytes 884744 | tf_op jit(solution)/shard_map/ppermute | solution.py:49
  31.5 15.5 %collective-permute-start.13 = (bf16[384,384]{1,0:T(8,128)(2,1)S(1)}, bf16[384,384]{1,0:T(8,128)(2,1)S(1)}, u32[]{:S(2)}, u32[]{:S(2)}) collective-permute-start(bf16[384,384]{1,0:T(8,128)(2,1)S(1)} %shard_map.249), channel_id=1, source_target_pairs={{0,2},{1,3},{2,0},{3,1},{4,6},{5,7},{6,4},{7,5},{8,10},{9,11},{10,... | collective-permute-start | bytes 884744 | tf_op jit(solution)/shard_map/ppermute | solution.py:49
  33.4 12.2 %collective-permute-start.4 = (bf16[128,768]{1,0:T(8,128)(2,1)S(1)}, bf16[128,768]{1,0:T(8,128)(2,1)S(1)}, u32[]{:S(2)}, u32[]{:S(2)}) collective-permute-start(bf16[128,768]{1,0:T(8,128)(2,1)S(1)} %get-tuple-element.126.refs_0_.xg.refs_4_), channel_id=1, source_target_pairs={{0,4},{4,0},{8,12},{12,8},{1,5},{5,1},{9,13},{13,9},{2,6},{6,2},{1... | collective-permute-start | bytes 589832 | tf_op jit(solution)/shard_map/ppermute | solution.py:49
  33.4 12.2 %collective-permute-start.5 = (bf16[128,768]{1,0:T(8,128)(2,1)S(1)}, bf16[128,768]{1,0:T(8,128)(2,1)S(1)}, u32[]{:S(2)}, u32[]{:S(2)}) collective-permute-start(bf16[128,768]{1,0:T(8,128)(2,1)S(1)} %collective-permute-done.3.refs_1_.refs_5_), channel_id=1, source_target_pairs={{0,4},{4,0},{8,12},{12,8},{1,5},{5,1},{9,13},{13,9},{2,6},{6,2},{1... | collective-permute-start | bytes 589832 | tf_op jit(solution)/shard_map/ppermute | solution.py:49
  33.9 11.7 %collective-permute-start.11 = (bf16[96,768]{1,0:T(8,128)(2,1)S(1)}, bf16[96,768]{1,0:T(8,128)(2,1)S(1)}, u32[]{:S(2)}, u32[]{:S(2)}) collective-permute-start(bf16[96,768]{1,0:T(8,128)(2,1)S(1)} %collective-permute-done.8.refs_10_), channel_id=1, source_target_pairs={{0,16},{16,0},{1,17},{17,1},{2,18},{18,2},{3,19},{19,3},{4,20},{20... | collective-permute-start | bytes 442376 | tf_op jit(solution)/shard_map/ppermute | solution.py:49
  44.1 13.2 %collective-permute-start.16 = (bf16[384,384]{1,0:T(8,128)(2,1)S(1)}, bf16[384,384]{1,0:T(8,128)(2,1)S(1)}, u32[]{:S(2)}, u32[]{:S(2)}) collective-permute-start(bf16[384,384]{1,0:T(8,128)(2,1)S(1)} %collective-permute-done.12.refs_11_), channel_id=1, source_target_pairs={{0,16},{16,0},{1,17},{17,1},{2,18},{18,2},{3,19},{19,3},{4,20},{20... | collective-permute-start | bytes 884744 | tf_op jit(solution)/shard_map/ppermute | solution.py:49
  47.0 10.3 %collective-permute-start.15 = (bf16[256,384]{1,0:T(8,128)(2,1)S(1)}, bf16[256,384]{1,0:T(8,128)(2,1)S(1)}, u32[]{:S(2)}, u32[]{:S(2)}) collective-permute-start(bf16[256,384]{1,0:T(8,128)(2,1)S(1)} %get-tuple-element.134.refs_0_), channel_id=1, source_target_pairs={{0,2},{1,3},{2,0},{3,1},{4,6},{5,7},{6,4},{7,5},{8,10},{9,11},{10,... | collective-permute-start | bytes 589832 | tf_op jit(solution)/shard_map/ppermute | solution.py:49
  47.1 11.1 %collective-permute-start.14 = (bf16[256,384]{1,0:T(8,128)(2,1)S(1)}, bf16[256,384]{1,0:T(8,128)(2,1)S(1)}, u32[]{:S(2)}, u32[]{:S(2)}) collective-permute-start(bf16[256,384]{1,0:T(8,128)(2,1)S(1)} %get-tuple-element.134.refs_0_), channel_id=1, source_target_pairs={{0,1},{1,0},{2,3},{3,2},{4,5},{5,4},{6,7},{7,6},{8,9},{9,8},{10,11... | collective-permute-start | bytes 589832 | tf_op jit(solution)/shard_map/ppermute | solution.py:49
  89.2 15.4 %collective-permute-start.31 = (bf16[768,384]{1,0:T(8,128)(2,1)S(1)}, bf16[768,384]{1,0:T(8,128)(2,1)S(1)}, u32[]{:S(2)}, u32[]{:S(2)}) collective-permute-start(bf16[768,384]{1,0:T(8,128)(2,1)S(1)} %get-tuple-element.155), channel_id=1, source_target_pairs={{0,16},{16,0},{1,17},{17,1},{2,18},{18,2},{3,19},{19,3},{4,20},{20... | collective-permute-start | bytes 1769480 | tf_op jit(solution)/shard_map/ppermute | solution.py:49
  107.2 18.3 %collective-permute-start.34 = (bf16[768,384]{1,0:T(8,128)(2,1)S(1)}, bf16[768,384]{1,0:T(8,128)(2,1)S(1)}, u32[]{:S(2)}, u32[]{:S(2)}) collective-permute-start(bf16[768,384]{1,0:T(8,128)(2,1)S(1)} %get-tuple-element.171), channel_id=1, source_target_pairs={{0,16},{16,0},{1,17},{17,1},{2,18},{18,2},{3,19},{19,3},{4,20},{20... | collective-permute-start | bytes 1769480 | tf_op jit(solution)/shard_map/ppermute | solution.py:49
  113.7 12.9 %collective-permute-start.33 = (bf16[512,384]{1,0:T(8,128)(2,1)S(1)}, bf16[512,384]{1,0:T(8,128)(2,1)S(1)}, u32[]{:S(2)}, u32[]{:S(2)}) collective-permute-start(bf16[512,384]{1,0:T(8,128)(2,1)S(1)} %get-tuple-element.170), channel_id=1, source_target_pairs={{0,1},{1,0},{2,3},{3,2},{4,5},{5,4},{6,7},{7,6},{8,9},{9,8},{10,11... | collective-permute-start | bytes 1179656 | tf_op jit(solution)/shard_map/ppermute | solution.py:49
  115.5 10.0 %collective-permute-start.35 = (bf16[192,384]{1,0:T(8,128)(2,1)S(1)}, bf16[192,384]{1,0:T(8,128)(2,1)S(1)}, u32[]{:S(2)}, u32[]{:S(2)}) collective-permute-start(bf16[192,384]{1,0:T(8,128)(2,1)S(1)} %get-tuple-element.174), channel_id=1, source_target_pairs={{0,2},{1,3},{2,0},{3,1},{4,6},{5,7},{6,4},{7,5},{8,10},{9,11},{10,... | collective-permute-start | bytes 442376 | tf_op jit(solution)/shard_map/ppermute | solution.py:49
  115.9 13.2 %collective-permute-start.40 = (bf16[192,384]{1,0:T(8,128)(2,1)S(1)}, bf16[192,384]{1,0:T(8,128)(2,1)S(1)}, u32[]{:S(2)}, u32[]{:S(2)}) collective-permute-start(bf16[192,384]{1,0:T(8,128)(2,1)S(1)} %get-tuple-element.196), channel_id=1, source_target_pairs={{0,16},{16,0},{1,17},{17,1},{2,18},{18,2},{3,19},{19,3},{4,20},{20... | collective-permute-start | bytes 442376 | tf_op jit(solution)/shard_map/ppermute | solution.py:49
  126.7 9.8 %collective-permute-start.36 = (bf16[256,384]{1,0:T(8,128)(2,1)S(1)}, bf16[256,384]{1,0:T(8,128)(2,1)S(1)}, u32[]{:S(2)}, u32[]{:S(2)}) collective-permute-start(bf16[256,384]{1,0:T(8,128)(2,1)S(1)} %get-tuple-element.177), channel_id=1, source_target_pairs={{0,2},{1,3},{2,0},{3,1},{4,6},{5,7},{6,4},{7,5},{8,10},{9,11},{10,... | collective-permute-start | bytes 589832 | tf_op jit(solution)/shard_map/ppermute | solution.py:49
  129.8 11.6 %collective-permute-start.41 = (bf16[480,384]{1,0:T(8,128)(2,1)S(1)}, bf16[480,384]{1,0:T(8,128)(2,1)S(1)}, u32[]{:S(2)}, u32[]{:S(2)}) collective-permute-start(bf16[480,384]{1,0:T(8,128)(2,1)S(1)} %get-tuple-element.200), channel_id=1, source_target_pairs={{0,1},{1,0},{2,3},{3,2},{4,5},{5,4},{6,7},{7,6},{8,9},{9,8},{10,11... | collective-permute-start | bytes 1105928 | tf_op jit(solution)/shard_map/ppermute | solution.py:49
  138.1 12.2 %collective-permute-start.39 = (bf16[576,384]{1,0:T(8,128)(2,1)S(1)}, bf16[576,384]{1,0:T(8,128)(2,1)S(1)}, u32[]{:S(2)}, u32[]{:S(2)}) collective-permute-start(bf16[576,384]{1,0:T(8,128)(2,1)S(1)} %get-tuple-element.193), channel_id=1, source_target_pairs={{0,16},{16,0},{1,17},{17,1},{2,18},{18,2},{3,19},{19,3},{4,20},{20... | collective-permute-start | bytes 1327112 | tf_op jit(solution)/shard_map/ppermute | solution.py:49
  141.4 8.9 %collective-permute-start.42 = (bf16[240,384]{1,0:T(8,128)(2,1)S(1)}, bf16[240,384]{1,0:T(8,128)(2,1)S(1)}, u32[]{:S(2)}, u32[]{:S(2)}) collective-permute-start(bf16[240,384]{1,0:T(8,128)(2,1)S(1)} %get-tuple-element.203), channel_id=1, source_target_pairs={{0,2},{1,3},{2,0},{3,1},{4,6},{5,7},{6,4},{7,5},{8,10},{9,11},{10,... | collective-permute-start | bytes 552968 | tf_op jit(solution)/shard_map/ppermute | solution.py:49
  151.1 14.5 %all-to-all-start = ((bf16[4,192,128]{2,1,0:T(8,128)(2,1)}), bf16[4,192,128]{2,1,0:T(8,128)(2,1)S(1)}, u32[]{:S(2)}, u32[]{:S(2)}) async-start(bf16[4,192,128]{2,1,0:T(8,128)(2,1)} %get-tuple-element.189), calls=%async_computation | async-start | bytes 393216 | tf_op jit(solution)/shard_map/all_to_all | solution.py:53
  155.5 8.6 %collective-permute-start.45 = (bf16[192,384]{1,0:T(8,128)(2,1)S(1)}, bf16[192,384]{1,0:T(8,128)(2,1)S(1)}, u32[]{:S(2)}, u32[]{:S(2)}) collective-permute-start(bf16[192,384]{1,0:T(8,128)(2,1)S(1)} %shard_map.270.part), channel_id=1, source_target_pairs={{0,16},{16,0},{1,17},{17,1},{2,18},{18,2},{3,19},{19,3},{4,20},{20... | collective-permute-start | bytes 442376 | tf_op jit(solution)/shard_map/ppermute | solution.py:49
  159.1 10.2 %collective-permute-start.44 = (bf16[192,384]{1,0:T(8,128)(2,1)S(1)}, bf16[192,384]{1,0:T(8,128)(2,1)S(1)}, u32[]{:S(2)}, u32[]{:S(2)}) collective-permute-start(bf16[192,384]{1,0:T(8,128)(2,1)S(1)} %get-tuple-element.209), channel_id=1, source_target_pairs={{0,2},{1,3},{2,0},{3,1},{4,6},{5,7},{6,4},{7,5},{8,10},{9,11},{10,... | collective-permute-start | bytes 442376 | tf_op jit(solution)/shard_map/ppermute | solution.py:49
  162.1 8.9 %collective-permute-start.47 = (bf16[240,384]{1,0:T(8,128)(2,1)S(1)}, bf16[240,384]{1,0:T(8,128)(2,1)S(1)}, u32[]{:S(2)}, u32[]{:S(2)}) collective-permute-start(bf16[240,384]{1,0:T(8,128)(2,1)S(1)} %shard_map.273.part), channel_id=1, source_target_pairs={{0,16},{16,0},{1,17},{17,1},{2,18},{18,2},{3,19},{19,3},{4,20},{20... | collective-permute-start | bytes 552968 | tf_op jit(solution)/shard_map/ppermute | solution.py:49
  (37 other events, 251.4 us)
